TPU v7x, 32 devices: a whole 2x2x4 slice. The times are simulated.
32 devices in a mesh: groups: 2 (over y), store: 4 (over x, core), tensor: 4 (over z).
Axes of the slice: x: 2, y: 2, z: 4, core: 2. Of those that a mesh axis runs over, the one named last changes fastest.
Arguments:
- normed_hidden_rows: bfloat16 [8192, 8192], P(('groups', 'store', 'tensor')), parts along dimension 0, may hold values from -6 to 6
- base_query_weight: bfloat16 [8192, 8192], P('tensor'), may hold values from -0.0625 to 0.0625
- adapter_down_maps: bfloat16 [128, 64, 8192], P('store', None, 'tensor'), may hold values from -0.0625 to 0.0625
- adapter_up_maps: bfloat16 [128, 64, 8192], P('store', None, 'tensor'), may hold values from -0.75 to 0.75
- row_adapter_ids: int32 [8192], P('groups'), parts along dimension 0, may hold values from 0 to 127, as said below
- adapter_store_slot: int32 [128], replicated, may hold values from 0 to 127, each once
Outputs:
- queries: bfloat16 [8192, 8192], P(('groups', 'store', 'tensor')), parts along dimension 0
There are 2 independent parts, one for each index of `groups`. A program takes and returns all parts, laid end to end along the dimension named above; an argument that names none is the same for every part. Nothing has to cross between parts.
Inputs may be any that keep to these rules, and one draw needn't show every extreme that they name: `row_adapter_ids`: constant over each aligned block of 128 rows. `adapter_store_slot`: each slot once.
All inputs are finite; a program needn't handle non-finite values.
Results may differ from a plain program's by a relative error of at most 0.014.
Values may be sent and summed in bfloat16 or wider, within the bound.
No kernel may reach another device: no remote copies, remote signals or barrier semaphores. Data moves between devices by JAX's collectives and lax.ppermute only.
A program may use at most 256 MiB of HBM per device.

v0:
```python
import jax
import jax.numpy as jnp
from jax import lax
from jax.sharding import PartitionSpec as P

TILE = 128


def body(
    normed_hidden_rows,
    base_query_weight,
    adapter_down_maps,
    adapter_up_maps,
    row_adapter_ids,
    adapter_store_slot,
):
    store_count = lax.axis_size("store")
    store_index = lax.axis_index("store")
    local_rows = lax.all_to_all(
        normed_hidden_rows, "tensor", split_axis=1, concat_axis=0, tiled=True
    )
    group_rows = local_rows.shape[0]
    feat = local_rows.shape[1]
    tile_count = group_rows // TILE
    tile_ids = row_adapter_ids.reshape(-1, TILE)[:, 0].reshape(store_count, tile_count)
    tile_slots = adapter_store_slot[tile_ids]
    every_down, every_up = (
        lax.all_gather(adapter_down_maps, "store", axis=0, tiled=True),
        lax.all_gather(adapter_up_maps, "store", axis=0, tiled=True),
    )
    mine = lax.dynamic_index_in_dim(tile_slots, store_index, 0, keepdims=False)
    tile_down = jnp.take(every_down, mine, axis=0)
    tile_up = jnp.take(every_up, mine, axis=0)
    tiled_rows = local_rows.reshape(tile_count, TILE, feat)
    low_part = jnp.einsum("tnd,trd->tnr", tiled_rows, tile_down, preferred_element_type=jnp.float32)
    low = lax.psum(low_part.astype(jnp.bfloat16), "tensor")
    delta = jnp.einsum("tnr,trd->tnd", low, tile_up, preferred_element_type=jnp.float32)
    delta = delta.astype(jnp.bfloat16).reshape(group_rows, feat)
    partial_sum = jnp.dot(local_rows, base_query_weight, preferred_element_type=jnp.float32)
    summed = lax.psum_scatter(
        partial_sum.astype(jnp.bfloat16), "tensor", scatter_dimension=1, tiled=True
    ).astype(jnp.float32)
    mixed = (summed + delta.astype(jnp.float32)).astype(jnp.bfloat16)
    return lax.all_to_all(mixed, "tensor", split_axis=0, concat_axis=1, tiled=True)


def solution(mesh):
    return jax.shard_map(
        body,
        mesh=mesh,
        in_specs=(
            P(("groups", "store", "tensor"), None),
            P("tensor", None),
            P("store", None, "tensor"),
            P("store", None, "tensor"),
            P("groups"),
            P(),
        ),
        out_specs=P(("groups", "store", "tensor"), None),
        check_vma=False,
    )
```

profile of v0, /device:TPU:0, one launch (start us, length us, event | category | flops | bytes accessed | tf_op | source)
XLA Modules:
  0.0 847.1 jit_solution(16937401346538715839)
XLA Ops:
  6.5 0.7 all-gather.3.cloned.1.call-update
  7.3 0.7 all-gather.5.cloned.1.call-update
  8.0 6.4 copy.13
  14.4 6.4 all-to-all-start
  20.8 0.1 slice_reduce_fusion
  20.9 0.1 reshape_squeeze.3
  21.0 0.1 reshape.70
  21.1 0.7 gather_fusion
  21.8 0.1 reshape.69
  22.0 92.5 %all-to-all-done = bf16[256,4,2048]{0,2,1:T(8,128)(2,1)} async-done(((bf16[256,4,2048]{0,2,1:T(8,128)(2,1)}), bf16[256,4,2048]{0,2,1:T(8,128)(2,1)}, u32[]{:S(2)}, u32[]{:S(2)}) %all-to-all-start) | async-done | bytes 4194336 | tf_op jit(solution)/shard_map/all_to_all | solution.py:19
  114.5 6.2 copy.14
  120.7 92.5 %all-gather.3.cloned.1.call-done = bf16[128,64,2048]{2,1,0:T(8,128)(2,1)} async-done(((bf16[32,64,2048]{2,1,0:T(8,128)(2,1)}), bf16[128,64,2048]{2,1,0:T(8,128)(2,1)}) %all-gather.3.cloned.1.call-update) | async-done | bytes 33554448 | tf_op jit(solution)/shard_map/all_gather | solution.py:28
  213.2 2.2 gather_fusion.1
  215.4 4.5 fusion.9
  219.9 0.0 reduce-scatter.2.cloned.1.call-start
  219.9 45.3 %convolution_convert_fusion = bf16[1024,8192]{1,0:T(8,128)(2,1)} fusion(bf16[1024,2048]{1,0:T(8,128)(2,1)} %bitcast.27, bf16[2048,8192]{1,0:T(8,128)(2,1)} %param.9), kind=kOutput, calls=%fused_computation.3 | convolution fusion | flops 34368126976 | bytes 54525952 | tf_op jit(solution)/shard_map/dot_general | solution.py:39
  265.2 151.1 %all-gather.5.cloned.1.call-done = bf16[128,64,2048]{2,1,0:T(8,128)(2,1)} async-done(((bf16[32,64,2048]{2,1,0:T(8,128)(2,1)}), bf16[128,64,2048]{2,1,0:T(8,128)(2,1)}) %all-gather.5.cloned.1.call-update) | async-done | bytes 33554448 | tf_op jit(solution)/shard_map/all_gather | solution.py:29
  416.3 2.2 gather_fusion.2
  418.5 34.6 %all-reduce.2.cloned.1.call-done = bf16[8,128,64]{1,2,0:T(8,128)(2,1)} async-done(((bf16[8,128,64]{1,2,0:T(8,128)(2,1)}), bf16[8,128,64]{1,2,0:T(8,128)(2,1)}) %all-reduce.2.cloned.1.call-update) | async-done | bytes 131088 | tf_op jit(solution)/shard_map/psum | solution.py:36
  453.1 4.2 convolution_convert_fusion.1
  457.4 278.1 %reduce-scatter.2.cloned.1.call-done = bf16[1024,2048]{1,0:T(8,128)(2,1)} async-done(((bf16[1024,8192]{1,0:T(8,128)(2,1)}), bf16[1024,2048]{1,0:T(8,128)(2,1)}) %reduce-scatter.2.cloned.1.call-update) | async-done | bytes 4194320 | tf_op jit(solution)/shard_map/reduce_scatter | solution.py:40
  735.4 5.4 fusion
  740.8 97.4 %all_to_all.38 = bf16[4,256,2048]{2,1,0:T(8,128)(2,1)S(1)} all-to-all(bf16[4,256,2048]{2,1,0:T(8,128)(2,1)S(1)} %bitcast.23), channel_id=1, replica_groups=mesh['groups'=2,'store'=4,'tensor'=4] {'tensor'}, dimensions={0} | all-to-all | bytes 8388608 | tf_op jit(solution)/shard_map/all_to_all | solution.py:44
  838.3 2.3 copy.17
  (15 shorter events, 0.1 us)
Async XLA Ops:
  6.5 14.6 %copy-start = (s32[128]{0:T(128)S(1)}, s32[128]{0:T(128)}, u32[]{:S(2)}) copy-start(s32[128]{0:T(128)} %param.13) | copy-start | bytes 1540
  6.5 206.6 %all-gather.3.cloned.1.call-start = ((), (), s32[]{:S(2)}) async-start(), calls=%async_computation.4 | async-start | bytes 41943040 | tf_op jit(solution)/shard_map/all_gather | solution.py:28
  7.3 409.0 %all-gather.5.cloned.1.call-start = ((), (), s32[]{:S(2)}) async-start(), calls=%async_computation.6 | async-start | bytes 41943040 | tf_op jit(solution)/shard_map/all_gather | solution.py:29
  14.4 6.5 copy-start.2
  14.4 100.1 %all-to-all-start = ((bf16[256,4,2048]{0,2,1:T(8,128)(2,1)}), bf16[256,4,2048]{0,2,1:T(8,128)(2,1)}, u32[]{:S(2)}, u32[]{:S(2)}) async-start(bf16[256,4,2048]{0,2,1:T(8,128)(2,1)} %bitcast.24), calls=%async_computation | async-start | bytes 8388608 | tf_op jit(solution)/shard_map/all_to_all | solution.py:19
  20.8 432.3 %all-reduce.2.cloned.1.call-start = ((), (), s32[]{:S(2)}) async-start(), calls=%async_computation.5 | async-start | bytes 262144 | tf_op jit(solution)/shard_map/psum | solution.py:36
  219.9 515.6 %reduce-scatter.2.cloned.1.call-start = ((), (), s32[]{:S(2)}) async-start(), calls=%async_computation.3 | async-start | bytes 20971520 | tf_op jit(solution)/shard_map/reduce_scatter | solution.py:40
  838.2 2.3 copy-start.1
Sparse Core Ops, SparseCore 0:
  8.9 204.2 all-gather.2
  214.7 201.5 all-gather.4
  418.6 34.4 all-reduce.1
  455.5 279.9 reduce-scatter.1
where the time goes:
time: 848 us; the launch traced here: 847 us
  waiting for transfers between devices  650 us (77%)
  blocking collectives  97.4 us (11%)
  matrix products  54 us (6%)
  local copies, waits for them, and re-layouts  20.3 us (2%)
  between operations  13.2 us (2%)
    reduce_scatter x1, waiting for transfers between devices, body(): lax.psum_scatter(partial_sum.astype(jnp.bfloat16), 'tensor', scatter_dime...  278 us
    all_gather x1, waiting for transfers between devices, body(): lax.all_gather(adapter_up_maps, 'store', axis=0, tiled=True)  151 us
    all_to_all x1, blocking collectives, body(): lax.all_to_all(mixed, 'tensor', split_axis=0, concat_axis=1, tiled=True)  97.4 us
    all_to_all x1, waiting for transfers between devices, body(): lax.all_to_all(normed_hidden_rows, 'tensor', split_axis=1, concat_axis=0,...  92.5 us
    all_gather x1, waiting for transfers between devices, body(): lax.all_gather(adapter_down_maps, 'store', axis=0, tiled=True)  92.5 us
    dot_general x1, matrix products, body(): jnp.dot(local_rows, base_query_weight, preferred_element_type=jnp.float32)  45.3 us
    psum x1, waiting for transfers between devices, body(): low = lax.psum(low_part.astype(jnp.bfloat16), 'tensor')  34.6 us
  transfers between devices with their start and end apart: 5, of which 5 were waited for; matrix products, arithmetic and copies ran while one was open for 8% of the time, Pallas kernels for 0%

commit v1 on v0

v1 whole, which is shorter than its diff:
```python
import jax
import jax.numpy as jnp
from jax import lax
from jax.sharding import PartitionSpec as P

TILE = 128
F32 = jnp.float32
BF16 = jnp.bfloat16


def xor_perm(x, axis, d):
    return lax.ppermute(x, axis, [(i, i ^ d) for i in range(lax.axis_size(axis))])


def pick(bank, first, slots):
    count = bank.shape[0]
    held = (slots >= first) & (slots < first + count)
    return jnp.take(bank, jnp.clip(slots - first, 0, count - 1), axis=0), held[:, None, None]


def fetch_maps(bank, slots, me):
    n = lax.axis_size("store")
    first = me * bank.shape[0]
    if n != 4:
        return jnp.take(lax.all_gather(bank, "store", axis=0, tiled=True), slots[me], axis=0)
    own, own_held = pick(bank, first, slots[me])
    mate, _ = pick(bank, first, slots[me ^ 1])
    far, far_held = pick(bank, first, slots[me ^ 2])
    far_mate, _ = pick(bank, first, slots[me ^ 3])
    from_mate = xor_perm(mate, "store", 1)
    far_from_mate = xor_perm(far_mate, "store", 1)
    from_far = xor_perm(jnp.where(far_held, far, far_from_mate), "store", 2)
    mate_first = (me ^ 1) * bank.shape[0]
    mate_held = (slots[me] >= mate_first) & (slots[me] < mate_first + bank.shape[0])
    return jnp.where(own_held, own, jnp.where(mate_held[:, None, None], from_mate, from_far))


def body(x, w, down, up, ids, slot_of):
    stores = lax.axis_size("store")
    n = lax.axis_size("tensor")
    si = lax.axis_index("store")
    ti = lax.axis_index("tensor")
    rows = x.shape[0]
    feat = w.shape[0]
    slots = slot_of[ids.reshape(-1, TILE)[:, 0]].reshape(stores, -1)
    tiles = slots.shape[1]
    blocks = x.reshape(rows, n, feat).transpose(1, 0, 2)
    blocks = lax.all_to_all(blocks, "tensor", split_axis=0, concat_axis=0, tiled=True)
    local = blocks.reshape(n * rows, feat)
    tile_down = fetch_maps(down, slots, si)
    tile_up = fetch_maps(up, slots, si)
    low = jnp.einsum("tnd,trd->tnr", local.reshape(tiles, TILE, feat), tile_down, preferred_element_type=F32)
    low = lax.psum(low.astype(BF16), "tensor")
    delta = jnp.einsum("tnr,trd->tnd", low, tile_up, preferred_element_type=F32).reshape(n * rows, feat)
    part = jnp.dot(local, w, preferred_element_type=F32).astype(BF16)
    w_own = lax.dynamic_slice_in_dim(w, ti * feat, feat, 1)
    own = jnp.dot(local, w_own, preferred_element_type=F32) + delta
    part = lax.dynamic_update_slice_in_dim(part, own.astype(BF16), ti * feat, 1)
    return lax.psum_scatter(part, "tensor", scatter_dimension=0, tiled=True)


def solution(mesh):
    return jax.shard_map(
        body,
        mesh=mesh,
        in_specs=(
            P(("groups", "store", "tensor"), None),
            P("tensor", None),
            P("store", None, "tensor"),
            P("store", None, "tensor"),
            P("groups"),
            P(),
        ),
        out_specs=P(("groups", "store", "tensor"), None),
        check_vma=False,
    )
```

time: 848 us -> 471 us (0.56)
  waiting for transfers between devices: 650 us -> 318 us
  blocking collectives: 97.4 us -> 0 us
  local copies, waits for them, and re-layouts: 20.3 us -> 51.2 us
  matrix products: 54 us -> 64.6 us
    all_gather x2 -> x0, waiting for transfers between devices: 244 us -> none  [the longest x1 151 us: body(): lax.all_gather(adapter_up_maps, 'store', axis=0, tiled=True)]
    all_to_all x1 -> x0, blocking collectives: 97.4 us -> none  [body(): lax.all_to_all(mixed, 'tensor', split_axis=0, concat_axis=1, tiled=True)]
    all_to_all x1, waiting for transfers between devices: 92.5 us -> 38 us  [body(): lax.all_to_all(blocks, 'tensor', split_axis=0, concat_axis=0, tiled=True)]
    psum x1, waiting for transfers between devices: 34.6 us -> 0.02 us  [body(): low = lax.psum(low.astype(BF16), 'tensor')]
    gather x4 -> x9, local copies, waits for them, and re-layouts: 5.15 us -> 38.5 us  [the longest x8 37.8 us: pick(): jnp.take(bank, jnp.clip(slots - first, 0, count - 1), axis=0)]
    select_n x1 -> x4, other arithmetic: 0.01 us -> 13.9 us  [the longest x2 8.24 us: pick(): jnp.take(bank, jnp.clip(slots - first, 0, count - 1), axis=0)]
    dot_general x3 -> x4, matrix products: 54 us -> 64.6 us  [the longest x1 41.9 us: body(): part = jnp.dot(local, w, preferred_element_type=F32).astype(BF16)]
  transfers between devices with their start and end apart: 5 -> 9, of which waited for: 5 -> 2; matrix products, arithmetic and copies ran while one was open for 8% -> 23% of each run, Pallas kernels for 0% -> 0%
where the time goes in v1:
time: 471 us; the launch traced here: 470 us
  waiting for transfers between devices  318 us (68%)
  matrix products  64.6 us (14%)
  local copies, waits for them, and re-layouts  51.2 us (11%)
  other arithmetic  13.9 us (3%)
  between operations  13.5 us (3%)
  starting transfers between devices  9.44 us (2%)
    reduce_scatter x1, waiting for transfers between devices, body(): return lax.psum_scatter(part, 'tensor', scatter_dimension=0, tiled=True)  280 us
    dot_general x1, matrix products, body(): part = jnp.dot(local, w, preferred_element_type=F32).astype(BF16)  41.9 us
    all_to_all x1, waiting for transfers between devices, body(): lax.all_to_all(blocks, 'tensor', split_axis=0, concat_axis=0, tiled=True)  38 us
    gather x8, local copies, waits for them, and re-layouts, pick(): jnp.take(bank, jnp.clip(slots - first, 0, count - 1), axis=0)  37.8 us
    dot_general x1, matrix products, body(): own = jnp.dot(local, w_own, preferred_element_type=F32) + delta  12.6 us
  transfers between devices with their start and end apart: 9, of which 2 were waited for; matrix products, arithmetic and copies ran while one was open for 23% of the time, Pallas kernels for 0%

profile of v1, /device:TPU:0, one launch (start us, length us, event | category | flops | bytes accessed | tf_op | source)
XLA Modules:
  0.0 470.3 jit_solution(14083752234095523497)
XLA Ops:
  6.5 6.4 %copy.9 = bf16[256,8192]{0,1:T(8,128)(2,1)} copy(bf16[256,8192]{1,0:T(8,128)(2,1)} %param.8) | data formatting | bytes 8388608 | tf_op args[0]
  12.9 6.4 %all-to-all-start = ((bf16[4,256,2048]{1,2,0:T(8,128)(2,1)}), bf16[4,256,2048]{1,2,0:T(8,128)(2,1)}, u32[]{:S(2)}, u32[]{:S(2)}) async-start(bf16[4,256,2048]{1,2,0:T(8,128)(2,1)} %bitcast.41), calls=%async_computation | async-start | bytes 8388608 | tf_op jit(solution)/shard_map/all_to_all | solution.py:48
  19.5 0.7 gather_fusion
  20.3 4.1 gather_fusion.8
  24.4 5.4 %gather_fusion.4 = bf16[8,64,2048]{2,1,0:T(8,128)(2,1)} fusion(bf16[32,64,2048]{2,1,0:T(8,128)(2,1)} %param.10, s32[1024]{0:T(1024)S(1)} %pad_clamp_fusion), kind=kCustom, calls=%fused_computation.3.clone | custom fusion | bytes 4194336 | tf_op jit(solution)/shard_map/jit(_take)/gather | solution.py:18
  29.8 4.1 broadcast_select_fusion
  33.9 0.5 collective-permute-start.1
  34.4 4.1 gather_fusion.6
  38.5 5.4 %gather_fusion.2 = bf16[8,64,2048]{2,1,0:T(8,128)(2,1)} fusion(bf16[32,64,2048]{2,1,0:T(8,128)(2,1)} %param.10, s32[1024]{0:T(1024)S(1)} %pad_clamp_fusion.2), kind=kCustom, calls=%fused_computation.1.clone | custom fusion | bytes 4194336 | tf_op jit(solution)/shard_map/jit(_take)/gather | solution.py:18
  43.8 4.1 broadcast_select_fusion.2
  48.0 4.1 gather_fusion.7
  52.1 5.4 %gather_fusion.3 = bf16[8,64,2048]{2,1,0:T(8,128)(2,1)} fusion(bf16[32,64,2048]{2,1,0:T(8,128)(2,1)} %param.10, s32[1024]{0:T(1024)S(1)} %pad_clamp_fusion.1), kind=kCustom, calls=%fused_computation.2.clone | custom fusion | bytes 4194336 | tf_op jit(solution)/shard_map/jit(_take)/gather | solution.py:18
  57.5 5.5 %select_select_fusion = (bf16[8,64,2048]{2,1,0:T(8,128)(2,1)}, bf16[8,64,2048]{2,1,0:T(8,128)(2,1)}) fusion(bf16[8,64,2048]{2,1,0:T(8,128)(2,1)} %collective-permute-done.4, bf16[8,64,2048]{2,1,0:T(8,128)(2,1)S(1)} %gather_fusion.7, pred[8]{0:T(512)(128)(4,1)S(1)} %get-tuple-element.8, pred[8]{0:T(512)(128)(4,1)S(1)} %get-tuple-element.16, ...), kind=kLoop, calls=%fused_computation.15 | loop fusion | flops 4194304 | bytes 12582928 | tf_op jit(solution)/shard_map/jit(_where)/select_n | solution.py:32
  63.0 1.6 collective-permute-start.2
  64.8 4.1 gather_fusion.5
  68.9 5.4 %gather_fusion.1 = bf16[8,64,2048]{2,1,0:T(8,128)(2,1)} fusion(bf16[32,64,2048]{2,1,0:T(8,128)(2,1)} %param.10, s32[1024]{0:T(1024)S(1)} %pad_clamp_fusion.3), kind=kCustom, calls=%fused_computation.clone | custom fusion | bytes 4194336 | tf_op jit(solution)/shard_map/jit(_take)/gather | solution.py:18
  74.3 0.5 collective-permute-start.5
  74.8 38.0 %all-to-all-done = bf16[4,256,2048]{1,2,0:T(8,128)(2,1)} async-done(((bf16[4,256,2048]{1,2,0:T(8,128)(2,1)}), bf16[4,256,2048]{1,2,0:T(8,128)(2,1)}, u32[]{:S(2)}, u32[]{:S(2)}) %all-to-all-start) | async-done | bytes 4194336 | tf_op jit(solution)/shard_map/all_to_all | solution.py:48
  112.8 6.2 %copy.10 = bf16[4,256,2048]{2,1,0:T(8,128)(2,1)} copy(bf16[4,256,2048]{1,2,0:T(8,128)(2,1)} %all-to-all-done) | data formatting | bytes 8388608 | tf_op jit(solution)/shard_map/all_to_all | solution.py:48
  119.0 6.3 %fusion.19 = bf16[8,128,64]{1,2,0:T(8,128)(2,1)} fusion(bf16[8,128,2048]{2,1,0:T(8,128)(2,1)} %bitcast.42, bf16[8,64,2048]{2,1,0:T(8,128)(2,1)} %gather_fusion.1, bf16[8,64,2048]{2,1,0:T(8,128)(2,1)} %collective-permute-done, bf16[8,64,2048]{2,1,0:T(8,128)(2,1)} %collective-permute-done.2, pred[8]{0:T(512)(128)(4,1)S(1)} %get-tuple-element.17, ...), kind=kOutput, calls=%fused_computation.34 | convolution fusion | flops 271646720 | bytes 10616856 | tf_op jit(solution)/shard_map/tnd,trd->tnr/dot_general | solution.py:52
  125.6 41.9 %convolution_convert_fusion = bf16[1024,8192]{1,0:T(8,128)(2,1)} fusion(bf16[1024,2048]{1,0:T(8,128)(2,1)} %bitcast.43, bf16[2048,8192]{1,0:T(8,128)(2,1)} %param.9), kind=kOutput, calls=%fused_computation.9 | convolution fusion | flops 34368126976 | bytes 54525952 | tf_op jit(solution)/shard_map/dot_general | solution.py:55
  167.5 3.8 fusion.8
  171.3 12.6 %fusion.5 = bf16[1024,8192]{1,0:T(8,128)(2,1)} fusion(bf16[1024,8192]{1,0:T(8,128)(2,1)} %convolution_convert_fusion, s32[]{:T(128)S(6)} %select_n.54, f32[8,128,2048]{2,1,0:T(8,128)S(1)} %fusion.8, bf16[1024,2048]{1,0:T(8,128)(2,1)S(1)} %bitcast.44, bf16[2048,8192]{1,0:T(8,128)(2,1)} %param.9), kind=kOutput, calls=%fused_computation.14 | convolution fusion | flops 8594128896 | bytes 25166848 | tf_op jit(solution)/shard_map/dot_general | solution.py:57
  183.9 279.6 %reduce-scatter.2.cloned.1.call-done = bf16[256,8192]{1,0:T(8,128)(2,1)} async-done(((bf16[1024,8192]{1,0:T(8,128)(2,1)}), bf16[256,8192]{1,0:T(8,128)(2,1)}) %reduce-scatter.2.cloned.1.call-update) | async-done | bytes 4194320 | tf_op jit(solution)/shard_map/reduce_scatter | solution.py:59
  (31 shorter events, 0.8 us)
Async XLA Ops:
  6.5 13.0 %copy-start = (s32[128]{0:T(128)S(1)}, s32[128]{0:T(128)}, u32[]{:S(2)}) copy-start(s32[128]{0:T(128)} %param.13) | copy-start | bytes 1540
  12.9 6.5 %copy-start.3 = (s32[4096]{0:T(1024)S(1)}, s32[4096]{0:T(1024)}, u32[]{:S(2)}) copy-start(s32[4096]{0:T(1024)} %param.12) | copy-start | bytes 49156
  12.9 99.9 %all-to-all-start = ((bf16[4,256,2048]{1,2,0:T(8,128)(2,1)}), bf16[4,256,2048]{1,2,0:T(8,128)(2,1)}, u32[]{:S(2)}, u32[]{:S(2)}) async-start(bf16[4,256,2048]{1,2,0:T(8,128)(2,1)} %bitcast.41), calls=%async_computation | async-start | bytes 8388608 | tf_op jit(solution)/shard_map/all_to_all | solution.py:48
  19.4 148.1 %all-reduce.2.cloned.1.call-start = ((), (), s32[]{:S(2)}) async-start(), calls=%async_computation.2 | async-start | bytes 262144 | tf_op jit(solution)/shard_map/psum | solution.py:53
  33.9 23.6 %collective-permute-start.4 = (bf16[8,64,2048]{2,1,0:T(8,128)(2,1)}, bf16[8,64,2048]{2,1,0:T(8,128)(2,1)}, u32[]{:S(2)}, u32[]{:S(2)}) collective-permute-start(bf16[8,64,2048]{2,1,0:T(8,128)(2,1)} %get-tuple-element.25), channel_id=1, source_target_pairs={{0,4},{4,0},{8,12},{12,8},{1,5},{5,1},{9,13},{13,9},{2,6},{6,2},{1... | collective-permute-start | bytes 6291464 | tf_op jit(solution)/shard_map/ppermute | solution.py:12
  33.9 23.6 %collective-permute-start.1 = (bf16[8,64,2048]{2,1,0:T(8,128)(2,1)}, bf16[8,64,2048]{2,1,0:T(8,128)(2,1)}, u32[]{:S(2)}, u32[]{:S(2)}) collective-permute-start(bf16[8,64,2048]{2,1,0:T(8,128)(2,1)} %get-tuple-element.26), channel_id=1, source_target_pairs={{0,4},{4,0},{8,12},{12,8},{1,5},{5,1},{9,13},{13,9},{2,6},{6,2},{1... | collective-permute-start | bytes 6291464 | tf_op jit(solution)/shard_map/ppermute | solution.py:12
  48.0 71.0 %collective-permute-start = (bf16[8,64,2048]{2,1,0:T(8,128)(2,1)}, bf16[8,64,2048]{2,1,0:T(8,128)(2,1)}, u32[]{:S(2)}, u32[]{:S(2)}) collective-permute-start(bf16[8,64,2048]{2,1,0:T(8,128)(2,1)} %get-tuple-element.28), channel_id=1, source_target_pairs={{0,4},{4,0},{8,12},{12,8},{1,5},{5,1},{9,13},{13,9},{2,6},{6,2},{1... | collective-permute-start | bytes 6291464 | tf_op jit(solution)/shard_map/ppermute | solution.py:12
  63.0 56.0 %collective-permute-start.2 = (bf16[8,64,2048]{2,1,0:T(8,128)(2,1)}, bf16[8,64,2048]{2,1,0:T(8,128)(2,1)}, u32[]{:S(2)}, u32[]{:S(2)}) collective-permute-start(bf16[8,64,2048]{2,1,0:T(8,128)(2,1)} %get-tuple-element.24), channel_id=1, source_target_pairs={{0,8},{4,12},{8,0},{12,4},{1,9},{5,13},{9,1},{13,5},{2,10},{6,14},... | collective-permute-start | bytes 6291464 | tf_op jit(solution)/shard_map/ppermute | solution.py:12
  64.6 102.9 %collective-permute-start.3 = (bf16[8,64,2048]{2,1,0:T(8,128)(2,1)}, bf16[8,64,2048]{2,1,0:T(8,128)(2,1)}, u32[]{:S(2)}, u32[]{:S(2)}) collective-permute-start(bf16[8,64,2048]{2,1,0:T(8,128)(2,1)} %get-tuple-element.27), channel_id=1, source_target_pairs={{0,4},{4,0},{8,12},{12,8},{1,5},{5,1},{9,13},{13,9},{2,6},{6,2},{1... | collective-permute-start | bytes 6291464 | tf_op jit(solution)/shard_map/ppermute | solution.py:12
  74.3 93.2 %collective-permute-start.5 = (bf16[8,64,2048]{2,1,0:T(8,128)(2,1)}, bf16[8,64,2048]{2,1,0:T(8,128)(2,1)}, u32[]{:S(2)}, u32[]{:S(2)}) collective-permute-start(bf16[8,64,2048]{2,1,0:T(8,128)(2,1)} %get-tuple-element.23), channel_id=1, source_target_pairs={{0,8},{4,12},{8,0},{12,4},{1,9},{5,13},{9,1},{13,5},{2,10},{6,14},... | collective-permute-start | bytes 6291464 | tf_op jit(solution)/shard_map/ppermute | solution.py:12
  125.3 338.1 %reduce-scatter.2.cloned.1.call-start = ((), (), s32[]{:S(2)}) async-start(), calls=%async_computation.3 | async-start | bytes 20971520 | tf_op jit(solution)/shard_map/reduce_scatter | solution.py:59
  167.5 3.8 copy-start.2
  183.9 279.6 %copy-start.1 = (s32[128]{0:T(128)S(1)}, s32[128]{0:T(128)}, u32[]{:S(2)}) copy-start(s32[128]{0:T(128)} %param.13) | copy-start | bytes 1540
Sparse Core Ops, SparseCore 0:
  125.5 33.5 all-reduce.1
  184.0 279.4 reduce-scatter.1

commit v2 on v1

--- a/solution.py
+++ b/solution.py
@@ -1,6 +1,8 @@
 import jax
 import jax.numpy as jnp
 from jax import lax
+from jax.experimental import pallas as pl
+from jax.experimental.pallas import tpu as pltpu
 from jax.sharding import PartitionSpec as P
 
 TILE = 128
@@ -35,7 +37,7 @@
     return jnp.where(own_held, own, jnp.where(mate_held[:, None, None], from_mate, from_far))
 
 
-def body(x, w, down, up, ids, slot_of):
+def general_body(x, w, down, up, ids, slot_of):
     stores = lax.axis_size("store")
     n = lax.axis_size("tensor")
     si = lax.axis_index("store")
@@ -59,6 +61,231 @@
     return lax.psum_scatter(part, "tensor", scatter_dimension=0, tiled=True)
 
 
+PLANE = ("groups", "store")
+COLS = 512
+VMEM = 48 * 1024 * 1024
+
+
+def chunk_partial(ti, blocks, feat, width, rows, w, term, terms, d, arrived, whole=None, into=None):
+    first, stride = blocks
+    count, depth = rows.shape
+    per = width // COLS
+    step = feat // COLS
+    packed = lambda b, k, t: (0, b * per + k)
+    spread = lambda b, k, t: (0, (first + b * stride) * step + k)
+    operands = [rows, w]
+    specs = [pl.BlockSpec((count, depth), lambda b, k, t: (0, 0)), pl.BlockSpec((depth, COLS), spread)]
+    if term:
+        operands.append(terms)
+        specs.append(pl.BlockSpec((None, count, COLS), lambda b, k, t: (d, 0, k)))
+    for piece in arrived:
+        operands.append(piece)
+        specs.append(pl.BlockSpec((count, COLS), packed))
+    aliases = {}
+    if into is not None:
+        aliases = {1 + len(operands): 0}
+        operands.append(into)
+        specs.append(pl.BlockSpec(memory_space=pl.ANY))
+
+    def kernel(t_ref, rows_ref, w_ref, *refs):
+        total = jnp.dot(rows_ref[...], w_ref[...], preferred_element_type=F32)
+        refs, out_ref = list(refs[:-1]), refs[-1]
+        if term:
+            own = first + pl.program_id(0) * stride == t_ref[0]
+            total = total + jnp.where(own, refs.pop(0)[...].astype(F32), 0.0)
+        for ref in refs[: len(arrived)]:
+            total = total + ref[...].astype(F32)
+        out_ref[...] = total.astype(BF16)
+
+    out_cols = whole if whole else 2 * width
+    return pl.pallas_call(
+        kernel,
+        grid_spec=pltpu.PrefetchScalarGridSpec(
+            num_scalar_prefetch=1,
+            grid=(2, per),
+            in_specs=specs,
+            out_specs=pl.BlockSpec((count, COLS), spread if whole else packed),
+        ),
+        out_shape=jax.ShapeDtypeStruct((count, out_cols), BF16),
+        input_output_aliases=aliases,
+        compiler_params=pltpu.CompilerParams(vmem_limit_bytes=VMEM),
+        cost_estimate=pl.CostEstimate(
+            flops=4 * count * depth * width, bytes_accessed=4 * depth * width + 8 * count * width, transcendentals=0
+        ),
+    )(ti, *operands)
+
+
+def plane_product(ti, gathered, shards, total, out_dtype):
+    m, _ = gathered.shape
+    depth, cols = shards[0][1].shape
+    tm = 256
+    operands, specs = [], []
+    for d, shard in shards:
+        operands += [gathered, shard]
+        specs += [
+            pl.BlockSpec((tm, depth), lambda i, t, d=d: (i, t[0] ^ d)),
+            pl.BlockSpec((depth, cols), lambda i, t: (0, 0)),
+        ]
+    if total is not None:
+        operands.append(total)
+        specs.append(pl.BlockSpec((tm, cols), lambda i, t: (i, 0)))
+
+    def kernel(t_ref, *refs):
+        acc = None
+        for at in range(len(shards)):
+            term = jnp.dot(refs[2 * at][...], refs[2 * at + 1][...], preferred_element_type=F32)
+            acc = term if acc is None else acc + term
+        if total is not None:
+            acc = acc + refs[-2][...]
+        refs[-1][...] = acc.astype(out_dtype)
+
+    return pl.pallas_call(
+        kernel,
+        grid_spec=pltpu.PrefetchScalarGridSpec(
+            num_scalar_prefetch=1,
+            grid=(m // tm,),
+            in_specs=specs,
+            out_specs=pl.BlockSpec((tm, cols), lambda i, t: (i, 0)),
+        ),
+        out_shape=jax.ShapeDtypeStruct((m, cols), out_dtype),
+        compiler_params=pltpu.CompilerParams(vmem_limit_bytes=VMEM),
+        cost_estimate=pl.CostEstimate(
+            flops=2 * m * depth * cols * len(shards),
+            bytes_accessed=(2 * m * depth + 2 * depth * cols) * len(shards) + 8 * m * cols,
+            transcendentals=0,
+        ),
+    )(ti, *operands)
+
+
+def plane_finish(ti, back, low, up_rel, feat, width, into):
+    parts, count, cols = back.shape
+    per = (feat - width) // cols
+    tiles, tile, rank = low.shape
+
+    def kernel(t_ref, back_ref, low_ref, up_ref, into_ref, out_ref):
+        for t in range(tiles):
+            delta = jnp.dot(low_ref[t], up_ref[t], preferred_element_type=F32).astype(BF16)
+            at = pl.ds(t * tile, tile)
+            out_ref[at, :] = (back_ref[at, :].astype(F32) + delta.astype(F32)).astype(BF16)
+
+    return pl.pallas_call(
+        kernel,
+        grid_spec=pltpu.PrefetchScalarGridSpec(
+            num_scalar_prefetch=1,
+            grid=(parts // per, per),
+            in_specs=[
+                pl.BlockSpec((None, count, cols), lambda j, k, t: (j * per + k, 0, 0)),
+                pl.BlockSpec((tiles, tile, rank), lambda j, k, t: (0, 0, 0)),
+                pl.BlockSpec((None, tiles, rank, cols), lambda j, k, t: (j ^ t[0], 0, 0, k)),
+                pl.BlockSpec(memory_space=pl.ANY),
+            ],
+            out_specs=pl.BlockSpec((count, cols), lambda j, k, t: (0, j * (feat // cols) + width // cols + k)),
+        ),
+        out_shape=jax.ShapeDtypeStruct(into.shape, BF16),
+        input_output_aliases={4: 0},
+        compiler_params=pltpu.CompilerParams(vmem_limit_bytes=VMEM),
+        cost_estimate=pl.CostEstimate(
+            flops=2 * parts * count * cols * rank, bytes_accessed=5 * parts * count * cols, transcendentals=0
+        ),
+    )(ti, back, low, up_rel, into)
+
+
+SPLIT = 2
+
+
+def line_body(x, w, down, up, ids, slot_of):
+    stores = lax.axis_size("store")
+    members = lax.axis_size("groups") * stores
+    n = 4
+    si = lax.axis_index("store")
+    ti = lax.axis_index("tensor")
+    pi = lax.axis_index("groups") * stores + si
+    scalar = ti.astype(jnp.int32).reshape(1)
+    rows = x.shape[0]
+    feat = w.shape[0]
+    own_tiles = rows // TILE
+    rank = down.shape[1]
+    plane_width = feat // SPLIT
+    width = feat - plane_width
+    end = (ti == 0) | (ti == n - 1)
+    ends_out = [(0, 1), (3, 2)]
+    inward_right, inward_left = [(0, 1), (1, 2)], [(3, 2), (2, 1)]
+    middle = [(1, 2), (2, 1)]
+    to_ends = [(1, 0), (2, 3)]
+    send = lambda v, pairs: lax.ppermute(v, "tensor", pairs)
+
+    slots = slot_of[ids.reshape(-1, TILE)[:, 0]].reshape(stores, n, own_tiles)
+    slots = jnp.take(slots, ti ^ jnp.arange(n), axis=1).reshape(stores, n * own_tiles)
+
+    piece = [lax.dynamic_slice_in_dim(x, (ti ^ d) * feat, feat, 1) for d in range(n)]
+    for d in (3, 2, 1):
+        piece[d] = xor_perm(piece[d], "tensor", d)
+
+    gathered = lax.all_gather(x, PLANE, axis=0, tiled=True)
+    tile_down = fetch_maps(down, slots, si)
+    tile_up = fetch_maps(up, slots, si)
+
+    cols = plane_width * n // members
+    per = plane_width // cols
+    w_own = lax.dynamic_slice_in_dim(w, (pi // per) * feat + width + (pi % per) * cols, cols, 1)
+    w_own, piece[1], piece[2], piece[3] = lax.optimization_barrier((w_own, piece[1], piece[2], piece[3]))
+    w_near = xor_perm(w_own, "tensor", 1)
+    w_mid = send(w_own, middle)
+    w_end2 = send(w_mid, to_ends)
+    w_mid2 = send(w_near, middle)
+    w_end3 = send(w_mid2, to_ends)
+    w_two = jnp.where(end, w_end2, w_mid2)
+    w_three = jnp.where(end, w_end3, w_mid)
+
+    low = jnp.stack([
+        jnp.einsum(
+            "tnd,trd->tnr",
+            piece[d].reshape(own_tiles, TILE, feat),
+            tile_down[d * own_tiles : (d + 1) * own_tiles],
+            preferred_element_type=F32,
+        )
+        for d in range(n)
+    ])
+    pair = low.shape[1:]
+    near = xor_perm(low.astype(BF16), "tensor", 1).reshape(2, 2, *pair)[:, ::-1].reshape(n, *pair)
+    low = low + near.astype(F32)
+    far = xor_perm(low.astype(BF16), "tensor", 2).reshape(2, 2, *pair)[::-1].reshape(n, *pair)
+    low = (low + far.astype(F32)).astype(BF16)
+    tile_up = tile_up.reshape(n, own_tiles, rank, feat)
+    terms = jnp.einsum("dtnr,dtrc->dtnc", low, tile_up[..., :width], preferred_element_type=F32)
+    terms = terms.astype(BF16).reshape(n, rows, width)
+    up_plane = tile_up[..., width:]
+    up_rel = jnp.stack([up_plane[0]] + [xor_perm(up_plane[d], "tensor", d) for d in range(1, n)])
+
+    def partial(chunk, d, arrived=(), term=True, **kw):
+        return chunk_partial(scalar, chunk, feat, width, piece[d], w, term, terms, d, arrived, **kw)
+
+    inner, outer = (1, 1), (0, 3)
+    first = [send(partial(inner, 3, term=False), ends_out), send(partial(outer, 3), ends_out)]
+    out = None
+    arrived = []
+    for chunk, came in zip((inner, outer), first):
+        second = partial(chunk, 2, (came,))
+        right, left = send(second, inward_right), send(second, inward_left)
+        to_near = partial(chunk, 1, (jnp.where(ti == 1, left, right),))
+        to_mid = partial(chunk, 3, (jnp.where(ti == 1, right, left),))
+        arrived.append((xor_perm(to_near, "tensor", 1), send(to_mid, middle)))
+
+    total = plane_product(scalar, gathered, [(0, w_own), (1, w_near)], None, F32)
+    total = plane_product(scalar, gathered, [(2, w_two), (3, w_three)], total, BF16)
+    back = lax.all_to_all(total.reshape(members, rows, cols), PLANE, split_axis=0, concat_axis=0, tiled=True)
+
+    for chunk, came in zip((inner, outer), arrived):
+        out = partial(chunk, 0, came, whole=n * feat, into=out)
+    return plane_finish(scalar, back, low[0], up_rel, feat, width, out)
+
+
+def body(x, w, down, up, ids, slot_of):
+    line = lax.axis_size("tensor") == 4 and lax.axis_size("store") == 4 and lax.axis_size("groups") == 2
+    line = line and x.shape[0] % TILE == 0 and w.shape[0] % (2 * COLS) == 0
+    return (line_body if line else general_body)(x, w, down, up, ids, slot_of)
+
+
 def solution(mesh):
     return jax.shard_map(
         body,

time: 471 us -> 500 us (1.062)
  waiting for transfers between devices: 318 us -> 205 us
  Pallas kernels: 0 us -> 99.4 us
  starting transfers between devices: 9.44 us -> 81.5 us
  matrix products: 64.6 us -> 4.84 us
  other arithmetic: 13.9 us -> 32.7 us
  local copies, waits for them, and re-layouts: 51.2 us -> 60.1 us
    reduce_scatter x1 -> x0, waiting for transfers between devices: 280 us -> none  [body(): return lax.psum_scatter(part, 'tensor', scatter_dimension=0, tiled=True)]
    ppermute x6 -> x17, waiting for transfers between devices: 0.02 us -> 189 us  [xor_perm(): lax.ppermute(x, axis, [(i, i ^ d) for i in range(lax.axis_size(axis))])]
    pallas_call x0 -> x13, Pallas kernels: none -> 99.4 us  [the longest x10 63.1 us: chunk_partial(): pl.pallas_call(kernel, grid_spec=pltpu.PrefetchScalarGridSpec(num_scalar_...]
    dot_general x4 -> x5, matrix products: 64.6 us -> 4.84 us  [the longest x4 2.93 us: line_body(): jnp.einsum('tnd,trd->tnr', piece[d].reshape(own_tiles, TILE, feat), tile_...]
    ppermute x6 -> x17, starting transfers between devices: 2.77 us -> 42.8 us  [xor_perm(): lax.ppermute(x, axis, [(i, i ^ d) for i in range(lax.axis_size(axis))])]
    all_to_all x1, waiting for transfers between devices: 38 us -> 0.01 us  [line_body(): lax.all_to_all(total.reshape(members, rows, cols), PLANE, split_axis=0, c...]
    ppermute x0 -> x12, starting transfers between devices: none -> 34.4 us  [line_body(): send = lambda v, pairs: lax.ppermute(v, 'tensor', pairs)]
    select_n x1 -> x8, other arithmetic: 0.11 us -> 16.5 us  [the longest x1 6.62 us: fetch_maps(): jnp.where(own_held, own, jnp.where(mate_held[:, None, None], from_mate, f...]
  transfers between devices with their start and end apart: 9 -> 31, of which waited for: 2 -> 8; matrix products, arithmetic and copies ran while one was open for 23% -> 19% of each run, Pallas kernels for 0% -> 19%
where the time goes in v2:
time: 500 us; the launch traced here: 497 us
  waiting for transfers between devices  205 us (41%)
  Pallas kernels  99.4 us (20%)
  starting transfers between devices  81.5 us (16%)
  local copies, waits for them, and re-layouts  60.1 us (12%)
  other arithmetic  32.7 us (7%)
  between operations  13.8 us (3%)
    ppermute x17, waiting for transfers between devices, xor_perm(): lax.ppermute(x, axis, [(i, i ^ d) for i in range(lax.axis_size(axis))])  189 us
    pallas_call x10, Pallas kernels, chunk_partial(): pl.pallas_call(kernel, grid_spec=pltpu.PrefetchScalarGridSpec(num_scalar_...  63.1 us
    gather x8, local copies, waits for them, and re-layouts, pick(): jnp.take(bank, jnp.clip(slots - first, 0, count - 1), axis=0)  45.7 us
    ppermute x17, starting transfers between devices, xor_perm(): lax.ppermute(x, axis, [(i, i ^ d) for i in range(lax.axis_size(axis))])  42.8 us
    ppermute x12, starting transfers between devices, line_body(): send = lambda v, pairs: lax.ppermute(v, 'tensor', pairs)  34.4 us
    pallas_call x2, Pallas kernels, plane_product(): pl.pallas_call(kernel, grid_spec=pltpu.PrefetchScalarGridSpec(num_scalar_...  30 us
    ppermute x12, waiting for transfers between devices, line_body(): send = lambda v, pairs: lax.ppermute(v, 'tensor', pairs)  15 us
  transfers between devices with their start and end apart: 31, of which 8 were waited for; matrix products, arithmetic and copies ran while one was open for 19% of the time, Pallas kernels for 19%

profile of v2, /device:TPU:0, one launch (start us, length us, event | category | flops | bytes accessed | tf_op | source)
XLA Modules:
  0.0 497.1 jit_solution(6830891502729202794)
XLA Ops:
  16.4 6.5 %gather_fusion.9 = bf16[8,64,2048]{2,1,0:T(8,128)(2,1)} fusion(bf16[32,64,2048]{2,1,0:T(8,128)(2,1)} %param.11, s32[1024]{0:T(1024)S(1)} %pad_clamp_fusion), kind=kCustom, calls=%fused_computation.7.clone | custom fusion | bytes 4194336 | tf_op jit(solution)/shard_map/jit(_take)/gather | solution.py:20
  22.9 6.8 %gather_fusion.5 = bf16[8,64,2048]{2,1,0:T(8,128)(2,1)} fusion(bf16[32,64,2048]{2,1,0:T(8,128)(2,1)} %param.10, s32[1024]{0:T(1024)S(1)} %pad_clamp_fusion), kind=kCustom, calls=%fused_computation.3.clone | custom fusion | bytes 4194336 | tf_op jit(solution)/shard_map/jit(_take)/gather | solution.py:20
  68.0 53.2 %collective-permute-done.1.rows_ref = bf16[256,2048]{1,0:T(8,128)(2,1)} collective-permute-done((bf16[256,2048]{1,0:T(8,128)(2,1)}, bf16[256,2048]{1,0:T(8,128)(2,1)}, u32[]{:S(2)}, u32[]{:S(2)}) %collective-permute-start.1) | collective-permute-done | bytes 1048608 | tf_op jit(solution)/shard_map/ppermute | solution.py:14
  123.2 24.6 %collective-permute-start.5 = (bf16[2048,512]{1,0:T(8,128)(2,1)}, bf16[2048,512]{1,0:T(8,128)(2,1)}, u32[]{:S(2)}, u32[]{:S(2)}) collective-permute-start(bf16[2048,512]{1,0:T(8,128)(2,1)} %constant_dynamic-slice_fusion.4.refs_1_), channel_id=1, source_target_pairs={{0,1},{1,0},{2,3},{3,2},{4,5},{5,4},{6,7},{7,6},{8,9},{9,8},{10,11... | collective-permute-start | bytes 6291464 | tf_op jit(solution)/shard_map/ppermute | solution.py:14
  166.8 26.7 %collective-permute-done.5.refs_3_ = bf16[2048,512]{1,0:T(8,128)(2,1)} collective-permute-done((bf16[2048,512]{1,0:T(8,128)(2,1)}, bf16[2048,512]{1,0:T(8,128)(2,1)}, u32[]{:S(2)}, u32[]{:S(2)}) %collective-permute-start.5) | collective-permute-done | bytes 2097184 | tf_op jit(solution)/shard_map/ppermute | solution.py:14
  195.5 19.1 %collective-permute-done.15 = bf16[8,64,2048]{2,1,0:T(8,128)(2,1)} collective-permute-done((bf16[8,64,2048]{2,1,0:T(8,128)(2,1)}, bf16[8,64,2048]{2,1,0:T(8,128)(2,1)}, u32[]{:S(2)}, u32[]{:S(2)}) %collective-permute-start.15) | collective-permute-done | bytes 2097184 | tf_op jit(solution)/shard_map/ppermute | solution.py:14
  214.6 44.5 %collective-permute-done.10 = bf16[8,64,2048]{2,1,0:T(8,128)(2,1)} collective-permute-done((bf16[8,64,2048]{2,1,0:T(8,128)(2,1)}, bf16[8,64,2048]{2,1,0:T(8,128)(2,1)}, u32[]{:S(2)}, u32[]{:S(2)}) %collective-permute-start.10) | collective-permute-done | bytes 2097184 | tf_op jit(solution)/shard_map/ppermute | solution.py:14
  259.1 6.6 %select_select_fusion.1 = (bf16[8,64,2048]{2,1,0:T(8,128)(2,1)}, bf16[8,64,2048]{2,1,0:T(8,128)(2,1)S(1)}) fusion(bf16[8,64,2048]{2,1,0:T(8,128)(2,1)} %gather_fusion.6, bf16[8,64,2048]{2,1,0:T(8,128)(2,1)} %collective-permute-done.13, bf16[8,64,2048]{2,1,0:T(8,128)(2,1)} %collective-permute-done.15, pred[8]{0:T(512)(128)(4,1)S(1)} %compare_and_fusion.3, ...), kind=kLoop, calls=%fused_computation.11 | loop fusion | flops 6291456 | bytes 16777240 | tf_op jit(solution)/shard_map/jit(_where)/select_n | solution.py:37
  270.3 6.3 %shard_map.70 = bf16[256,2048]{1,0:T(8,128)(2,1)} custom-call(s32[1]{0:T(128)} %bitcast.t_ref, bf16[256,2048]{1,0:T(8,128)(2,1)S(1)} %collective-permute-done.2.rows_ref, bf16[2048,8192]{1,0:T(8,128)(2,1)} %w_ref.19), custom_call_target="tpu_custom_call" | custom-call | flops 2147483648 | bytes 10485760 | tf_op jit(solution)/shard_map/pallas_call | solution.py:101
  280.5 26.3 %collective-permute-done.12 = bf16[4,2,128,64]{3,2,1,0:T(8,128)(2,1)S(1)} collective-permute-done((bf16[4,2,128,64]{3,2,1,0:T(8,128)(2,1)S(1)}, bf16[4,2,128,64]{3,2,1,0:T(8,128)(2,1)S(1)}, u32[]{:S(2)}, u32[]{:S(2)}) %collective-permute-start.12) | collective-permute-done | bytes 131104 | tf_op jit(solution)/shard_map/ppermute | solution.py:14
  308.9 6.4 %shard_map.66 = bf16[256,2048]{1,0:T(8,128)(2,1)} custom-call(s32[1]{0:T(128)} %bitcast.t_ref, bf16[256,2048]{1,0:T(8,128)(2,1)S(1)} %collective-permute-done.2.rows_ref, bf16[2048,8192]{1,0:T(8,128)(2,1)} %w_ref.19, bf16[4,256,1024]{2,1,0:T(8,128)(2,1)S(1)} %bitcast.47), custom_call_target="tpu_custom_call" | custom-call | flops 2147483648 | bytes 10485760 | tf_op jit(solution)/shard_map/pallas_call | solution.py:101
  315.3 7.2 %collective-permute-start.19 = (bf16[256,2048]{1,0:T(8,128)(2,1)}, bf16[256,2048]{1,0:T(8,128)(2,1)}, u32[]{:S(2)}, u32[]{:S(2)}) collective-permute-start(bf16[256,2048]{1,0:T(8,128)(2,1)} %shard_map.66), channel_id=1, source_target_pairs={{0,1},{3,2},{4,5},{7,6},{8,9},{11,10},{12,13},{15,14},{16,17},{19,... | collective-permute-start | bytes 3145736 | tf_op jit(solution)/shard_map/ppermute | solution.py:215
  323.8 6.9 %shard_map.71 = bf16[256,2048]{1,0:T(8,128)(2,1)} custom-call(s32[1]{0:T(128)} %bitcast.t_ref, bf16[256,2048]{1,0:T(8,128)(2,1)} %collective-permute-done.1.rows_ref, bf16[2048,8192]{1,0:T(8,128)(2,1)} %w_ref.19, bf16[4,256,1024]{2,1,0:T(8,128)(2,1)S(1)} %bitcast.48, bf16[256,2048]{1,0:T(8,128)(2,1)} %collective-permute-done.24.refs_1_), custom_call_target="tpu_custom_call" | custom-call | flops 2147483648 | bytes 10485760 | tf_op jit(solution)/shard_map/pallas_call | solution.py:101
  330.7 6.8 %collective-permute-start.26 = (bf16[256,2048]{1,0:T(8,128)(2,1)}, bf16[256,2048]{1,0:T(8,128)(2,1)}, u32[]{:S(2)}, u32[]{:S(2)}) collective-permute-start(bf16[256,2048]{1,0:T(8,128)(2,1)} %shard_map.71), channel_id=1, source_target_pairs={{0,1},{1,2},{4,5},{5,6},{8,9},{9,10},{12,13},{13,14},{16,17},{17,1... | collective-permute-start | bytes 3145736 | tf_op jit(solution)/shard_map/ppermute | solution.py:215
  346.9 6.8 %shard_map.67 = bf16[256,2048]{1,0:T(8,128)(2,1)} custom-call(s32[1]{0:T(128)} %bitcast.t_ref, bf16[256,2048]{1,0:T(8,128)(2,1)} %collective-permute-done.1.rows_ref, bf16[2048,8192]{1,0:T(8,128)(2,1)} %w_ref.19, bf16[4,256,1024]{2,1,0:T(8,128)(2,1)S(1)} %bitcast.49, bf16[256,2048]{1,0:T(8,128)(2,1)} %collective-permute-done.19.refs_1_), custom_call_target="tpu_custom_call" | custom-call | flops 2147483648 | bytes 10485760 | tf_op jit(solution)/shard_map/pallas_call | solution.py:101
  353.8 14.2 %collective-permute-done.26 = bf16[256,2048]{1,0:T(8,128)(2,1)} collective-permute-done((bf16[256,2048]{1,0:T(8,128)(2,1)}, bf16[256,2048]{1,0:T(8,128)(2,1)}, u32[]{:S(2)}, u32[]{:S(2)}) %collective-permute-start.26) | collective-permute-done | bytes 1048608 | tf_op jit(solution)/shard_map/ppermute | solution.py:215
  376.6 6.5 %shard_map.72 = bf16[256,2048]{1,0:T(8,128)(2,1)} custom-call(s32[1]{0:T(128)} %bitcast.t_ref, bf16[256,2048]{1,0:T(8,128)(2,1)S(1)} %copy-done.8, bf16[2048,8192]{1,0:T(8,128)(2,1)} %w_ref.19, bf16[4,256,1024]{2,1,0:T(8,128)(2,1)S(1)} %bitcast.50, bf16[256,2048]{1,0:T(8,128)(2,1)S(1)} %get-tuple-element.26.refs_1_), custom_call_target="tpu_custom_call" | custom-call | flops 2147483648 | bytes 10485760 | tf_op jit(solution)/shard_map/pallas_call | solution.py:101
  392.9 15.6 %shard_map.64.refs_4_ = f32[2048,512]{1,0:T(8,128)} custom-call(s32[1]{0:T(128)} %bitcast.t_ref, bf16[2048,8192]{1,0:T(8,128)(2,1)} %all-gather.2.cloned.1.call-done.refs_0_.refs_2_, bf16[2048,512]{1,0:T(8,128)(2,1)} %constant_dynamic-slice_fusion.4.refs_1_, bf16[2048,8192]{1,0:T(8,128)(2,1)} %all-gather.2.cloned.1.call-done.refs_0_.refs_2_, ...), custom_call_target="tpu_custom_call" | custom-call | flops 8589934592 | bytes 29360128 | tf_op jit(solution)/shard_map/pallas_call | solution.py:142
  408.5 14.4 %shard_map.65 = bf16[2048,512]{1,0:T(8,128)(2,1)S(1)} custom-call(s32[1]{0:T(128)} %bitcast.t_ref, bf16[2048,8192]{1,0:T(8,128)(2,1)} %all-gather.2.cloned.1.call-done.refs_0_.refs_2_, bf16[2048,512]{1,0:T(8,128)(2,1)S(1)} %copy-done.4, bf16[2048,8192]{1,0:T(8,128)(2,1)} %all-gather.2.cloned.1.call-done.refs_0_.refs_2_, ...), custom_call_target="tpu_custom_call" | custom-call | flops 8589934592 | bytes 29360128 | tf_op jit(solution)/shard_map/pallas_call | solution.py:142
  431.3 5.7 %shard_map.68 = bf16[256,2048]{1,0:T(8,128)(2,1)S(1)} custom-call(s32[1]{0:T(128)} %bitcast.t_ref, bf16[256,2048]{1,0:T(8,128)(2,1)S(1)} %copy-done.9, bf16[2048,8192]{1,0:T(8,128)(2,1)} %w_ref.19, bf16[4,256,1024]{2,1,0:T(8,128)(2,1)S(1)} %bitcast.52, bf16[256,2048]{1,0:T(8,128)(2,1)S(1)} %get-tuple-element.28.refs_1_), custom_call_target="tpu_custom_call" | custom-call | flops 2147483648 | bytes 10485760 | tf_op jit(solution)/shard_map/pallas_call | solution.py:101
  450.3 19.3 %collective-permute-done.16 = bf16[2,64,1024]{2,1,0:T(8,128)(2,1)S(1)} collective-permute-done((bf16[2,64,1024]{2,1,0:T(8,128)(2,1)S(1)}, bf16[2,64,1024]{2,1,0:T(8,128)(2,1)S(1)}, u32[]{:S(2)}, u32[]{:S(2)}) %collective-permute-start.16) | collective-permute-done | bytes 262176 | tf_op jit(solution)/shard_map/ppermute | solution.py:14
  470.8 6.6 %shard_map.74.refs_3_ = bf16[256,8192]{1,0:T(8,128)(2,1)} custom-call(s32[1]{0:T(128)} %bitcast.t_ref, bf16[256,2048]{1,0:T(8,128)(2,1)S(1)} %copy-done.3, bf16[2048,8192]{1,0:T(8,128)(2,1)} %w_ref.19, bf16[4,256,1024]{2,1,0:T(8,128)(2,1)S(1)} %bitcast.54, bf16[256,2048]{1,0:T(8,128)(2,1)} %collective-permute-done.27.refs_1_, ...), custom_call_target="tpu_custom_call" | custom-call | flops 2147483648 | bytes 10485760 | tf_op jit(solution)/shard_map/pallas_call | solution.py:101
  477.4 6.5 %shard_map.75.into_ref = bf16[256,8192]{1,0:T(8,128)(2,1)} custom-call(s32[1]{0:T(128)} %bitcast.t_ref, bf16[256,2048]{1,0:T(8,128)(2,1)S(1)} %copy-done.3, bf16[2048,8192]{1,0:T(8,128)(2,1)} %w_ref.19, bf16[4,256,1024]{2,1,0:T(8,128)(2,1)S(1)} %bitcast.55, bf16[256,2048]{1,0:T(8,128)(2,1)S(1)} %collective-permute-done.22.refs_1_, ...), custom_call_target="tpu_custom_call", output_to_operand_aliasing={{}: (6, {})} | custom-call | flops 2147483648 | bytes 10485760 | tf_op jit(solution)/shard_map/pallas_call | solution.py:101
  483.9 6.3 %shard_map.76 = bf16[256,8192]{1,0:T(8,128)(2,1)} custom-call(s32[1]{0:T(128)} %bitcast.t_ref, bf16[8,256,512]{2,1,0:T(8,128)(2,1)} %all-to-all-done.back_ref, bf16[2,128,64]{2,1,0:T(8,128)(2,1)S(1)} %slice_bitcast_fusion.3.low_ref, bf16[4,2,64,1024]{3,2,1,0:T(8,128)(2,1)S(1)} %pad_maximum_fusion.up_ref, ...), custom_call_target="tpu_custom_call", output_to_operand_aliasing={{}: (4, {})} | custom-call | flops 134217728 | bytes 5242880 | tf_op jit(solution)/shard_map/pallas_call | solution.py:171
  (138 shorter events, 133.4 us)
Async XLA Ops:
  6.5 386.4 %all-gather.2.cloned.1.call-start = ((), (), s32[]{:S(2)}) async-start(), calls=%async_computation.1 | async-start | bytes 37748736 | tf_op jit(solution)/shard_map/all_gather | solution.py:224
  11.2 41.6 %collective-permute-start = (bf16[256,2048]{1,0:T(8,128)(2,1)S(1)}, bf16[256,2048]{1,0:T(8,128)(2,1)S(1)}, u32[]{:S(2)}, u32[]{:S(2)}) collective-permute-start(bf16[256,2048]{1,0:T(8,128)(2,1)S(1)} %get-tuple-element.23), channel_id=1, source_target_pairs={{0,1},{1,0},{2,3},{3,2},{4,5},{5,4},{6,7},{7,6},{8,9},{9,8},{10,11... | collective-permute-start | bytes 3145736 | tf_op jit(solution)/shard_map/ppermute | solution.py:14
  34.4 88.8 %collective-permute-start.14 = (bf16[8,64,2048]{2,1,0:T(8,128)(2,1)}, bf16[8,64,2048]{2,1,0:T(8,128)(2,1)}, u32[]{:S(2)}, u32[]{:S(2)}) collective-permute-start(bf16[8,64,2048]{2,1,0:T(8,128)(2,1)} %get-tuple-element.37), channel_id=1, source_target_pairs={{0,4},{4,0},{8,12},{12,8},{1,5},{5,1},{9,13},{13,9},{2,6},{6,2},{1... | collective-permute-start | bytes 6291464 | tf_op jit(solution)/shard_map/ppermute | solution.py:14
  34.4 113.4 %collective-permute-start.9 = (bf16[8,64,2048]{2,1,0:T(8,128)(2,1)}, bf16[8,64,2048]{2,1,0:T(8,128)(2,1)}, u32[]{:S(2)}, u32[]{:S(2)}) collective-permute-start(bf16[8,64,2048]{2,1,0:T(8,128)(2,1)} %get-tuple-element.38), channel_id=1, source_target_pairs={{0,4},{4,0},{8,12},{12,8},{1,5},{5,1},{9,13},{13,9},{2,6},{6,2},{1... | collective-permute-start | bytes 6291464 | tf_op jit(solution)/shard_map/ppermute | solution.py:14
  50.5 103.7 %collective-permute-start.13 = (bf16[8,64,2048]{2,1,0:T(8,128)(2,1)}, bf16[8,64,2048]{2,1,0:T(8,128)(2,1)}, u32[]{:S(2)}, u32[]{:S(2)}) collective-permute-start(bf16[8,64,2048]{2,1,0:T(8,128)(2,1)} %get-tuple-element.39), channel_id=1, source_target_pairs={{0,4},{4,0},{8,12},{12,8},{1,5},{5,1},{9,13},{13,9},{2,6},{6,2},{1... | collective-permute-start | bytes 6291464 | tf_op jit(solution)/shard_map/ppermute | solution.py:14
  50.5 70.7 %collective-permute-start.1 = (bf16[256,2048]{1,0:T(8,128)(2,1)}, bf16[256,2048]{1,0:T(8,128)(2,1)}, u32[]{:S(2)}, u32[]{:S(2)}) collective-permute-start(bf16[256,2048]{1,0:T(8,128)(2,1)} %get-tuple-element.22), channel_id=1, source_target_pairs={{0,2},{1,3},{2,0},{3,1},{4,6},{5,7},{6,4},{7,5},{8,10},{9,11},{10,... | collective-permute-start | bytes 3145736 | tf_op jit(solution)/shard_map/ppermute | solution.py:14
  53.8 67.4 %collective-permute-start.2 = (bf16[256,2048]{1,0:T(8,128)(2,1)}, bf16[256,2048]{1,0:T(8,128)(2,1)S(1)}, u32[]{:S(2)}, u32[]{:S(2)}) collective-permute-start(bf16[256,2048]{1,0:T(8,128)(2,1)} %get-tuple-element.24), channel_id=1, source_target_pairs={{0,3},{1,2},{2,1},{3,0},{4,7},{5,6},{6,5},{7,4},{8,11},{9,10},{10,... | collective-permute-start | bytes 3145736 | tf_op jit(solution)/shard_map/ppermute | solution.py:14
  121.2 74.3 %collective-permute-start.8 = (bf16[8,64,2048]{2,1,0:T(8,128)(2,1)}, bf16[8,64,2048]{2,1,0:T(8,128)(2,1)}, u32[]{:S(2)}, u32[]{:S(2)}) collective-permute-start(bf16[8,64,2048]{2,1,0:T(8,128)(2,1)} %get-tuple-element.40), channel_id=1, source_target_pairs={{0,4},{4,0},{8,12},{12,8},{1,5},{5,1},{9,13},{13,9},{2,6},{6,2},{1... | collective-permute-start | bytes 6291464 | tf_op jit(solution)/shard_map/ppermute | solution.py:14
  121.2 44.3 %collective-permute-start.3 = (bf16[2048,512]{1,0:T(8,128)(2,1)}, bf16[2048,512]{1,0:T(8,128)(2,1)}, u32[]{:S(2)}, u32[]{:S(2)}) collective-permute-start(bf16[2048,512]{1,0:T(8,128)(2,1)} %constant_dynamic-slice_fusion.4.refs_1_), channel_id=1, source_target_pairs={{1,2},{2,1},{5,6},{6,5},{9,10},{10,9},{13,14},{14,13},{17,18},{18,... | collective-permute-start | bytes 6291464 | tf_op jit(solution)/shard_map/ppermute | solution.py:215
  123.2 70.3 %collective-permute-start.5 = (bf16[2048,512]{1,0:T(8,128)(2,1)}, bf16[2048,512]{1,0:T(8,128)(2,1)}, u32[]{:S(2)}, u32[]{:S(2)}) collective-permute-start(bf16[2048,512]{1,0:T(8,128)(2,1)} %constant_dynamic-slice_fusion.4.refs_1_), channel_id=1, source_target_pairs={{0,1},{1,0},{2,3},{3,2},{4,5},{5,4},{6,7},{7,6},{8,9},{9,8},{10,11... | collective-permute-start | bytes 6291464 | tf_op jit(solution)/shard_map/ppermute | solution.py:14
  152.6 62.0 %collective-permute-start.15 = (bf16[8,64,2048]{2,1,0:T(8,128)(2,1)}, bf16[8,64,2048]{2,1,0:T(8,128)(2,1)}, u32[]{:S(2)}, u32[]{:S(2)}) collective-permute-start(bf16[8,64,2048]{2,1,0:T(8,128)(2,1)} %get-tuple-element.35), channel_id=1, source_target_pairs={{0,8},{4,12},{8,0},{12,4},{1,9},{5,13},{9,1},{13,5},{2,10},{6,14},... | collective-permute-start | bytes 6291464 | tf_op jit(solution)/shard_map/ppermute | solution.py:14
  154.1 105.0 %collective-permute-start.10 = (bf16[8,64,2048]{2,1,0:T(8,128)(2,1)}, bf16[8,64,2048]{2,1,0:T(8,128)(2,1)}, u32[]{:S(2)}, u32[]{:S(2)}) collective-permute-start(bf16[8,64,2048]{2,1,0:T(8,128)(2,1)} %get-tuple-element.36), channel_id=1, source_target_pairs={{0,8},{4,12},{8,0},{12,4},{1,9},{5,13},{9,1},{13,5},{2,10},{6,14},... | collective-permute-start | bytes 6291464 | tf_op jit(solution)/shard_map/ppermute | solution.py:14
  165.5 175.8 %collective-permute-start.4 = (bf16[2048,512]{1,0:T(8,128)(2,1)}, bf16[2048,512]{1,0:T(8,128)(2,1)}, u32[]{:S(2)}, u32[]{:S(2)}) collective-permute-start(bf16[2048,512]{1,0:T(8,128)(2,1)} %collective-permute-done.3), channel_id=1, source_target_pairs={{1,0},{2,3},{5,4},{6,7},{9,8},{10,11},{13,12},{14,15},{17,16},{18,... | collective-permute-start | bytes 6291464 | tf_op jit(solution)/shard_map/ppermute | solution.py:215
  193.5 129.1 %collective-permute-start.6 = (bf16[2048,512]{1,0:T(8,128)(2,1)}, bf16[2048,512]{1,0:T(8,128)(2,1)}, u32[]{:S(2)}, u32[]{:S(2)}) collective-permute-start(bf16[2048,512]{1,0:T(8,128)(2,1)} %collective-permute-done.5.refs_3_), channel_id=1, source_target_pairs={{1,2},{2,1},{5,6},{6,5},{9,10},{10,9},{13,14},{14,13},{17,18},{18,... | collective-permute-start | bytes 6291464 | tf_op jit(solution)/shard_map/ppermute | solution.py:215
  276.6 47.2 %collective-permute-start.24 = (bf16[256,2048]{1,0:T(8,128)(2,1)}, bf16[256,2048]{1,0:T(8,128)(2,1)}, u32[]{:S(2)}, u32[]{:S(2)}) collective-permute-start(bf16[256,2048]{1,0:T(8,128)(2,1)} %shard_map.70), channel_id=1, source_target_pairs={{0,1},{3,2},{4,5},{7,6},{8,9},{11,10},{12,13},{15,14},{16,17},{19,... | collective-permute-start | bytes 3145736 | tf_op jit(solution)/shard_map/ppermute | solution.py:215
  322.5 67.2 %collective-permute-start.7 = (bf16[2048,512]{1,0:T(8,128)(2,1)}, bf16[2048,512]{1,0:T(8,128)(2,1)}, u32[]{:S(2)}, u32[]{:S(2)}) collective-permute-start(bf16[2048,512]{1,0:T(8,128)(2,1)} %collective-permute-done.6), channel_id=1, source_target_pairs={{1,0},{2,3},{5,4},{6,7},{9,8},{10,11},{13,12},{14,15},{17,16},{18,... | collective-permute-start | bytes 6291464 | tf_op jit(solution)/shard_map/ppermute | solution.py:215
  341.3 104.7 %collective-permute-start.18 = (bf16[2,64,1024]{2,1,0:T(8,128)(2,1)}, bf16[2,64,1024]{2,1,0:T(8,128)(2,1)}, u32[]{:S(2)}, u32[]{:S(2)}) collective-permute-start(bf16[2,64,1024]{2,1,0:T(8,128)(2,1)} %get-tuple-element.30), channel_id=1, source_target_pairs={{0,3},{1,2},{2,1},{3,0},{4,7},{5,6},{6,5},{7,4},{8,11},{9,10},{10,... | collective-permute-start | bytes 786440 | tf_op jit(solution)/shard_map/ppermute | solution.py:14
  345.5 101.4 %collective-permute-start.17 = (bf16[2,64,1024]{2,1,0:T(8,128)(2,1)}, bf16[2,64,1024]{2,1,0:T(8,128)(2,1)}, u32[]{:S(2)}, u32[]{:S(2)}) collective-permute-start(bf16[2,64,1024]{2,1,0:T(8,128)(2,1)} %get-tuple-element.31), channel_id=1, source_target_pairs={{0,2},{1,3},{2,0},{3,1},{4,6},{5,7},{6,4},{7,5},{8,10},{9,11},{10,... | collective-permute-start | bytes 786440 | tf_op jit(solution)/shard_map/ppermute | solution.py:14
  367.9 60.7 %collective-permute-start.21 = (bf16[256,2048]{1,0:T(8,128)(2,1)}, bf16[256,2048]{1,0:T(8,128)(2,1)}, u32[]{:S(2)}, u32[]{:S(2)}) collective-permute-start(bf16[256,2048]{1,0:T(8,128)(2,1)} %shard_map.67), channel_id=1, source_target_pairs={{0,1},{1,2},{4,5},{5,6},{8,9},{9,10},{12,13},{13,14},{16,17},{17,1... | collective-permute-start | bytes 3145736 | tf_op jit(solution)/shard_map/ppermute | solution.py:215
  373.3 56.3 %collective-permute-start.20 = (bf16[256,2048]{1,0:T(8,128)(2,1)}, bf16[256,2048]{1,0:T(8,128)(2,1)}, u32[]{:S(2)}, u32[]{:S(2)}) collective-permute-start(bf16[256,2048]{1,0:T(8,128)(2,1)} %shard_map.67), channel_id=1, source_target_pairs={{3,2},{2,1},{7,6},{6,5},{11,10},{10,9},{15,14},{14,13},{19,18},{18... | collective-permute-start | bytes 3145736 | tf_op jit(solution)/shard_map/ppermute | solution.py:215
  389.7 81.0 %collective-permute-start.27 = (bf16[256,2048]{1,0:T(8,128)(2,1)}, bf16[256,2048]{1,0:T(8,128)(2,1)}, u32[]{:S(2)}, u32[]{:S(2)}) collective-permute-start(bf16[256,2048]{1,0:T(8,128)(2,1)} %shard_map.72), channel_id=1, source_target_pairs={{0,1},{1,0},{2,3},{3,2},{4,5},{5,4},{6,7},{7,6},{8,9},{9,8},{10,11... | collective-permute-start | bytes 3145736 | tf_op jit(solution)/shard_map/ppermute | solution.py:14
  424.3 59.6 %all-to-all-start = ((bf16[8,256,512]{2,1,0:T(8,128)(2,1)}), bf16[8,256,512]{2,1,0:T(8,128)(2,1)}, u32[]{:S(2)}, u32[]{:S(2)}) async-start(bf16[8,256,512]{2,1,0:T(8,128)(2,1)} %bitcast.58), calls=%async_computation | async-start | bytes 4194304 | tf_op jit(solution)/shard_map/all_to_all | solution.py:276
  428.7 42.1 %collective-permute-start.28 = (bf16[256,2048]{1,0:T(8,128)(2,1)}, bf16[256,2048]{1,0:T(8,128)(2,1)S(1)}, u32[]{:S(2)}, u32[]{:S(2)}) collective-permute-start(bf16[256,2048]{1,0:T(8,128)(2,1)} %copy-done.10), channel_id=1, source_target_pairs={{1,2},{2,1},{5,6},{6,5},{9,10},{10,9},{13,14},{14,13},{17,18},{18,... | collective-permute-start | bytes 3145736 | tf_op jit(solution)/shard_map/ppermute | solution.py:215
  437.0 40.4 %collective-permute-start.22 = (bf16[256,2048]{1,0:T(8,128)(2,1)S(1)}, bf16[256,2048]{1,0:T(8,128)(2,1)S(1)}, u32[]{:S(2)}, u32[]{:S(2)}) collective-permute-start(bf16[256,2048]{1,0:T(8,128)(2,1)S(1)} %shard_map.68), channel_id=1, source_target_pairs={{0,1},{1,0},{2,3},{3,2},{4,5},{5,4},{6,7},{7,6},{8,9},{9,8},{10,11... | collective-permute-start | bytes 3145736 | tf_op jit(solution)/shard_map/ppermute | solution.py:14
  (23 other events, 746.4 us)
Sparse Core Ops, SparseCore 0:
  9.2 175.8 all-gather.1

commit v3 on v2

--- a/solution.py
+++ b/solution.py
@@ -68,16 +68,16 @@
 
 def chunk_partial(ti, blocks, feat, width, rows, w, term, terms, d, arrived, whole=None, into=None):
     first, stride = blocks
-    count, depth = rows.shape
+    _, count, depth = rows.shape
     per = width // COLS
     step = feat // COLS
     packed = lambda b, k, t: (0, b * per + k)
     spread = lambda b, k, t: (0, (first + b * stride) * step + k)
     operands = [rows, w]
-    specs = [pl.BlockSpec((count, depth), lambda b, k, t: (0, 0)), pl.BlockSpec((depth, COLS), spread)]
+    specs = [pl.BlockSpec((None, count, depth), lambda b, k, t: (t[0] ^ d, 0, 0)), pl.BlockSpec((depth, COLS), spread)]
     if term:
         operands.append(terms)
-        specs.append(pl.BlockSpec((None, count, COLS), lambda b, k, t: (d, 0, k)))
+        specs.append(pl.BlockSpec((None, count, COLS), lambda b, k, t: (t[0] ^ d, 0, k)))
     for piece in arrived:
         operands.append(piece)
         specs.append(pl.BlockSpec((count, COLS), packed))
@@ -115,7 +115,7 @@
     )(ti, *operands)
 
 
-def plane_product(ti, gathered, shards, total, out_dtype):
+def plane_product(ti, gathered, shards):
     m, _ = gathered.shape
     depth, cols = shards[0][1].shape
     tm = 256
@@ -126,18 +126,12 @@
             pl.BlockSpec((tm, depth), lambda i, t, d=d: (i, t[0] ^ d)),
             pl.BlockSpec((depth, cols), lambda i, t: (0, 0)),
         ]
-    if total is not None:
-        operands.append(total)
-        specs.append(pl.BlockSpec((tm, cols), lambda i, t: (i, 0)))
 
     def kernel(t_ref, *refs):
-        acc = None
+        acc = jnp.zeros((tm, cols), F32)
         for at in range(len(shards)):
-            term = jnp.dot(refs[2 * at][...], refs[2 * at + 1][...], preferred_element_type=F32)
-            acc = term if acc is None else acc + term
-        if total is not None:
-            acc = acc + refs[-2][...]
-        refs[-1][...] = acc.astype(out_dtype)
+            acc = acc + jnp.dot(refs[2 * at][...], refs[2 * at + 1][...], preferred_element_type=F32)
+        refs[-1][...] = acc.astype(BF16)
 
     return pl.pallas_call(
         kernel,
@@ -147,26 +141,24 @@
             in_specs=specs,
             out_specs=pl.BlockSpec((tm, cols), lambda i, t: (i, 0)),
         ),
-        out_shape=jax.ShapeDtypeStruct((m, cols), out_dtype),
+        out_shape=jax.ShapeDtypeStruct((m, cols), BF16),
         compiler_params=pltpu.CompilerParams(vmem_limit_bytes=VMEM),
         cost_estimate=pl.CostEstimate(
             flops=2 * m * depth * cols * len(shards),
-            bytes_accessed=(2 * m * depth + 2 * depth * cols) * len(shards) + 8 * m * cols,
+            bytes_accessed=(2 * m * depth + 2 * depth * cols) * len(shards) + 2 * m * cols,
             transcendentals=0,
         ),
     )(ti, *operands)
 
 
-def plane_finish(ti, back, low, up_rel, feat, width, into):
-    parts, count, cols = back.shape
+def plane_finish(ti, back, low, up_plane, feat, width, into, h):
+    parts, tile, cols = back.shape
     per = (feat - width) // cols
-    tiles, tile, rank = low.shape
+    rank = low.shape[-1]
 
     def kernel(t_ref, back_ref, low_ref, up_ref, into_ref, out_ref):
-        for t in range(tiles):
-            delta = jnp.dot(low_ref[t], up_ref[t], preferred_element_type=F32).astype(BF16)
-            at = pl.ds(t * tile, tile)
-            out_ref[at, :] = (back_ref[at, :].astype(F32) + delta.astype(F32)).astype(BF16)
+        delta = jnp.dot(low_ref[...], up_ref[...], preferred_element_type=F32).astype(BF16)
+        out_ref[...] = (back_ref[...].astype(F32) + delta.astype(F32)).astype(BF16)
 
     return pl.pallas_call(
         kernel,
@@ -174,20 +166,166 @@
             num_scalar_prefetch=1,
             grid=(parts // per, per),
             in_specs=[
-                pl.BlockSpec((None, count, cols), lambda j, k, t: (j * per + k, 0, 0)),
-                pl.BlockSpec((tiles, tile, rank), lambda j, k, t: (0, 0, 0)),
-                pl.BlockSpec((None, tiles, rank, cols), lambda j, k, t: (j ^ t[0], 0, 0, k)),
+                pl.BlockSpec((None, tile, cols), lambda j, k, t: (j * per + k, 0, 0)),
+                pl.BlockSpec((None, None, tile, rank), lambda j, k, t: (t[0], h, 0, 0)),
+                pl.BlockSpec((None, None, rank, cols), lambda j, k, t: (j, h, 0, k)),
                 pl.BlockSpec(memory_space=pl.ANY),
             ],
-            out_specs=pl.BlockSpec((count, cols), lambda j, k, t: (0, j * (feat // cols) + width // cols + k)),
+            out_specs=pl.BlockSpec((tile, cols), lambda j, k, t: (h, j * (feat // cols) + width // cols + k)),
         ),
         out_shape=jax.ShapeDtypeStruct(into.shape, BF16),
         input_output_aliases={4: 0},
         compiler_params=pltpu.CompilerParams(vmem_limit_bytes=VMEM),
         cost_estimate=pl.CostEstimate(
-            flops=2 * parts * count * cols * rank, bytes_accessed=5 * parts * count * cols, transcendentals=0
-        ),
-    )(ti, back, low, up_rel, into)
+            flops=2 * parts * tile * cols * rank, bytes_accessed=5 * parts * tile * cols, transcendentals=0
+        ),
+    )(ti, back, low, up_plane, into)
+
+
+def tile_slot(t, i, place):
+    ids, slot_of, meta = t
+    last = ids.shape[0] // TILE - 1
+    return slot_of[ids[jnp.minimum(place * meta[2] + i, last) * TILE]]
+
+
+def held_index(t, slot, count):
+    return jnp.clip(slot - t[2][0] * count, 0, count - 1)
+
+
+def map_call(kernel, scalars, grid, in_specs, out_specs, out_shape, nbytes, flops=0):
+    return pl.pallas_call(
+        kernel,
+        grid_spec=pltpu.PrefetchScalarGridSpec(
+            num_scalar_prefetch=3, grid=grid, in_specs=in_specs, out_specs=out_specs
+        ),
+        out_shape=out_shape,
+        compiler_params=pltpu.CompilerParams(vmem_limit_bytes=VMEM),
+        cost_estimate=pl.CostEstimate(flops=flops, bytes_accessed=nbytes, transcendentals=0),
+    )
+
+
+def maps_for_mate(scalars, bank, tiles, rows=None):
+    count, rank, feat = bank.shape
+    steps = 2 * tiles
+
+    def at(h, i, *t):
+        return (held_index(t, tile_slot(t, i, t[2][0] ^ (1 + 2 * h)), count), 0, 0)
+
+    tile = lambda h, i, *t: (h * tiles + i, 0, 0)
+    in_specs = [pl.BlockSpec((1, rank, feat), at)]
+    out_specs = [pl.BlockSpec((1, rank, feat), tile)]
+    out_shape = [jax.ShapeDtypeStruct((steps, rank, feat), BF16)]
+    operands = [bank]
+    if rows is not None:
+        n = rows.shape[1] // feat
+        some = rows.shape[0] // steps
+        in_specs.append(pl.BlockSpec((some, n * feat), lambda h, i, *t: (h * tiles + i, 0)))
+        out_specs.append(pl.BlockSpec((n, some, feat), lambda h, i, *t: (0, h * tiles + i, 0)))
+        out_shape.append(jax.ShapeDtypeStruct((n, rows.shape[0], feat), BF16))
+        operands.append(rows)
+
+    def kernel(ids, slot_of, meta, bank_ref, *refs):
+        if rows is None:
+            refs[0][...] = bank_ref[...]
+        else:
+            rows_ref, out_ref, blocks_ref = refs
+            out_ref[...] = bank_ref[...]
+            for j in range(n):
+                blocks_ref[j] = rows_ref[:, j * feat : (j + 1) * feat]
+
+    return map_call(
+        kernel, scalars, (2, tiles), in_specs, out_specs, out_shape, 4 * steps * rank * feat
+    )(*scalars, *operands)
+
+
+def maps_for_far(scalars, bank, got, tiles):
+    count, rank, feat = bank.shape
+
+    def at(i, *t):
+        return (held_index(t, tile_slot(t, i, t[2][0] ^ 2), count), 0, 0)
+
+    def kernel(ids, slot_of, meta, bank_ref, got_ref, out_ref):
+        slot = tile_slot((ids, slot_of, meta), pl.program_id(0), meta[0] ^ 2)
+        mine = slot // count == meta[0]
+
+        @pl.when(mine)
+        def _():
+            out_ref[...] = bank_ref[...]
+
+        @pl.when(jnp.logical_not(mine))
+        def _():
+            out_ref[...] = got_ref[...]
+
+    return map_call(
+        kernel, scalars, (tiles,),
+        [pl.BlockSpec((1, rank, feat), at), pl.BlockSpec((1, rank, feat), lambda i, *t: (tiles + i, 0, 0))],
+        pl.BlockSpec((1, rank, feat), lambda i, *t: (i, 0, 0)),
+        jax.ShapeDtypeStruct((tiles, rank, feat), BF16),
+        6 * tiles * rank * feat,
+    )(*scalars, bank, got)
+
+
+def own_specs(bank, tiles):
+    count, rank, feat = bank.shape
+
+    def at(i, *t):
+        return (held_index(t, tile_slot(t, i, t[2][0]), count), 0, 0)
+
+    tile = lambda i, *t: (i, 0, 0)
+    block = (None, rank, feat)
+    return [pl.BlockSpec(block, at), pl.BlockSpec(block, tile), pl.BlockSpec(block, tile)]
+
+
+def with_own(scalar_refs, count, refs, use):
+    meta = scalar_refs[2]
+    place = tile_slot(scalar_refs, pl.program_id(0), meta[0]) // count
+    here, mate = place == meta[0], place == (meta[0] ^ 1)
+    far = jnp.logical_not(jnp.logical_or(here, mate))
+    for flag, ref in zip((here, mate, far), refs):
+        pl.when(flag)(lambda ref=ref: use(ref))
+
+
+def low_parts(scalars, rows, bank, got, far, tiles):
+    count, rank, feat = bank.shape
+
+    def kernel(ids, slot_of, meta, rows_ref, bank_ref, got_ref, far_ref, out_ref):
+        def use(ref):
+            out_ref[...] = lax.dot_general(
+                rows_ref[...], ref[...], (((1,), (1,)), ((), ())), preferred_element_type=F32
+            )
+
+        with_own((ids, slot_of, meta), count, (bank_ref, got_ref, far_ref), use)
+
+    return map_call(
+        kernel, scalars, (tiles,),
+        [pl.BlockSpec((None, TILE, feat), lambda i, *t: (i, 0, 0))] + own_specs(bank, tiles),
+        pl.BlockSpec((None, TILE, rank), lambda i, *t: (i, 0, 0)),
+        jax.ShapeDtypeStruct((tiles, TILE, rank), F32),
+        (6 * rank + 2 * TILE) * tiles * feat, 2 * tiles * TILE * rank * feat,
+    )(*scalars, rows, bank, got, far)
+
+
+def adapter_terms(scalars, low, bank, got, far, tiles, width):
+    count, rank, feat = bank.shape
+
+    def kernel(ids, slot_of, meta, low_ref, bank_ref, got_ref, far_ref, term_ref, up_ref):
+        def use(ref):
+            term_ref[...] = jnp.dot(low_ref[...], ref[:, :width], preferred_element_type=F32).astype(BF16)
+            up_ref[...] = ref[:, width:]
+
+        with_own((ids, slot_of, meta), count, (bank_ref, got_ref, far_ref), use)
+
+    tile = lambda i, *t: (i, 0, 0)
+    return map_call(
+        kernel, scalars, (tiles,),
+        [pl.BlockSpec((None, TILE, rank), tile)] + own_specs(bank, tiles),
+        [pl.BlockSpec((None, TILE, width), tile), pl.BlockSpec((None, rank, feat - width), tile)],
+        [
+            jax.ShapeDtypeStruct((tiles, TILE, width), BF16),
+            jax.ShapeDtypeStruct((tiles, rank, feat - width), BF16),
+        ],
+        (7 * rank + TILE) * tiles * feat, 2 * tiles * TILE * rank * width,
+    )(*scalars, low, bank, got, far)
 
 
 SPLIT = 2
@@ -204,6 +342,7 @@
     rows = x.shape[0]
     feat = w.shape[0]
     own_tiles = rows // TILE
+    tiles = n * own_tiles
     rank = down.shape[1]
     plane_width = feat // SPLIT
     width = feat - plane_width
@@ -214,70 +353,72 @@
     to_ends = [(1, 0), (2, 3)]
     send = lambda v, pairs: lax.ppermute(v, "tensor", pairs)
 
-    slots = slot_of[ids.reshape(-1, TILE)[:, 0]].reshape(stores, n, own_tiles)
-    slots = jnp.take(slots, ti ^ jnp.arange(n), axis=1).reshape(stores, n * own_tiles)
-
-    piece = [lax.dynamic_slice_in_dim(x, (ti ^ d) * feat, feat, 1) for d in range(n)]
-    for d in (3, 2, 1):
-        piece[d] = xor_perm(piece[d], "tensor", d)
-
-    gathered = lax.all_gather(x, PLANE, axis=0, tiled=True)
-    tile_down = fetch_maps(down, slots, si)
-    tile_up = fetch_maps(up, slots, si)
+    meta = jnp.stack([si, ti, jnp.int32(tiles)]).astype(jnp.int32)
+    scalars = (ids, slot_of, meta)
+    after = lambda value, *others: lax.optimization_barrier((value, *others))[0]
+
+    down_send, blocks = maps_for_mate(scalars, down, tiles, x)
+    blocks = lax.all_to_all(blocks, "tensor", split_axis=0, concat_axis=0, tiled=True)
+    down_got = xor_perm(down_send, "store", 1)
+    down_to_far = maps_for_far(scalars, down, down_got, tiles)
+    down_far = xor_perm(down_to_far, "store", 2)
+    (up_send,) = maps_for_mate(scalars, up, tiles)
+    up_got = xor_perm(up_send, "store", 1)
+    up_far = xor_perm(maps_for_far(scalars, up, up_got, tiles), "store", 2)
 
     cols = plane_width * n // members
     per = plane_width // cols
     w_own = lax.dynamic_slice_in_dim(w, (pi // per) * feat + width + (pi % per) * cols, cols, 1)
-    w_own, piece[1], piece[2], piece[3] = lax.optimization_barrier((w_own, piece[1], piece[2], piece[3]))
     w_near = xor_perm(w_own, "tensor", 1)
     w_mid = send(w_own, middle)
-    w_end2 = send(w_mid, to_ends)
-    w_mid2 = send(w_near, middle)
+
+    gathered = []
+    for h in range(own_tiles):
+        half = after(x[h * TILE : (h + 1) * TILE], up_far, down_far, blocks, w_near, w_mid)
+        gathered.append(lax.all_gather(half, PLANE, axis=0, tiled=True))
+
+    low = low_parts(scalars, after(blocks, w_near, w_mid).reshape(tiles, TILE, feat), down, down_got, down_far, tiles)
+    low = low + xor_perm(low.astype(BF16), "tensor", 1).astype(F32)
+    low = (low + xor_perm(low.astype(BF16), "tensor", 2).astype(F32)).astype(BF16)
+    near_on, mid_on = lax.optimization_barrier((w_near, w_mid, low))[:2]
+    w_end2 = send(mid_on, to_ends)
+    w_mid2 = send(near_on, middle)
     w_end3 = send(w_mid2, to_ends)
     w_two = jnp.where(end, w_end2, w_mid2)
     w_three = jnp.where(end, w_end3, w_mid)
-
-    low = jnp.stack([
-        jnp.einsum(
-            "tnd,trd->tnr",
-            piece[d].reshape(own_tiles, TILE, feat),
-            tile_down[d * own_tiles : (d + 1) * own_tiles],
-            preferred_element_type=F32,
-        )
-        for d in range(n)
-    ])
-    pair = low.shape[1:]
-    near = xor_perm(low.astype(BF16), "tensor", 1).reshape(2, 2, *pair)[:, ::-1].reshape(n, *pair)
-    low = low + near.astype(F32)
-    far = xor_perm(low.astype(BF16), "tensor", 2).reshape(2, 2, *pair)[::-1].reshape(n, *pair)
-    low = (low + far.astype(F32)).astype(BF16)
-    tile_up = tile_up.reshape(n, own_tiles, rank, feat)
-    terms = jnp.einsum("dtnr,dtrc->dtnc", low, tile_up[..., :width], preferred_element_type=F32)
-    terms = terms.astype(BF16).reshape(n, rows, width)
-    up_plane = tile_up[..., width:]
-    up_rel = jnp.stack([up_plane[0]] + [xor_perm(up_plane[d], "tensor", d) for d in range(1, n)])
+    terms, up_plane = adapter_terms(scalars, low, up, up_got, up_far, tiles, width)
+    terms = terms.reshape(n, rows, width)
+    up_plane = lax.all_to_all(
+        up_plane.reshape(n, own_tiles, rank, plane_width), "tensor", split_axis=0, concat_axis=0, tiled=True
+    )
 
     def partial(chunk, d, arrived=(), term=True, **kw):
-        return chunk_partial(scalar, chunk, feat, width, piece[d], w, term, terms, d, arrived, **kw)
+        return chunk_partial(scalar, chunk, feat, width, blocks, w, term, terms, d, arrived, **kw)
 
     inner, outer = (1, 1), (0, 3)
     first = [send(partial(inner, 3, term=False), ends_out), send(partial(outer, 3), ends_out)]
-    out = None
-    arrived = []
+    arrived, seconds = [], []
     for chunk, came in zip((inner, outer), first):
         second = partial(chunk, 2, (came,))
         right, left = send(second, inward_right), send(second, inward_left)
         to_near = partial(chunk, 1, (jnp.where(ti == 1, left, right),))
         to_mid = partial(chunk, 3, (jnp.where(ti == 1, right, left),))
+        seconds.append(second)
         arrived.append((xor_perm(to_near, "tensor", 1), send(to_mid, middle)))
 
-    total = plane_product(scalar, gathered, [(0, w_own), (1, w_near)], None, F32)
-    total = plane_product(scalar, gathered, [(2, w_two), (3, w_three)], total, BF16)
-    back = lax.all_to_all(total.reshape(members, rows, cols), PLANE, split_axis=0, concat_axis=0, tiled=True)
-
-    for chunk, came in zip((inner, outer), arrived):
-        out = partial(chunk, 0, came, whole=n * feat, into=out)
-    return plane_finish(scalar, back, low[0], up_rel, feat, width, out)
+    shards = [(0, w_own), (1, w_near), (2, w_two), (3, w_three)]
+    waits = [(seconds[1],), arrived[0]]
+    back = []
+    for h in range(own_tiles):
+        total = plane_product(scalar, after(gathered[h], *waits[min(h, 1)]), shards)
+        back.append(lax.all_to_all(total.reshape(members, TILE, cols), PLANE, split_axis=0, concat_axis=0, tiled=True))
+
+    out = partial(inner, 0, arrived[0], whole=n * feat)
+    low = low.reshape(n, own_tiles, TILE, rank)
+    for h in range(own_tiles - 1):
+        out = plane_finish(scalar, back[h], low, up_plane, feat, width, out, h)
+    out = partial(outer, 0, arrived[1], whole=n * feat, into=out)
+    return plane_finish(scalar, back[-1], low, up_plane, feat, width, out, own_tiles - 1)
 
 
 def body(x, w, down, up, ids, slot_of):

time: 500 us -> 439 us (0.88)
  waiting for transfers between devices: 205 us -> 146 us
  Pallas kernels: 99.4 us -> 155 us
  local copies, waits for them, and re-layouts: 60.1 us -> 13.3 us
  other arithmetic: 32.7 us -> 9.28 us
  starting transfers between devices: 81.5 us -> 99.1 us
    ppermute x17 -> x9, waiting for transfers between devices: 189 us -> 103 us  [xor_perm(): lax.ppermute(x, axis, [(i, i ^ d) for i in range(lax.axis_size(axis))])]
    gather x10 -> x0, local copies, waits for them, and re-layouts: 47 us -> none  [the longest x8 45.7 us: pick(): jnp.take(bank, jnp.clip(slots - first, 0, count - 1), axis=0)]
    pallas_call x0 -> x6, Pallas kernels: none -> 46.1 us  [the longest x2 22 us: maps_for_mate(): map_call(kernel, scalars, (2, tiles), in_specs, out_specs, out_shape, 4 *...]
    ppermute x12, waiting for transfers between devices: 15 us -> 41.9 us  [line_body(): send = lambda v, pairs: lax.ppermute(v, 'tensor', pairs)]
    all_to_all x1 -> x4, starting transfers between devices: 4.34 us -> 28.9 us  [the longest x1 13.4 us: line_body(): lax.all_to_all(up_plane.reshape(n, own_tiles, rank, plane_width), 'tensor...]
    select_n x9 -> x0, other arithmetic: 21 us -> none  [the longest x4 9.38 us: pick(): jnp.take(bank, jnp.clip(slots - first, 0, count - 1), axis=0)]
    ppermute x12, starting transfers between devices: 34.4 us -> 27.7 us  [line_body(): send = lambda v, pairs: lax.ppermute(v, 'tensor', pairs)]
    pallas_call x10, Pallas kernels: 63.1 us -> 69.4 us  [chunk_partial(): pl.pallas_call(kernel, grid_spec=pltpu.PrefetchScalarGridSpec(num_scalar_...]
  transfers between devices with their start and end apart: 31 -> 27, of which waited for: 8 -> 7; matrix products, arithmetic and copies ran while one was open for 19% -> 3% of each run, Pallas kernels for 19% -> 32%
where the time goes in v3:
time: 439 us; the launch traced here: 436 us
  Pallas kernels  155 us (35%)
  waiting for transfers between devices  146 us (33%)
  starting transfers between devices  99.1 us (23%)
  between operations  13.6 us (3%)
  local copies, waits for them, and re-layouts  13.3 us (3%)
  other arithmetic  9.28 us (2%)
    ppermute x9, waiting for transfers between devices, xor_perm(): lax.ppermute(x, axis, [(i, i ^ d) for i in range(lax.axis_size(axis))])  103 us
    pallas_call x10, Pallas kernels, chunk_partial(): pl.pallas_call(kernel, grid_spec=pltpu.PrefetchScalarGridSpec(num_scalar_...  69.4 us
    ppermute x9, starting transfers between devices, xor_perm(): lax.ppermute(x, axis, [(i, i ^ d) for i in range(lax.axis_size(axis))])  42.5 us
    ppermute x12, waiting for transfers between devices, line_body(): send = lambda v, pairs: lax.ppermute(v, 'tensor', pairs)  41.9 us
    pallas_call x2, Pallas kernels, plane_product(): pl.pallas_call(kernel, grid_spec=pltpu.PrefetchScalarGridSpec(num_scalar_...  27.8 us
    ppermute x12, starting transfers between devices, line_body(): send = lambda v, pairs: lax.ppermute(v, 'tensor', pairs)  27.7 us
    pallas_call x2, Pallas kernels, maps_for_mate(): map_call(kernel, scalars, (2, tiles), in_specs, out_specs, out_shape, 4 *...  22 us
    all_to_all x1, starting transfers between devices, line_body(): lax.all_to_all(up_plane.reshape(n, own_tiles, rank, plane_width), 'tensor...  13.4 us
  transfers between devices with their start and end apart: 27, of which 7 were waited for; matrix products, arithmetic and copies ran while one was open for 3% of the time, Pallas kernels for 32%

profile of v3, /device:TPU:0, one launch (start us, length us, event | category | flops | bytes accessed | tf_op | source)
XLA Modules:
  0.0 435.7 jit_solution(7472606013985376487)
XLA Ops:
  8.0 9.8 %shard_map.64 = bf16[16,64,2048]{2,1,0:T(8,128)(2,1)} custom-call(s32[4096]{0:T(1024)S(1)} %copy-done.9, s32[128]{0:T(128)S(1)} %copy-done.11, s32[3]{0:T(128)S(1)} %pad_add_fusion.meta, bf16[32,64,2048]{2,1,0:T(8,128)(2,1)} %bank_ref.11), custom_call_target="tpu_custom_call" | custom-call | bytes 8388608 | tf_op jit(solution)/shard_map/pallas_call | solution.py:236
  18.8 12.2 %shard_map.66 = (bf16[16,64,2048]{2,1,0:T(8,128)(2,1)}, bf16[4,256,2048]{2,1,0:T(8,128)(2,1)}) custom-call(s32[4096]{0:T(1024)S(1)} %copy-done.9, s32[128]{0:T(128)S(1)} %copy-done.11, s32[3]{0:T(128)S(1)} %pad_add_fusion.meta, bf16[32,64,2048]{2,1,0:T(8,128)(2,1)} %bank_ref.10, bf16[256,8192]{1,0:T(8,128)(2,1)} %refs_0_.1), custom_call_target="tpu_custom_call" | custom-call | bytes 8388608 | tf_op jit(solution)/shard_map/pallas_call | solution.py:236
  31.0 5.9 %all-to-all-start = ((bf16[4,256,2048]{2,1,0:T(8,128)(2,1)}), bf16[4,256,2048]{2,1,0:T(8,128)(2,1)}, u32[]{:S(2)}, u32[]{:S(2)}) async-start(bf16[4,256,2048]{2,1,0:T(8,128)(2,1)} %get-tuple-element.17), calls=%async_computation | async-start | bytes 8388608 | tf_op jit(solution)/shard_map/all_to_all | solution.py:361
  58.6 93.6 %collective-permute-done.4.refs_3_ = bf16[2048,512]{1,0:T(8,128)(2,1)} collective-permute-done((bf16[2048,512]{1,0:T(8,128)(2,1)S(1)}, bf16[2048,512]{1,0:T(8,128)(2,1)}, u32[]{:S(2)}, u32[]{:S(2)}) %collective-permute-start.4) | collective-permute-done | bytes 2097184 | tf_op jit(solution)/shard_map/ppermute | solution.py:14
  154.3 7.3 %shard_map.68 = f32[8,128,64]{2,1,0:T(8,128)S(1)} custom-call(s32[4096]{0:T(1024)S(1)} %copy-done.10, s32[128]{0:T(128)S(1)} %copy-done.12, s32[3]{0:T(128)S(1)} %pad_add_fusion.meta, bf16[8,128,2048]{2,1,0:T(8,128)(2,1)} %bitcast.2.rows_ref, bf16[32,64,2048]{2,1,0:T(8,128)(2,1)} %bank_ref.10, bf16[16,64,2048]{2,1,0:T(8,128)(2,1)} %collective-permute-done.2.got_ref, ...), custom_call_target="tpu_custom_call" | custom-call | flops 268435456 | bytes 10485760 | tf_op jit(solution)/shard_map/pallas_call | solution.py:299
  161.6 24.3 %collective-permute-start.6 = (bf16[8,128,64]{2,1,0:T(8,128)(2,1)S(1)}, bf16[8,128,64]{2,1,0:T(8,128)(2,1)S(1)}, u32[]{:S(2)}, u32[]{:S(2)}) collective-permute-start(bf16[8,128,64]{2,1,0:T(8,128)(2,1)S(1)} %convert_element_type.15), channel_id=1, source_target_pairs={{0,1},{1,0},{2,3},{3,2},{4,5},{5,4},{6,7},{7,6},{8,9},{9,8},{10,11... | collective-permute-start | bytes 393224 | tf_op jit(solution)/shard_map/ppermute | solution.py:14
  193.3 6.0 %shard_map.70 = bf16[256,2048]{1,0:T(8,128)(2,1)S(1)} custom-call(s32[1]{0:T(128)} %bitcast.t_ref, bf16[4,256,2048]{2,1,0:T(8,128)(2,1)} %all-to-all-done.rows_ref, bf16[2048,8192]{1,0:T(8,128)(2,1)} %w_ref.19), custom_call_target="tpu_custom_call" | custom-call | flops 2147483648 | bytes 10485760 | tf_op jit(solution)/shard_map/pallas_call | solution.py:101
  207.3 6.1 %shard_map.69 = (bf16[8,128,1024]{2,1,0:T(8,128)(2,1)S(1)}, bf16[8,64,1024]{2,1,0:T(8,128)(2,1)S(1)}) custom-call(s32[4096]{0:T(1024)S(1)} %copy-done.10, s32[128]{0:T(128)S(1)} %copy-done.12, s32[3]{0:T(128)S(1)} %pad_add_fusion.meta, bf16[8,128,64]{2,1,0:T(8,128)(2,1)S(1)} %add_convert_fusion.low_ref, bf16[32,64,2048]{2,1,0:T(8,128)(2,1)} %bank_ref.11, ...), custom_call_target="tpu_custom_call" | custom-call | flops 134217728 | bytes 9437184 | tf_op jit(solution)/shard_map/pallas_call | solution.py:319
  213.4 7.3 %shard_map.75 = bf16[256,2048]{1,0:T(8,128)(2,1)S(1)} custom-call(s32[1]{0:T(128)} %bitcast.t_ref, bf16[4,256,2048]{2,1,0:T(8,128)(2,1)} %all-to-all-done.rows_ref, bf16[2048,8192]{1,0:T(8,128)(2,1)} %w_ref.19, bf16[4,256,1024]{2,1,0:T(8,128)(2,1)S(1)} %bitcast.8), custom_call_target="tpu_custom_call" | custom-call | flops 2147483648 | bytes 10485760 | tf_op jit(solution)/shard_map/pallas_call | solution.py:101
  223.6 6.7 %shard_map.71 = bf16[256,2048]{1,0:T(8,128)(2,1)} custom-call(s32[1]{0:T(128)} %bitcast.t_ref, bf16[4,256,2048]{2,1,0:T(8,128)(2,1)} %all-to-all-done.rows_ref, bf16[2048,8192]{1,0:T(8,128)(2,1)} %w_ref.19, bf16[4,256,1024]{2,1,0:T(8,128)(2,1)S(1)} %bitcast.9, bf16[256,2048]{1,0:T(8,128)(2,1)S(1)} %collective-permute-done.8.refs_1_), custom_call_target="tpu_custom_call" | custom-call | flops 2147483648 | bytes 10485760 | tf_op jit(solution)/shard_map/pallas_call | solution.py:101
  238.7 7.4 %collective-permute-done.16.refs_1_ = bf16[256,2048]{1,0:T(8,128)(2,1)S(1)} collective-permute-done((bf16[256,2048]{1,0:T(8,128)(2,1)S(1)}, bf16[256,2048]{1,0:T(8,128)(2,1)S(1)}, u32[]{:S(2)}, u32[]{:S(2)}) %collective-permute-start.16) | collective-permute-done | bytes 1048608 | tf_op jit(solution)/shard_map/ppermute | solution.py:354
  246.1 6.7 %shard_map.76 = bf16[256,2048]{1,0:T(8,128)(2,1)} custom-call(s32[1]{0:T(128)} %bitcast.t_ref, bf16[4,256,2048]{2,1,0:T(8,128)(2,1)} %all-to-all-done.rows_ref, bf16[2048,8192]{1,0:T(8,128)(2,1)} %w_ref.19, bf16[4,256,1024]{2,1,0:T(8,128)(2,1)S(1)} %bitcast.10, bf16[256,2048]{1,0:T(8,128)(2,1)S(1)} %collective-permute-done.16.refs_1_), custom_call_target="tpu_custom_call" | custom-call | flops 2147483648 | bytes 10485760 | tf_op jit(solution)/shard_map/pallas_call | solution.py:101
  258.3 10.4 %collective-permute-done.10 = bf16[256,2048]{1,0:T(8,128)(2,1)} collective-permute-done((bf16[256,2048]{1,0:T(8,128)(2,1)}, bf16[256,2048]{1,0:T(8,128)(2,1)}, u32[]{:S(2)}, u32[]{:S(2)}) %collective-permute-start.10) | collective-permute-done | bytes 1048608 | tf_op jit(solution)/shard_map/ppermute | solution.py:354
  270.3 13.4 %all-to-all-start.2 = ((bf16[4,2,64,1024]{3,2,1,0:T(8,128)(2,1)}), bf16[4,2,64,1024]{3,2,1,0:T(8,128)(2,1)S(1)}, u32[]{:S(2)}, u32[]{:S(2)}) async-start(bf16[4,2,64,1024]{3,2,1,0:T(8,128)(2,1)} %bitcast.21), calls=%async_computation.2 | async-start | bytes 2097152 | tf_op jit(solution)/shard_map/all_to_all | solution.py:391
  286.7 6.7 %shard_map.72 = bf16[256,2048]{1,0:T(8,128)(2,1)} custom-call(s32[1]{0:T(128)} %bitcast.t_ref, bf16[4,256,2048]{2,1,0:T(8,128)(2,1)} %all-to-all-done.rows_ref, bf16[2048,8192]{1,0:T(8,128)(2,1)} %w_ref.19, bf16[4,256,1024]{2,1,0:T(8,128)(2,1)S(1)} %bitcast.11, bf16[256,2048]{1,0:T(8,128)(2,1)S(1)} %get-tuple-element.32.refs_1_), custom_call_target="tpu_custom_call" | custom-call | flops 2147483648 | bytes 10485760 | tf_op jit(solution)/shard_map/pallas_call | solution.py:101
  296.2 6.7 %shard_map.73 = bf16[256,2048]{1,0:T(8,128)(2,1)} custom-call(s32[1]{0:T(128)} %bitcast.t_ref, bf16[4,256,2048]{2,1,0:T(8,128)(2,1)} %all-to-all-done.rows_ref, bf16[2048,8192]{1,0:T(8,128)(2,1)} %w_ref.19, bf16[4,256,1024]{2,1,0:T(8,128)(2,1)S(1)} %bitcast.12, bf16[256,2048]{1,0:T(8,128)(2,1)S(1)} %get-tuple-element.31.refs_1_), custom_call_target="tpu_custom_call" | custom-call | flops 2147483648 | bytes 10485760 | tf_op jit(solution)/shard_map/pallas_call | solution.py:101
  307.2 8.2 %shard_map.77 = bf16[256,2048]{1,0:T(8,128)(2,1)} custom-call(s32[1]{0:T(128)} %bitcast.t_ref, bf16[4,256,2048]{2,1,0:T(8,128)(2,1)} %all-to-all-done.rows_ref, bf16[2048,8192]{1,0:T(8,128)(2,1)} %w_ref.19, bf16[4,256,1024]{2,1,0:T(8,128)(2,1)S(1)} %bitcast.13, bf16[256,2048]{1,0:T(8,128)(2,1)S(1)} %get-tuple-element.30.refs_1_), custom_call_target="tpu_custom_call" | custom-call | flops 2147483648 | bytes 10485760 | tf_op jit(solution)/shard_map/pallas_call | solution.py:101
  315.4 8.2 %collective-permute-start.19 = (bf16[256,2048]{1,0:T(8,128)(2,1)}, bf16[256,2048]{1,0:T(8,128)(2,1)}, u32[]{:S(2)}, u32[]{:S(2)}) collective-permute-start(bf16[256,2048]{1,0:T(8,128)(2,1)} %shard_map.77), channel_id=1, source_target_pairs={{0,1},{1,0},{2,3},{3,2},{4,5},{5,4},{6,7},{7,6},{8,9},{9,8},{10,11... | collective-permute-start | bytes 3145736 | tf_op jit(solution)/shard_map/ppermute | solution.py:14
  326.8 22.5 %collective-permute-done.15 = bf16[2048,512]{1,0:T(8,128)(2,1)S(1)} collective-permute-done((bf16[2048,512]{1,0:T(8,128)(2,1)}, bf16[2048,512]{1,0:T(8,128)(2,1)S(1)}, u32[]{:S(2)}, u32[]{:S(2)}) %collective-permute-start.15) | collective-permute-done | bytes 2097184 | tf_op jit(solution)/shard_map/ppermute | solution.py:354
  352.5 13.9 %shard_map.79 = bf16[1024,512]{1,0:T(8,128)(2,1)S(1)} custom-call(s32[1]{0:T(128)} %bitcast.t_ref, bf16[1024,8192]{1,0:T(8,128)(2,1)} %all-gather.5.cloned.1.call-done.refs_0_.refs_2_.refs_4_.refs_6_, bf16[2048,512]{1,0:T(8,128)(2,1)S(1)} %copy-done.1, bf16[1024,8192]{1,0:T(8,128)(2,1)} %all-gather.5.cloned.1.call-done.refs_0_.refs_2_.refs_4_.refs_6_, ...), custom_call_target="tpu_custom_call" | custom-call | flops 8589934592 | bytes 26214400 | tf_op jit(solution)/shard_map/pallas_call | solution.py:136
  373.9 6.7 %shard_map.78 = bf16[256,2048]{1,0:T(8,128)(2,1)} custom-call(s32[1]{0:T(128)} %bitcast.t_ref, bf16[4,256,2048]{2,1,0:T(8,128)(2,1)} %all-to-all-done.rows_ref, bf16[2048,8192]{1,0:T(8,128)(2,1)} %w_ref.19, bf16[4,256,1024]{2,1,0:T(8,128)(2,1)S(1)} %bitcast.14, bf16[256,2048]{1,0:T(8,128)(2,1)S(1)} %copy-done.5), custom_call_target="tpu_custom_call" | custom-call | flops 2147483648 | bytes 10485760 | tf_op jit(solution)/shard_map/pallas_call | solution.py:101
  383.9 13.9 %shard_map.74 = bf16[1024,512]{1,0:T(8,128)(2,1)S(1)} custom-call(s32[1]{0:T(128)} %bitcast.t_ref, bf16[1024,8192]{1,0:T(8,128)(2,1)} %all-gather.3.cloned.1.call-done.refs_0_.refs_2_.refs_4_.refs_6_, bf16[2048,512]{1,0:T(8,128)(2,1)S(1)} %copy-done.2, bf16[1024,8192]{1,0:T(8,128)(2,1)} %all-gather.3.cloned.1.call-done.refs_0_.refs_2_.refs_4_.refs_6_, ...), custom_call_target="tpu_custom_call" | custom-call | flops 8589934592 | bytes 26214400 | tf_op jit(solution)/shard_map/pallas_call | solution.py:136
  403.0 7.1 %shard_map.80.into_ref = bf16[256,8192]{1,0:T(8,128)(2,1)} custom-call(s32[1]{0:T(128)} %bitcast.t_ref, bf16[4,256,2048]{2,1,0:T(8,128)(2,1)} %all-to-all-done.rows_ref, bf16[2048,8192]{1,0:T(8,128)(2,1)} %w_ref.19, bf16[4,256,1024]{2,1,0:T(8,128)(2,1)S(1)} %bitcast.15, bf16[256,2048]{1,0:T(8,128)(2,1)} %collective-permute-done.11.refs_1_, ...), custom_call_target="tpu_custom_call" | custom-call | flops 2147483648 | bytes 10485760 | tf_op jit(solution)/shard_map/pallas_call | solution.py:101
  415.9 7.1 %shard_map.82.into_ref = bf16[256,8192]{1,0:T(8,128)(2,1)} custom-call(s32[1]{0:T(128)} %bitcast.t_ref, bf16[4,256,2048]{2,1,0:T(8,128)(2,1)} %all-to-all-done.rows_ref, bf16[2048,8192]{1,0:T(8,128)(2,1)} %w_ref.19, bf16[4,256,1024]{2,1,0:T(8,128)(2,1)S(1)} %bitcast.16, ...), custom_call_target="tpu_custom_call", output_to_operand_aliasing={{}: (6, {})} | custom-call | flops 2147483648 | bytes 10485760 | tf_op jit(solution)/shard_map/pallas_call | solution.py:101
  (90 shorter events, 103.7 us)
Async XLA Ops:
  17.8 25.0 %collective-permute-start = (bf16[16,64,2048]{2,1,0:T(8,128)(2,1)}, bf16[16,64,2048]{2,1,0:T(8,128)(2,1)}, u32[]{:S(2)}, u32[]{:S(2)}) collective-permute-start(bf16[16,64,2048]{2,1,0:T(8,128)(2,1)} %shard_map.64), channel_id=1, source_target_pairs={{0,4},{4,0},{8,12},{12,8},{1,5},{5,1},{9,13},{13,9},{2,6},{6,2},{1... | collective-permute-start | bytes 12582920 | tf_op jit(solution)/shard_map/ppermute | solution.py:14
  31.0 122.6 %all-to-all-start = ((bf16[4,256,2048]{2,1,0:T(8,128)(2,1)}), bf16[4,256,2048]{2,1,0:T(8,128)(2,1)}, u32[]{:S(2)}, u32[]{:S(2)}) async-start(bf16[4,256,2048]{2,1,0:T(8,128)(2,1)} %get-tuple-element.17), calls=%async_computation | async-start | bytes 8388608 | tf_op jit(solution)/shard_map/all_to_all | solution.py:361
  36.9 314.0 %all-gather.5.cloned.1.call-start = ((), (), s32[]{:S(2)}) async-start(), calls=%async_computation.5 | async-start | bytes 18874368 | tf_op jit(solution)/shard_map/all_gather | solution.py:378
  38.6 113.5 %collective-permute-start.4 = (bf16[2048,512]{1,0:T(8,128)(2,1)S(1)}, bf16[2048,512]{1,0:T(8,128)(2,1)}, u32[]{:S(2)}, u32[]{:S(2)}) collective-permute-start(bf16[2048,512]{1,0:T(8,128)(2,1)S(1)} %constant_dynamic-slice_fusion.refs_1_), channel_id=1, source_target_pairs={{0,1},{1,0},{2,3},{3,2},{4,5},{5,4},{6,7},{7,6},{8,9},{9,8},{10,11... | collective-permute-start | bytes 6291464 | tf_op jit(solution)/shard_map/ppermute | solution.py:14
  40.7 111.5 %collective-permute-start.5 = (bf16[2048,512]{1,0:T(8,128)(2,1)S(1)}, bf16[2048,512]{1,0:T(8,128)(2,1)}, u32[]{:S(2)}, u32[]{:S(2)}) collective-permute-start(bf16[2048,512]{1,0:T(8,128)(2,1)S(1)} %constant_dynamic-slice_fusion.refs_1_), channel_id=1, source_target_pairs={{1,2},{2,1},{5,6},{6,5},{9,10},{10,9},{13,14},{14,13},{17,18},{18,... | collective-permute-start | bytes 6291464 | tf_op jit(solution)/shard_map/ppermute | solution.py:354
  48.0 104.2 %collective-permute-start.1 = (bf16[8,64,2048]{2,1,0:T(8,128)(2,1)S(1)}, bf16[8,64,2048]{2,1,0:T(8,128)(2,1)S(1)}, u32[]{:S(2)}, u32[]{:S(2)}) collective-permute-start(bf16[8,64,2048]{2,1,0:T(8,128)(2,1)S(1)} %shard_map.65), channel_id=1, source_target_pairs={{0,8},{4,12},{8,0},{12,4},{1,9},{5,13},{9,1},{13,5},{2,10},{6,14},... | collective-permute-start | bytes 6291464 | tf_op jit(solution)/shard_map/ppermute | solution.py:14
  55.9 97.7 %collective-permute-start.3 = (bf16[8,64,2048]{2,1,0:T(8,128)(2,1)S(1)}, bf16[8,64,2048]{2,1,0:T(8,128)(2,1)S(1)}, u32[]{:S(2)}, u32[]{:S(2)}) collective-permute-start(bf16[8,64,2048]{2,1,0:T(8,128)(2,1)S(1)} %shard_map.67), channel_id=1, source_target_pairs={{0,8},{4,12},{8,0},{12,4},{1,9},{5,13},{9,1},{13,5},{2,10},{6,14},... | collective-permute-start | bytes 6291464 | tf_op jit(solution)/shard_map/ppermute | solution.py:14
  153.6 228.7 %all-gather.3.cloned.1.call-start = ((), (), s32[]{:S(2)}) async-start(), calls=%async_computation.4 | async-start | bytes 18874368 | tf_op jit(solution)/shard_map/all_gather | solution.py:378
  161.6 30.0 %collective-permute-start.6 = (bf16[8,128,64]{2,1,0:T(8,128)(2,1)S(1)}, bf16[8,128,64]{2,1,0:T(8,128)(2,1)S(1)}, u32[]{:S(2)}, u32[]{:S(2)}) collective-permute-start(bf16[8,128,64]{2,1,0:T(8,128)(2,1)S(1)} %convert_element_type.15), channel_id=1, source_target_pairs={{0,1},{1,0},{2,3},{3,2},{4,5},{5,4},{6,7},{7,6},{8,9},{9,8},{10,11... | collective-permute-start | bytes 393224 | tf_op jit(solution)/shard_map/ppermute | solution.py:14
  199.3 24.4 %collective-permute-start.8 = (bf16[256,2048]{1,0:T(8,128)(2,1)S(1)}, bf16[256,2048]{1,0:T(8,128)(2,1)S(1)}, u32[]{:S(2)}, u32[]{:S(2)}) collective-permute-start(bf16[256,2048]{1,0:T(8,128)(2,1)S(1)} %shard_map.70), channel_id=1, source_target_pairs={{0,1},{3,2},{4,5},{7,6},{8,9},{11,10},{12,13},{15,14},{16,17},{19,... | collective-permute-start | bytes 3145736 | tf_op jit(solution)/shard_map/ppermute | solution.py:354
  205.3 78.4 %collective-permute-start.14 = (bf16[2048,512]{1,0:T(8,128)(2,1)}, bf16[2048,512]{1,0:T(8,128)(2,1)}, u32[]{:S(2)}, u32[]{:S(2)}) collective-permute-start(bf16[2048,512]{1,0:T(8,128)(2,1)} %collective-permute-done.4.refs_3_), channel_id=1, source_target_pairs={{1,2},{2,1},{5,6},{6,5},{9,10},{10,9},{13,14},{14,13},{17,18},{18,... | collective-permute-start | bytes 6291464 | tf_op jit(solution)/shard_map/ppermute | solution.py:354
  220.8 25.3 %collective-permute-start.16 = (bf16[256,2048]{1,0:T(8,128)(2,1)S(1)}, bf16[256,2048]{1,0:T(8,128)(2,1)S(1)}, u32[]{:S(2)}, u32[]{:S(2)}) collective-permute-start(bf16[256,2048]{1,0:T(8,128)(2,1)S(1)} %shard_map.75), channel_id=1, source_target_pairs={{0,1},{3,2},{4,5},{7,6},{8,9},{11,10},{12,13},{15,14},{16,17},{19,... | collective-permute-start | bytes 3145736 | tf_op jit(solution)/shard_map/ppermute | solution.py:354
  230.3 38.3 %collective-permute-start.10 = (bf16[256,2048]{1,0:T(8,128)(2,1)}, bf16[256,2048]{1,0:T(8,128)(2,1)}, u32[]{:S(2)}, u32[]{:S(2)}) collective-permute-start(bf16[256,2048]{1,0:T(8,128)(2,1)} %shard_map.71), channel_id=1, source_target_pairs={{0,1},{1,2},{4,5},{5,6},{8,9},{9,10},{12,13},{13,14},{16,17},{17,1... | collective-permute-start | bytes 3145736 | tf_op jit(solution)/shard_map/ppermute | solution.py:354
  235.8 49.3 %collective-permute-start.9 = (bf16[256,2048]{1,0:T(8,128)(2,1)}, bf16[256,2048]{1,0:T(8,128)(2,1)}, u32[]{:S(2)}, u32[]{:S(2)}) collective-permute-start(bf16[256,2048]{1,0:T(8,128)(2,1)} %shard_map.71), channel_id=1, source_target_pairs={{3,2},{2,1},{7,6},{6,5},{11,10},{10,9},{15,14},{14,13},{19,18},{18... | collective-permute-start | bytes 3145736 | tf_op jit(solution)/shard_map/ppermute | solution.py:354
  237.4 86.3 %collective-permute-start.13 = (bf16[2048,512]{1,0:T(8,128)(2,1)}, bf16[2048,512]{1,0:T(8,128)(2,1)}, u32[]{:S(2)}, u32[]{:S(2)}) collective-permute-start(bf16[2048,512]{1,0:T(8,128)(2,1)} %collective-permute-done.5), channel_id=1, source_target_pairs={{1,0},{2,3},{5,4},{6,7},{9,8},{10,11},{13,12},{14,15},{17,16},{18,... | collective-permute-start | bytes 6291464 | tf_op jit(solution)/shard_map/ppermute | solution.py:354
  252.8 50.1 %collective-permute-start.18 = (bf16[256,2048]{1,0:T(8,128)(2,1)}, bf16[256,2048]{1,0:T(8,128)(2,1)}, u32[]{:S(2)}, u32[]{:S(2)}) collective-permute-start(bf16[256,2048]{1,0:T(8,128)(2,1)} %shard_map.76), channel_id=1, source_target_pairs={{0,1},{1,2},{4,5},{5,6},{8,9},{9,10},{12,13},{13,14},{16,17},{17,1... | collective-permute-start | bytes 3145736 | tf_op jit(solution)/shard_map/ppermute | solution.py:354
  268.7 35.9 %collective-permute-start.17 = (bf16[256,2048]{1,0:T(8,128)(2,1)}, bf16[256,2048]{1,0:T(8,128)(2,1)}, u32[]{:S(2)}, u32[]{:S(2)}) collective-permute-start(bf16[256,2048]{1,0:T(8,128)(2,1)} %shard_map.76), channel_id=1, source_target_pairs={{3,2},{2,1},{7,6},{6,5},{11,10},{10,9},{15,14},{14,13},{19,18},{18... | collective-permute-start | bytes 3145736 | tf_op jit(solution)/shard_map/ppermute | solution.py:354
  270.3 97.0 %all-to-all-start.2 = ((bf16[4,2,64,1024]{3,2,1,0:T(8,128)(2,1)}), bf16[4,2,64,1024]{3,2,1,0:T(8,128)(2,1)S(1)}, u32[]{:S(2)}, u32[]{:S(2)}) async-start(bf16[4,2,64,1024]{3,2,1,0:T(8,128)(2,1)} %bitcast.21), calls=%async_computation.2 | async-start | bytes 2097152 | tf_op jit(solution)/shard_map/all_to_all | solution.py:391
  283.7 65.6 %collective-permute-start.15 = (bf16[2048,512]{1,0:T(8,128)(2,1)}, bf16[2048,512]{1,0:T(8,128)(2,1)S(1)}, u32[]{:S(2)}, u32[]{:S(2)}) collective-permute-start(bf16[2048,512]{1,0:T(8,128)(2,1)} %collective-permute-done.14), channel_id=1, source_target_pairs={{1,0},{2,3},{5,4},{6,7},{9,8},{10,11},{13,12},{14,15},{17,16},{18,... | collective-permute-start | bytes 6291464 | tf_op jit(solution)/shard_map/ppermute | solution.py:354
  293.4 88.8 %collective-permute-start.11 = (bf16[256,2048]{1,0:T(8,128)(2,1)}, bf16[256,2048]{1,0:T(8,128)(2,1)}, u32[]{:S(2)}, u32[]{:S(2)}) collective-permute-start(bf16[256,2048]{1,0:T(8,128)(2,1)} %shard_map.72), channel_id=1, source_target_pairs={{0,1},{1,0},{2,3},{3,2},{4,5},{5,4},{6,7},{7,6},{8,9},{9,8},{10,11... | collective-permute-start | bytes 3145736 | tf_op jit(solution)/shard_map/ppermute | solution.py:14
  302.9 79.4 %collective-permute-start.12 = (bf16[256,2048]{1,0:T(8,128)(2,1)}, bf16[256,2048]{1,0:T(8,128)(2,1)}, u32[]{:S(2)}, u32[]{:S(2)}) collective-permute-start(bf16[256,2048]{1,0:T(8,128)(2,1)} %shard_map.73), channel_id=1, source_target_pairs={{1,2},{2,1},{5,6},{6,5},{9,10},{10,9},{13,14},{14,13},{17,18},{18,... | collective-permute-start | bytes 3145736 | tf_op jit(solution)/shard_map/ppermute | solution.py:354
  315.4 100.5 %collective-permute-start.19 = (bf16[256,2048]{1,0:T(8,128)(2,1)}, bf16[256,2048]{1,0:T(8,128)(2,1)}, u32[]{:S(2)}, u32[]{:S(2)}) collective-permute-start(bf16[256,2048]{1,0:T(8,128)(2,1)} %shard_map.77), channel_id=1, source_target_pairs={{0,1},{1,0},{2,3},{3,2},{4,5},{5,4},{6,7},{7,6},{8,9},{9,8},{10,11... | collective-permute-start | bytes 3145736 | tf_op jit(solution)/shard_map/ppermute | solution.py:14
  367.3 31.4 %all-to-all-start.3 = ((bf16[8,128,512]{2,1,0:T(8,128)(2,1)}), bf16[8,128,512]{2,1,0:T(8,128)(2,1)}, u32[]{:S(2)}, u32[]{:S(2)}) async-start(bf16[8,128,512]{2,1,0:T(8,128)(2,1)} %bitcast.17), calls=%async_computation.3 | async-start | bytes 2097152 | tf_op jit(solution)/shard_map/all_to_all | solution.py:414
  380.6 35.3 %collective-permute-start.20 = (bf16[256,2048]{1,0:T(8,128)(2,1)}, bf16[256,2048]{1,0:T(8,128)(2,1)}, u32[]{:S(2)}, u32[]{:S(2)}) collective-permute-start(bf16[256,2048]{1,0:T(8,128)(2,1)} %shard_map.78), channel_id=1, source_target_pairs={{1,2},{2,1},{5,6},{6,5},{9,10},{10,9},{13,14},{14,13},{17,18},{18,... | collective-permute-start | bytes 3145736 | tf_op jit(solution)/shard_map/ppermute | solution.py:354
  (17 other events, 114.6 us)
Sparse Core Ops, SparseCore 0:
  153.7 112.5 all-gather.4
  268.1 89.8 all-gather.2

commit v4 on v3

--- a/solution.py
+++ b/solution.py
@@ -66,12 +66,13 @@
 VMEM = 48 * 1024 * 1024
 
 
-def chunk_partial(ti, blocks, feat, width, rows, w, term, terms, d, arrived, whole=None, into=None):
+def chunk_partial(ti, blocks, feat, width, rows, w, term, terms, d, arrived, whole=None, into=None, choose=None, half=None, came_half=0):
     first, stride = blocks
     _, count, depth = rows.shape
     per = width // COLS
     step = feat // COLS
-    packed = lambda b, k, t: (0, b * per + k)
+    packed = lambda b, k, t: (0, ((half or 0) * 2 + b) * per + k)
+    came = lambda b, k, t: (0, (came_half * 2 + b) * per + k)
     spread = lambda b, k, t: (0, (first + b * stride) * step + k)
     operands = [rows, w]
     specs = [pl.BlockSpec((None, count, depth), lambda b, k, t: (t[0] ^ d, 0, 0)), pl.BlockSpec((depth, COLS), spread)]
@@ -80,7 +81,7 @@
         specs.append(pl.BlockSpec((None, count, COLS), lambda b, k, t: (t[0] ^ d, 0, k)))
     for piece in arrived:
         operands.append(piece)
-        specs.append(pl.BlockSpec((count, COLS), packed))
+        specs.append(pl.BlockSpec((count, COLS), came))
     aliases = {}
     if into is not None:
         aliases = {1 + len(operands): 0}
@@ -93,11 +94,15 @@
         if term:
             own = first + pl.program_id(0) * stride == t_ref[0]
             total = total + jnp.where(own, refs.pop(0)[...].astype(F32), 0.0)
-        for ref in refs[: len(arrived)]:
-            total = total + ref[...].astype(F32)
+        if choose is None:
+            for ref in refs[: len(arrived)]:
+                total = total + ref[...].astype(F32)
+        else:
+            one, other = refs[0][...].astype(F32), refs[1][...].astype(F32)
+            total = total + jnp.where(t_ref[0] == choose, one, other)
         out_ref[...] = total.astype(BF16)
 
-    out_cols = whole if whole else 2 * width
+    out_cols = whole if whole else (2 if half is None else 4) * width
     return pl.pallas_call(
         kernel,
         grid_spec=pltpu.PrefetchScalarGridSpec(
@@ -206,36 +211,34 @@
 
 def maps_for_mate(scalars, bank, tiles, rows=None):
     count, rank, feat = bank.shape
-    steps = 2 * tiles
-
-    def at(h, i, *t):
-        return (held_index(t, tile_slot(t, i, t[2][0] ^ (1 + 2 * h)), count), 0, 0)
-
-    tile = lambda h, i, *t: (h * tiles + i, 0, 0)
-    in_specs = [pl.BlockSpec((1, rank, feat), at)]
-    out_specs = [pl.BlockSpec((1, rank, feat), tile)]
-    out_shape = [jax.ShapeDtypeStruct((steps, rank, feat), BF16)]
-    operands = [bank]
+
+    def at(h):
+        return lambda i, *t: (held_index(t, tile_slot(t, i, t[2][0] ^ (1 + 2 * h)), count), 0, 0)
+
+    in_specs = [pl.BlockSpec((None, rank, feat), at(h)) for h in range(2)]
+    out_specs = [pl.BlockSpec((2, None, rank, feat), lambda i, *t: (0, i, 0, 0))]
+    out_shape = [jax.ShapeDtypeStruct((2, tiles, rank, feat), BF16)]
+    operands = [bank, bank]
     if rows is not None:
         n = rows.shape[1] // feat
-        some = rows.shape[0] // steps
-        in_specs.append(pl.BlockSpec((some, n * feat), lambda h, i, *t: (h * tiles + i, 0)))
-        out_specs.append(pl.BlockSpec((n, some, feat), lambda h, i, *t: (0, h * tiles + i, 0)))
+        some = rows.shape[0] // tiles
+        in_specs.append(pl.BlockSpec((some, n * feat), lambda i, *t: (i, 0)))
+        out_specs.append(pl.BlockSpec((n, some, feat), lambda i, *t: (0, i, 0)))
         out_shape.append(jax.ShapeDtypeStruct((n, rows.shape[0], feat), BF16))
         operands.append(rows)
 
-    def kernel(ids, slot_of, meta, bank_ref, *refs):
-        if rows is None:
-            refs[0][...] = bank_ref[...]
-        else:
-            rows_ref, out_ref, blocks_ref = refs
-            out_ref[...] = bank_ref[...]
+    def kernel(ids, slot_of, meta, one_ref, other_ref, *refs):
+        out_ref = refs[0] if rows is None else refs[1]
+        out_ref[0] = one_ref[...]
+        out_ref[1] = other_ref[...]
+        if rows is not None:
             for j in range(n):
-                blocks_ref[j] = rows_ref[:, j * feat : (j + 1) * feat]
-
-    return map_call(
-        kernel, scalars, (2, tiles), in_specs, out_specs, out_shape, 4 * steps * rank * feat
+                refs[2][j] = refs[0][:, j * feat : (j + 1) * feat]
+
+    out = map_call(
+        kernel, scalars, (tiles,), in_specs, out_specs, out_shape, 8 * tiles * rank * feat
     )(*scalars, *operands)
+    return [out[0].reshape(2 * tiles, rank, feat)] + list(out[1:])
 
 
 def maps_for_far(scalars, bank, got, tiles):
@@ -362,7 +365,7 @@
     down_got = xor_perm(down_send, "store", 1)
     down_to_far = maps_for_far(scalars, down, down_got, tiles)
     down_far = xor_perm(down_to_far, "store", 2)
-    (up_send,) = maps_for_mate(scalars, up, tiles)
+    (up_send,) = maps_for_mate(after(scalars, down_send), up, tiles)
     up_got = xor_perm(up_send, "store", 1)
     up_far = xor_perm(maps_for_far(scalars, up, up_got, tiles), "store", 2)
 
@@ -374,50 +377,50 @@
 
     gathered = []
     for h in range(own_tiles):
-        half = after(x[h * TILE : (h + 1) * TILE], up_far, down_far, blocks, w_near, w_mid)
+        half = after(x[h * TILE : (h + 1) * TILE], up_far, down_far, blocks)
         gathered.append(lax.all_gather(half, PLANE, axis=0, tiled=True))
 
-    low = low_parts(scalars, after(blocks, w_near, w_mid).reshape(tiles, TILE, feat), down, down_got, down_far, tiles)
+    low = low_parts(scalars, blocks.reshape(tiles, TILE, feat), down, down_got, down_far, tiles)
     low = low + xor_perm(low.astype(BF16), "tensor", 1).astype(F32)
     low = (low + xor_perm(low.astype(BF16), "tensor", 2).astype(F32)).astype(BF16)
-    near_on, mid_on = lax.optimization_barrier((w_near, w_mid, low))[:2]
+    near_on, mid_on = after(w_near, low), w_mid
     w_end2 = send(mid_on, to_ends)
     w_mid2 = send(near_on, middle)
-    w_end3 = send(w_mid2, to_ends)
+    terms, up_plane = adapter_terms(scalars, low, up, up_got, up_far, tiles, width)
+    terms = terms.reshape(n, rows, width)
+    def partial(chunk, d, arrived=(), term=True, **kw):
+        return chunk_partial(scalar, chunk, feat, width, blocks, w, term, terms, d, arrived, **kw)
+
+    inner, outer = (1, 1), (0, 3)
+    first = [send(partial(inner, 3, term=False), ends_out), send(partial(outer, 3), ends_out)]
+    seconds, to_near, to_mid = [], None, None
+    for half, (chunk, came) in enumerate(zip((inner, outer), first)):
+        second = partial(chunk, 2, (came,))
+        seconds.append(second)
+        right, left = send(second, inward_right), send(second, inward_left)
+        to_near = partial(chunk, 1, (left, right), choose=1, half=half, into=to_near)
+        to_mid = partial(chunk, 3, (right, left), choose=1, half=half, into=to_mid)
+    lasts = (to_near, to_mid)
+    arrived = (xor_perm(to_near, "tensor", 1), send(to_mid, middle))
+
+    w_end3 = send(after(w_mid2, *seconds), to_ends)
     w_two = jnp.where(end, w_end2, w_mid2)
     w_three = jnp.where(end, w_end3, w_mid)
-    terms, up_plane = adapter_terms(scalars, low, up, up_got, up_far, tiles, width)
-    terms = terms.reshape(n, rows, width)
     up_plane = lax.all_to_all(
         up_plane.reshape(n, own_tiles, rank, plane_width), "tensor", split_axis=0, concat_axis=0, tiled=True
     )
-
-    def partial(chunk, d, arrived=(), term=True, **kw):
-        return chunk_partial(scalar, chunk, feat, width, blocks, w, term, terms, d, arrived, **kw)
-
-    inner, outer = (1, 1), (0, 3)
-    first = [send(partial(inner, 3, term=False), ends_out), send(partial(outer, 3), ends_out)]
-    arrived, seconds = [], []
-    for chunk, came in zip((inner, outer), first):
-        second = partial(chunk, 2, (came,))
-        right, left = send(second, inward_right), send(second, inward_left)
-        to_near = partial(chunk, 1, (jnp.where(ti == 1, left, right),))
-        to_mid = partial(chunk, 3, (jnp.where(ti == 1, right, left),))
-        seconds.append(second)
-        arrived.append((xor_perm(to_near, "tensor", 1), send(to_mid, middle)))
-
     shards = [(0, w_own), (1, w_near), (2, w_two), (3, w_three)]
-    waits = [(seconds[1],), arrived[0]]
+    waits = [lasts, lasts]
     back = []
     for h in range(own_tiles):
         total = plane_product(scalar, after(gathered[h], *waits[min(h, 1)]), shards)
         back.append(lax.all_to_all(total.reshape(members, TILE, cols), PLANE, split_axis=0, concat_axis=0, tiled=True))
 
-    out = partial(inner, 0, arrived[0], whole=n * feat)
+    out = partial(inner, 0, arrived, whole=n * feat, came_half=0)
     low = low.reshape(n, own_tiles, TILE, rank)
     for h in range(own_tiles - 1):
         out = plane_finish(scalar, back[h], low, up_plane, feat, width, out, h)
-    out = partial(outer, 0, arrived[1], whole=n * feat, into=out)
+    out = partial(outer, 0, arrived, whole=n * feat, into=out, came_half=1)
     return plane_finish(scalar, back[-1], low, up_plane, feat, width, out, own_tiles - 1)
 
 

time: 439 us -> 420 us (0.957)
  starting transfers between devices: 99.1 us -> 83.3 us
  waiting for transfers between devices: 146 us -> 155 us
  Pallas kernels: 155 us -> 148 us
    ppermute x9 -> x8, waiting for transfers between devices: 103 us -> 134 us  [xor_perm(): lax.ppermute(x, axis, [(i, i ^ d) for i in range(lax.axis_size(axis))])]
    ppermute x9 -> x8, starting transfers between devices: 42.5 us -> 17.4 us  [xor_perm(): lax.ppermute(x, axis, [(i, i ^ d) for i in range(lax.axis_size(axis))])]
    ppermute x12 -> x11, waiting for transfers between devices: 41.9 us -> 19.7 us  [line_body(): send = lambda v, pairs: lax.ppermute(v, 'tensor', pairs)]
    ppermute x12 -> x11, starting transfers between devices: 27.7 us -> 47.6 us  [line_body(): send = lambda v, pairs: lax.ppermute(v, 'tensor', pairs)]
    all_to_all x1, starting transfers between devices: 13.4 us -> 3.51 us  [line_body(): lax.all_to_all(up_plane.reshape(n, own_tiles, rank, plane_width), 'tensor...]
    pallas_call x2, Pallas kernels: 22 us -> 16.4 us  [maps_for_mate(): map_call(kernel, scalars, (tiles,), in_specs, out_specs, out_shape, 8 * t...]
    unnamed x28 -> x34, local copies, waits for them, and re-layouts: 9.08 us -> 7.84 us
  transfers between devices with their start and end apart: 27 -> 25, of which waited for: 7 -> 9; matrix products, arithmetic and copies ran while one was open for 3% -> 3% of each run, Pallas kernels for 32% -> 30%
where the time goes in v4:
time: 420 us; the launch traced here: 419 us
  waiting for transfers between devices  155 us (37%)
  Pallas kernels  148 us (35%)
  starting transfers between devices  83.3 us (20%)
  between operations  13.7 us (3%)
  local copies, waits for them, and re-layouts  12 us (3%)
  other arithmetic  6.55 us (2%)
    ppermute x8, waiting for transfers between devices, xor_perm(): lax.ppermute(x, axis, [(i, i ^ d) for i in range(lax.axis_size(axis))])  134 us
    pallas_call x10, Pallas kernels, chunk_partial(): pl.pallas_call(kernel, grid_spec=pltpu.PrefetchScalarGridSpec(num_scalar_...  69.1 us
    ppermute x11, starting transfers between devices, line_body(): send = lambda v, pairs: lax.ppermute(v, 'tensor', pairs)  47.6 us
    pallas_call x2, Pallas kernels, plane_product(): pl.pallas_call(kernel, grid_spec=pltpu.PrefetchScalarGridSpec(num_scalar_...  26.6 us
    ppermute x11, waiting for transfers between devices, line_body(): send = lambda v, pairs: lax.ppermute(v, 'tensor', pairs)  19.7 us
    ppermute x8, starting transfers between devices, xor_perm(): lax.ppermute(x, axis, [(i, i ^ d) for i in range(lax.axis_size(axis))])  17.4 us
    pallas_call x2, Pallas kernels, maps_for_mate(): map_call(kernel, scalars, (tiles,), in_specs, out_specs, out_shape, 8 * t...  16.4 us
    pallas_call x2, Pallas kernels, plane_finish(): pl.pallas_call(kernel, grid_spec=pltpu.PrefetchScalarGridSpec(num_scalar_...  11.6 us
  transfers between devices with their start and end apart: 25, of which 9 were waited for; matrix products, arithmetic and copies ran while one was open for 3% of the time, Pallas kernels for 30%

profile of v4, /device:TPU:0, one launch (start us, length us, event | category | flops | bytes accessed | tf_op | source)
XLA Modules:
  0.0 418.8 jit_solution(11279072007754694083)
XLA Ops:
  8.0 9.1 %shard_map.64 = (bf16[2,8,64,2048]{3,2,1,0:T(8,128)(2,1)}, bf16[4,256,2048]{2,1,0:T(8,128)(2,1)}) custom-call(s32[4096]{0:T(1024)S(1)} %copy-done.12, s32[128]{0:T(128)S(1)} %copy-done.14, s32[3]{0:T(128)S(1)} %pad_add_fusion.meta, bf16[32,64,2048]{2,1,0:T(8,128)(2,1)} %bank_ref.6, bf16[32,64,2048]{2,1,0:T(8,128)(2,1)} %bank_ref.6, bf16[256,8192]{1,0:T(8,128)(2,1)} %refs_0_.1), custom_call_target="tpu_custom_call" | custom-call | bytes 8388608 | tf_op jit(solution)/shard_map/pallas_call | solution.py:238
  17.1 7.3 %shard_map.65 = bf16[2,8,64,2048]{3,2,1,0:T(8,128)(2,1)} custom-call(s32[4096]{0:T(1024)S(1)} %copy-done.12, s32[128]{0:T(128)S(1)} %copy-done.14, s32[3]{0:T(128)S(1)} %pad_add_fusion.meta, bf16[32,64,2048]{2,1,0:T(8,128)(2,1)} %bank_ref.7, bf16[32,64,2048]{2,1,0:T(8,128)(2,1)} %bank_ref.7), custom_call_target="tpu_custom_call" | custom-call | bytes 8388608 | tf_op jit(solution)/shard_map/pallas_call | solution.py:238
  25.4 6.0 %all-to-all-start = ((bf16[4,256,2048]{2,1,0:T(8,128)(2,1)}), bf16[4,256,2048]{2,1,0:T(8,128)(2,1)}, u32[]{:S(2)}, u32[]{:S(2)}) async-start(bf16[4,256,2048]{2,1,0:T(8,128)(2,1)} %get-tuple-element.22), calls=%async_computation | async-start | bytes 8388608 | tf_op jit(solution)/shard_map/all_to_all | solution.py:364
  49.3 37.7 %collective-permute-done.1.far_ref = bf16[8,64,2048]{2,1,0:T(8,128)(2,1)S(1)} collective-permute-done((bf16[8,64,2048]{2,1,0:T(8,128)(2,1)S(1)}, bf16[8,64,2048]{2,1,0:T(8,128)(2,1)S(1)}, u32[]{:S(2)}, u32[]{:S(2)}) %collective-permute-start.1) | collective-permute-done | bytes 2097184 | tf_op jit(solution)/shard_map/ppermute | solution.py:14
  87.0 44.3 %collective-permute-done.3.far_ref = bf16[8,64,2048]{2,1,0:T(8,128)(2,1)S(1)} collective-permute-done((bf16[8,64,2048]{2,1,0:T(8,128)(2,1)S(1)}, bf16[8,64,2048]{2,1,0:T(8,128)(2,1)S(1)}, u32[]{:S(2)}, u32[]{:S(2)}) %collective-permute-start.3) | collective-permute-done | bytes 2097184 | tf_op jit(solution)/shard_map/ppermute | solution.py:14
  137.3 7.6 %shard_map.68 = f32[8,128,64]{2,1,0:T(8,128)S(1)} custom-call(s32[4096]{0:T(1024)S(1)} %copy-done.13, s32[128]{0:T(128)S(1)} %copy-done.15, s32[3]{0:T(128)S(1)} %pad_add_fusion.meta, bf16[8,128,2048]{2,1,0:T(8,128)(2,1)} %bitcast.4.rows_ref, bf16[32,64,2048]{2,1,0:T(8,128)(2,1)} %bank_ref.6, bf16[16,64,2048]{2,1,0:T(8,128)(2,1)} %collective-permute-done.2.got_ref, ...), custom_call_target="tpu_custom_call" | custom-call | flops 268435456 | bytes 10485760 | tf_op jit(solution)/shard_map/pallas_call | solution.py:302
  147.1 41.3 %collective-permute-done.4 = bf16[8,128,64]{2,1,0:T(8,128)(2,1)S(1)} collective-permute-done((bf16[8,128,64]{2,1,0:T(8,128)(2,1)S(1)}, bf16[8,128,64]{2,1,0:T(8,128)(2,1)S(1)}, u32[]{:S(2)}, u32[]{:S(2)}) %collective-permute-start.4) | collective-permute-done | bytes 131104 | tf_op jit(solution)/shard_map/ppermute | solution.py:14
  191.3 5.9 %shard_map.72 = bf16[256,2048]{1,0:T(8,128)(2,1)S(1)} custom-call(s32[1]{0:T(128)} %bitcast.t_ref, bf16[4,256,2048]{2,1,0:T(8,128)(2,1)} %all-to-all-done.rows_ref, bf16[2048,8192]{1,0:T(8,128)(2,1)} %w_ref.19), custom_call_target="tpu_custom_call" | custom-call | flops 2147483648 | bytes 10485760 | tf_op jit(solution)/shard_map/pallas_call | solution.py:106
  208.6 6.0 %shard_map.69 = (bf16[8,128,1024]{2,1,0:T(8,128)(2,1)S(1)}, bf16[8,64,1024]{2,1,0:T(8,128)(2,1)S(1)}) custom-call(s32[4096]{0:T(1024)S(1)} %copy-done.13, s32[128]{0:T(128)S(1)} %copy-done.15, s32[3]{0:T(128)S(1)} %pad_add_fusion.meta, bf16[8,128,64]{2,1,0:T(8,128)(2,1)S(1)} %add_convert_fusion.low_ref, bf16[32,64,2048]{2,1,0:T(8,128)(2,1)} %bank_ref.7, ...), custom_call_target="tpu_custom_call" | custom-call | flops 134217728 | bytes 9437184 | tf_op jit(solution)/shard_map/pallas_call | solution.py:322
  214.6 7.0 %shard_map.70 = bf16[256,2048]{1,0:T(8,128)(2,1)S(1)} custom-call(s32[1]{0:T(128)} %bitcast.t_ref, bf16[4,256,2048]{2,1,0:T(8,128)(2,1)} %all-to-all-done.rows_ref, bf16[2048,8192]{1,0:T(8,128)(2,1)} %w_ref.19, bf16[4,256,1024]{2,1,0:T(8,128)(2,1)S(1)} %bitcast.10), custom_call_target="tpu_custom_call" | custom-call | flops 2147483648 | bytes 10485760 | tf_op jit(solution)/shard_map/pallas_call | solution.py:106
  223.7 6.8 %shard_map.73 = bf16[256,2048]{1,0:T(8,128)(2,1)} custom-call(s32[1]{0:T(128)} %bitcast.t_ref, bf16[4,256,2048]{2,1,0:T(8,128)(2,1)} %all-to-all-done.rows_ref, bf16[2048,8192]{1,0:T(8,128)(2,1)} %w_ref.19, bf16[4,256,1024]{2,1,0:T(8,128)(2,1)S(1)} %bitcast.11, bf16[256,2048]{1,0:T(8,128)(2,1)S(1)} %collective-permute-done.9.refs_1_), custom_call_target="tpu_custom_call" | custom-call | flops 2147483648 | bytes 10485760 | tf_op jit(solution)/shard_map/pallas_call | solution.py:106
  232.5 6.0 %collective-permute-start.11 = (bf16[256,2048]{1,0:T(8,128)(2,1)}, bf16[256,2048]{1,0:T(8,128)(2,1)S(1)}, u32[]{:S(2)}, u32[]{:S(2)}) collective-permute-start(bf16[256,2048]{1,0:T(8,128)(2,1)} %shard_map.73), channel_id=1, source_target_pairs={{0,1},{1,2},{4,5},{5,6},{8,9},{9,10},{12,13},{13,14},{16,17},{17,1... | collective-permute-start | bytes 3145736 | tf_op jit(solution)/shard_map/ppermute | solution.py:357
  238.5 8.7 %collective-permute-done.6.refs_1_ = bf16[256,2048]{1,0:T(8,128)(2,1)S(1)} collective-permute-done((bf16[256,2048]{1,0:T(8,128)(2,1)S(1)}, bf16[256,2048]{1,0:T(8,128)(2,1)S(1)}, u32[]{:S(2)}, u32[]{:S(2)}) %collective-permute-start.6) | collective-permute-done | bytes 1048608 | tf_op jit(solution)/shard_map/ppermute | solution.py:357
  247.2 6.7 %shard_map.71 = bf16[256,2048]{1,0:T(8,128)(2,1)} custom-call(s32[1]{0:T(128)} %bitcast.t_ref, bf16[4,256,2048]{2,1,0:T(8,128)(2,1)} %all-to-all-done.rows_ref, bf16[2048,8192]{1,0:T(8,128)(2,1)} %w_ref.19, bf16[4,256,1024]{2,1,0:T(8,128)(2,1)S(1)} %bitcast.12, bf16[256,2048]{1,0:T(8,128)(2,1)S(1)} %collective-permute-done.6.refs_1_), custom_call_target="tpu_custom_call" | custom-call | flops 2147483648 | bytes 10485760 | tf_op jit(solution)/shard_map/pallas_call | solution.py:106
  256.9 25.1 %collective-permute-start.8 = (bf16[256,2048]{1,0:T(8,128)(2,1)}, bf16[256,2048]{1,0:T(8,128)(2,1)}, u32[]{:S(2)}, u32[]{:S(2)}) collective-permute-start(bf16[256,2048]{1,0:T(8,128)(2,1)} %shard_map.71), channel_id=1, source_target_pairs={{0,1},{1,2},{4,5},{5,6},{8,9},{9,10},{12,13},{13,14},{16,17},{17,1... | collective-permute-start | bytes 3145736 | tf_op jit(solution)/shard_map/ppermute | solution.py:357
  285.5 6.9 %shard_map.74.refs_3_ = bf16[256,4096]{1,0:T(8,128)(2,1)} custom-call(s32[1]{0:T(128)} %bitcast.t_ref, bf16[4,256,2048]{2,1,0:T(8,128)(2,1)} %all-to-all-done.rows_ref, bf16[2048,8192]{1,0:T(8,128)(2,1)} %w_ref.19, bf16[4,256,1024]{2,1,0:T(8,128)(2,1)} %bitcast.13, bf16[256,2048]{1,0:T(8,128)(2,1)S(1)} %collective-permute-done.10.refs_1_.refs_2_, ...), custom_call_target="tpu_custom_call" | custom-call | flops 2147483648 | bytes 10485760 | tf_op jit(solution)/shard_map/pallas_call | solution.py:106
  292.4 6.8 %shard_map.76.refs_3_ = bf16[256,4096]{1,0:T(8,128)(2,1)} custom-call(s32[1]{0:T(128)} %bitcast.t_ref, bf16[4,256,2048]{2,1,0:T(8,128)(2,1)} %all-to-all-done.rows_ref, bf16[2048,8192]{1,0:T(8,128)(2,1)} %w_ref.19, bf16[4,256,1024]{2,1,0:T(8,128)(2,1)} %bitcast.14, bf16[256,2048]{1,0:T(8,128)(2,1)S(1)} %collective-permute-done.11.refs_2_.refs_1_, ...), custom_call_target="tpu_custom_call" | custom-call | flops 2147483648 | bytes 10485760 | tf_op jit(solution)/shard_map/pallas_call | solution.py:106
  304.9 7.4 %shard_map.75 = bf16[256,4096]{1,0:T(8,128)(2,1)} custom-call(s32[1]{0:T(128)} %bitcast.t_ref, bf16[4,256,2048]{2,1,0:T(8,128)(2,1)} %all-to-all-done.rows_ref, bf16[2048,8192]{1,0:T(8,128)(2,1)} %w_ref.19, bf16[4,256,1024]{2,1,0:T(8,128)(2,1)} %bitcast.15, bf16[256,2048]{1,0:T(8,128)(2,1)} %collective-permute-done.7.refs_1_.refs_2_, ...), custom_call_target="tpu_custom_call", output_to_operand_aliasing={{}: (6, {})} | custom-call | flops 2147483648 | bytes 10485760 | tf_op jit(solution)/shard_map/pallas_call | solution.py:106
  312.3 8.0 %collective-permute-start.17 = (bf16[256,4096]{1,0:T(8,128)(2,1)}, bf16[256,4096]{1,0:T(8,128)(2,1)}, u32[]{:S(2)}, u32[]{:S(2)}) collective-permute-start(bf16[256,4096]{1,0:T(8,128)(2,1)} %shard_map.75), channel_id=1, source_target_pairs={{0,1},{1,0},{2,3},{3,2},{4,5},{5,4},{6,7},{7,6},{8,9},{9,8},{10,11... | collective-permute-start | bytes 6291464 | tf_op jit(solution)/shard_map/ppermute | solution.py:14
  320.3 7.3 %shard_map.77 = bf16[256,4096]{1,0:T(8,128)(2,1)} custom-call(s32[1]{0:T(128)} %bitcast.t_ref, bf16[4,256,2048]{2,1,0:T(8,128)(2,1)} %all-to-all-done.rows_ref, bf16[2048,8192]{1,0:T(8,128)(2,1)} %w_ref.19, bf16[4,256,1024]{2,1,0:T(8,128)(2,1)} %bitcast.16, bf16[256,2048]{1,0:T(8,128)(2,1)} %collective-permute-done.8.refs_2_.refs_1_, ...), custom_call_target="tpu_custom_call", output_to_operand_aliasing={{}: (6, {})} | custom-call | flops 2147483648 | bytes 10485760 | tf_op jit(solution)/shard_map/pallas_call | solution.py:106
  342.9 13.3 %shard_map.79 = bf16[1024,512]{1,0:T(8,128)(2,1)S(1)} custom-call(s32[1]{0:T(128)} %bitcast.t_ref, bf16[1024,8192]{1,0:T(8,128)(2,1)} %all-gather.5.cloned.1.call-done.refs_0_.refs_2_.refs_4_.refs_6_, bf16[2048,512]{1,0:T(8,128)(2,1)S(1)} %copy-done.3, bf16[1024,8192]{1,0:T(8,128)(2,1)} %all-gather.5.cloned.1.call-done.refs_0_.refs_2_.refs_4_.refs_6_, ...), custom_call_target="tpu_custom_call" | custom-call | flops 8589934592 | bytes 26214400 | tf_op jit(solution)/shard_map/pallas_call | solution.py:141
  363.2 13.3 %shard_map.78 = bf16[1024,512]{1,0:T(8,128)(2,1)S(1)} custom-call(s32[1]{0:T(128)} %bitcast.t_ref, bf16[1024,8192]{1,0:T(8,128)(2,1)} %all-gather.3.cloned.1.call-done.refs_0_.refs_2_.refs_4_.refs_6_, bf16[2048,512]{1,0:T(8,128)(2,1)S(1)} %copy-done.3, bf16[1024,8192]{1,0:T(8,128)(2,1)} %all-gather.3.cloned.1.call-done.refs_0_.refs_2_.refs_4_.refs_6_, ...), custom_call_target="tpu_custom_call" | custom-call | flops 8589934592 | bytes 26214400 | tf_op jit(solution)/shard_map/pallas_call | solution.py:141
  386.1 7.1 %shard_map.80.into_ref = bf16[256,8192]{1,0:T(8,128)(2,1)} custom-call(s32[1]{0:T(128)} %bitcast.t_ref, bf16[4,256,2048]{2,1,0:T(8,128)(2,1)} %all-to-all-done.rows_ref, bf16[2048,8192]{1,0:T(8,128)(2,1)} %w_ref.19, bf16[4,256,1024]{2,1,0:T(8,128)(2,1)S(1)} %bitcast.17, bf16[256,4096]{1,0:T(8,128)(2,1)} %collective-permute-done.17.refs_1_, ...), custom_call_target="tpu_custom_call" | custom-call | flops 2147483648 | bytes 10485760 | tf_op jit(solution)/shard_map/pallas_call | solution.py:106
  399.1 7.1 %shard_map.82.into_ref = bf16[256,8192]{1,0:T(8,128)(2,1)} custom-call(s32[1]{0:T(128)} %bitcast.t_ref, bf16[4,256,2048]{2,1,0:T(8,128)(2,1)} %all-to-all-done.rows_ref, bf16[2048,8192]{1,0:T(8,128)(2,1)} %w_ref.19, bf16[4,256,1024]{2,1,0:T(8,128)(2,1)S(1)} %bitcast.18, ...), custom_call_target="tpu_custom_call", output_to_operand_aliasing={{}: (6, {})} | custom-call | flops 2147483648 | bytes 10485760 | tf_op jit(solution)/shard_map/pallas_call | solution.py:106
  (90 shorter events, 102.4 us)
Async XLA Ops:
  25.4 15.2 %collective-permute-start.2 = (bf16[16,64,2048]{2,1,0:T(8,128)(2,1)}, bf16[16,64,2048]{2,1,0:T(8,128)(2,1)}, u32[]{:S(2)}, u32[]{:S(2)}) collective-permute-start(bf16[16,64,2048]{2,1,0:T(8,128)(2,1)} %bitcast.2), channel_id=1, source_target_pairs={{0,4},{4,0},{8,12},{12,8},{1,5},{5,1},{9,13},{13,9},{2,6},{6,2},{1... | collective-permute-start | bytes 12582920 | tf_op jit(solution)/shard_map/ppermute | solution.py:14
  25.4 107.2 %all-to-all-start = ((bf16[4,256,2048]{2,1,0:T(8,128)(2,1)}), bf16[4,256,2048]{2,1,0:T(8,128)(2,1)}, u32[]{:S(2)}, u32[]{:S(2)}) async-start(bf16[4,256,2048]{2,1,0:T(8,128)(2,1)} %get-tuple-element.22), calls=%async_computation | async-start | bytes 8388608 | tf_op jit(solution)/shard_map/all_to_all | solution.py:364
  31.4 309.9 %all-gather.5.cloned.1.call-start = ((), (), s32[]{:S(2)}) async-start(), calls=%async_computation.5 | async-start | bytes 18874368 | tf_op jit(solution)/shard_map/all_gather | solution.py:381
  37.8 49.2 %collective-permute-start.1 = (bf16[8,64,2048]{2,1,0:T(8,128)(2,1)S(1)}, bf16[8,64,2048]{2,1,0:T(8,128)(2,1)S(1)}, u32[]{:S(2)}, u32[]{:S(2)}) collective-permute-start(bf16[8,64,2048]{2,1,0:T(8,128)(2,1)S(1)} %shard_map.66), channel_id=1, source_target_pairs={{0,8},{4,12},{8,0},{12,4},{1,9},{5,13},{9,1},{13,5},{2,10},{6,14},... | collective-permute-start | bytes 6291464 | tf_op jit(solution)/shard_map/ppermute | solution.py:14
  46.3 85.0 %collective-permute-start.3 = (bf16[8,64,2048]{2,1,0:T(8,128)(2,1)S(1)}, bf16[8,64,2048]{2,1,0:T(8,128)(2,1)S(1)}, u32[]{:S(2)}, u32[]{:S(2)}) collective-permute-start(bf16[8,64,2048]{2,1,0:T(8,128)(2,1)S(1)} %shard_map.67), channel_id=1, source_target_pairs={{0,8},{4,12},{8,0},{12,4},{1,9},{5,13},{9,1},{13,5},{2,10},{6,14},... | collective-permute-start | bytes 6291464 | tf_op jit(solution)/shard_map/ppermute | solution.py:14
  132.6 229.0 %all-gather.3.cloned.1.call-start = ((), (), s32[]{:S(2)}) async-start(), calls=%async_computation.4 | async-start | bytes 18874368 | tf_op jit(solution)/shard_map/all_gather | solution.py:381
  135.3 71.3 %collective-permute-start.12 = (bf16[2048,512]{1,0:T(8,128)(2,1)S(1)}, bf16[2048,512]{1,0:T(8,128)(2,1)S(1)}, u32[]{:S(2)}, u32[]{:S(2)}) collective-permute-start(bf16[2048,512]{1,0:T(8,128)(2,1)S(1)} %constant_dynamic-slice_fusion.refs_1_), channel_id=1, source_target_pairs={{0,1},{1,0},{2,3},{3,2},{4,5},{5,4},{6,7},{7,6},{8,9},{9,8},{10,11... | collective-permute-start | bytes 6291464 | tf_op jit(solution)/shard_map/ppermute | solution.py:14
  144.9 43.5 %collective-permute-start.4 = (bf16[8,128,64]{2,1,0:T(8,128)(2,1)S(1)}, bf16[8,128,64]{2,1,0:T(8,128)(2,1)S(1)}, u32[]{:S(2)}, u32[]{:S(2)}) collective-permute-start(bf16[8,128,64]{2,1,0:T(8,128)(2,1)S(1)} %convert_element_type.15), channel_id=1, source_target_pairs={{0,1},{1,0},{2,3},{3,2},{4,5},{5,4},{6,7},{7,6},{8,9},{9,8},{10,11... | collective-permute-start | bytes 393224 | tf_op jit(solution)/shard_map/ppermute | solution.py:14
  145.1 86.1 %collective-permute-start.13 = (bf16[2048,512]{1,0:T(8,128)(2,1)S(1)}, bf16[2048,512]{1,0:T(8,128)(2,1)}, u32[]{:S(2)}, u32[]{:S(2)}) collective-permute-start(bf16[2048,512]{1,0:T(8,128)(2,1)S(1)} %constant_dynamic-slice_fusion.refs_1_), channel_id=1, source_target_pairs={{1,2},{2,1},{5,6},{6,5},{9,10},{10,9},{13,14},{14,13},{17,18},{18,... | collective-permute-start | bytes 6291464 | tf_op jit(solution)/shard_map/ppermute | solution.py:357
  188.5 18.0 %collective-permute-start.5 = (bf16[8,128,64]{2,1,0:T(8,128)(2,1)S(1)}, bf16[8,128,64]{2,1,0:T(8,128)(2,1)S(1)}, u32[]{:S(2)}, u32[]{:S(2)}) collective-permute-start(bf16[8,128,64]{2,1,0:T(8,128)(2,1)S(1)} %fusion), channel_id=1, source_target_pairs={{0,2},{1,3},{2,0},{3,1},{4,6},{5,7},{6,4},{7,5},{8,10},{9,11},{10,... | collective-permute-start | bytes 393224 | tf_op jit(solution)/shard_map/ppermute | solution.py:14
  197.1 26.5 %collective-permute-start.9 = (bf16[256,2048]{1,0:T(8,128)(2,1)S(1)}, bf16[256,2048]{1,0:T(8,128)(2,1)S(1)}, u32[]{:S(2)}, u32[]{:S(2)}) collective-permute-start(bf16[256,2048]{1,0:T(8,128)(2,1)S(1)} %shard_map.72), channel_id=1, source_target_pairs={{0,1},{3,2},{4,5},{7,6},{8,9},{11,10},{12,13},{15,14},{16,17},{19,... | collective-permute-start | bytes 3145736 | tf_op jit(solution)/shard_map/ppermute | solution.py:357
  206.6 47.3 %collective-permute-start.15 = (bf16[2048,512]{1,0:T(8,128)(2,1)S(1)}, bf16[2048,512]{1,0:T(8,128)(2,1)}, u32[]{:S(2)}, u32[]{:S(2)}) collective-permute-start(bf16[2048,512]{1,0:T(8,128)(2,1)S(1)} %collective-permute-done.12.refs_3_), channel_id=1, source_target_pairs={{1,2},{2,1},{5,6},{6,5},{9,10},{10,9},{13,14},{14,13},{17,18},{18,... | collective-permute-start | bytes 6291464 | tf_op jit(solution)/shard_map/ppermute | solution.py:357
  221.6 25.6 %collective-permute-start.6 = (bf16[256,2048]{1,0:T(8,128)(2,1)S(1)}, bf16[256,2048]{1,0:T(8,128)(2,1)S(1)}, u32[]{:S(2)}, u32[]{:S(2)}) collective-permute-start(bf16[256,2048]{1,0:T(8,128)(2,1)S(1)} %shard_map.70), channel_id=1, source_target_pairs={{0,1},{3,2},{4,5},{7,6},{8,9},{11,10},{12,13},{15,14},{16,17},{19,... | collective-permute-start | bytes 3145736 | tf_op jit(solution)/shard_map/ppermute | solution.py:357
  230.5 26.4 %collective-permute-start.10 = (bf16[256,2048]{1,0:T(8,128)(2,1)}, bf16[256,2048]{1,0:T(8,128)(2,1)S(1)}, u32[]{:S(2)}, u32[]{:S(2)}) collective-permute-start(bf16[256,2048]{1,0:T(8,128)(2,1)} %shard_map.73), channel_id=1, source_target_pairs={{3,2},{2,1},{7,6},{6,5},{11,10},{10,9},{15,14},{14,13},{19,18},{18... | collective-permute-start | bytes 3145736 | tf_op jit(solution)/shard_map/ppermute | solution.py:357
  231.2 98.4 %collective-permute-start.14 = (bf16[2048,512]{1,0:T(8,128)(2,1)}, bf16[2048,512]{1,0:T(8,128)(2,1)}, u32[]{:S(2)}, u32[]{:S(2)}) collective-permute-start(bf16[2048,512]{1,0:T(8,128)(2,1)} %collective-permute-done.13), channel_id=1, source_target_pairs={{1,0},{2,3},{5,4},{6,7},{9,8},{10,11},{13,12},{14,15},{17,16},{18,... | collective-permute-start | bytes 6291464 | tf_op jit(solution)/shard_map/ppermute | solution.py:357
  232.5 53.0 %collective-permute-start.11 = (bf16[256,2048]{1,0:T(8,128)(2,1)}, bf16[256,2048]{1,0:T(8,128)(2,1)S(1)}, u32[]{:S(2)}, u32[]{:S(2)}) collective-permute-start(bf16[256,2048]{1,0:T(8,128)(2,1)} %shard_map.73), channel_id=1, source_target_pairs={{0,1},{1,2},{4,5},{5,6},{8,9},{9,10},{12,13},{13,14},{16,17},{17,1... | collective-permute-start | bytes 3145736 | tf_op jit(solution)/shard_map/ppermute | solution.py:357
  253.9 84.2 %collective-permute-start.16 = (bf16[2048,512]{1,0:T(8,128)(2,1)}, bf16[2048,512]{1,0:T(8,128)(2,1)}, u32[]{:S(2)}, u32[]{:S(2)}) collective-permute-start(bf16[2048,512]{1,0:T(8,128)(2,1)} %collective-permute-done.15), channel_id=1, source_target_pairs={{1,0},{2,3},{5,4},{6,7},{9,8},{10,11},{13,12},{14,15},{17,16},{18,... | collective-permute-start | bytes 6291464 | tf_op jit(solution)/shard_map/ppermute | solution.py:357
  255.2 44.0 %collective-permute-start.7 = (bf16[256,2048]{1,0:T(8,128)(2,1)}, bf16[256,2048]{1,0:T(8,128)(2,1)}, u32[]{:S(2)}, u32[]{:S(2)}) collective-permute-start(bf16[256,2048]{1,0:T(8,128)(2,1)} %shard_map.71), channel_id=1, source_target_pairs={{3,2},{2,1},{7,6},{6,5},{11,10},{10,9},{15,14},{14,13},{19,18},{18... | collective-permute-start | bytes 3145736 | tf_op jit(solution)/shard_map/ppermute | solution.py:357
  256.9 48.0 %collective-permute-start.8 = (bf16[256,2048]{1,0:T(8,128)(2,1)}, bf16[256,2048]{1,0:T(8,128)(2,1)}, u32[]{:S(2)}, u32[]{:S(2)}) collective-permute-start(bf16[256,2048]{1,0:T(8,128)(2,1)} %shard_map.71), channel_id=1, source_target_pairs={{0,1},{1,2},{4,5},{5,6},{8,9},{9,10},{12,13},{13,14},{16,17},{17,1... | collective-permute-start | bytes 3145736 | tf_op jit(solution)/shard_map/ppermute | solution.py:357
  281.9 75.2 %all-to-all-start.2 = ((bf16[4,2,64,1024]{3,2,1,0:T(8,128)(2,1)}), bf16[4,2,64,1024]{3,2,1,0:T(8,128)(2,1)S(1)}, u32[]{:S(2)}, u32[]{:S(2)}) async-start(bf16[4,2,64,1024]{3,2,1,0:T(8,128)(2,1)} %bitcast.23), calls=%async_computation.2 | async-start | bytes 2097152 | tf_op jit(solution)/shard_map/all_to_all | solution.py:409
  312.3 73.9 %collective-permute-start.17 = (bf16[256,4096]{1,0:T(8,128)(2,1)}, bf16[256,4096]{1,0:T(8,128)(2,1)}, u32[]{:S(2)}, u32[]{:S(2)}) collective-permute-start(bf16[256,4096]{1,0:T(8,128)(2,1)} %shard_map.75), channel_id=1, source_target_pairs={{0,1},{1,0},{2,3},{3,2},{4,5},{5,4},{6,7},{7,6},{8,9},{9,8},{10,11... | collective-permute-start | bytes 6291464 | tf_op jit(solution)/shard_map/ppermute | solution.py:14
  327.6 58.5 %collective-permute-start.18 = (bf16[256,4096]{1,0:T(8,128)(2,1)}, bf16[256,4096]{1,0:T(8,128)(2,1)}, u32[]{:S(2)}, u32[]{:S(2)}) collective-permute-start(bf16[256,4096]{1,0:T(8,128)(2,1)} %shard_map.77), channel_id=1, source_target_pairs={{1,2},{2,1},{5,6},{6,5},{9,10},{10,9},{13,14},{14,13},{17,18},{18,... | collective-permute-start | bytes 6291464 | tf_op jit(solution)/shard_map/ppermute | solution.py:357
  357.2 20.4 %all-to-all-start.3 = ((bf16[8,128,512]{2,1,0:T(8,128)(2,1)}), bf16[8,128,512]{2,1,0:T(8,128)(2,1)}, u32[]{:S(2)}, u32[]{:S(2)}) async-start(bf16[8,128,512]{2,1,0:T(8,128)(2,1)} %bitcast.20), calls=%async_computation.3 | async-start | bytes 2097152 | tf_op jit(solution)/shard_map/all_to_all | solution.py:417
  377.6 28.6 %all-to-all-start.1 = ((bf16[8,128,512]{2,1,0:T(8,128)(2,1)}), bf16[8,128,512]{2,1,0:T(8,128)(2,1)}, u32[]{:S(2)}, u32[]{:S(2)}) async-start(bf16[8,128,512]{2,1,0:T(8,128)(2,1)} %bitcast.19), calls=%async_computation.1 | async-start | bytes 2097152 | tf_op jit(solution)/shard_map/all_to_all | solution.py:417
  (18 other events, 115.0 us)
Sparse Core Ops, SparseCore 0:
  132.7 91.5 all-gather.4
  226.2 89.8 all-gather.2

commit v5 on v4

--- a/solution.py
+++ b/solution.py
@@ -66,13 +66,12 @@
 VMEM = 48 * 1024 * 1024
 
 
-def chunk_partial(ti, blocks, feat, width, rows, w, term, terms, d, arrived, whole=None, into=None, choose=None, half=None, came_half=0):
+def chunk_partial(ti, blocks, feat, width, rows, w, term, terms, d, arrived, whole=None, into=None, choose=None, half=None, dtype=BF16):
     first, stride = blocks
     _, count, depth = rows.shape
     per = width // COLS
     step = feat // COLS
     packed = lambda b, k, t: (0, ((half or 0) * 2 + b) * per + k)
-    came = lambda b, k, t: (0, (came_half * 2 + b) * per + k)
     spread = lambda b, k, t: (0, (first + b * stride) * step + k)
     operands = [rows, w]
     specs = [pl.BlockSpec((None, count, depth), lambda b, k, t: (t[0] ^ d, 0, 0)), pl.BlockSpec((depth, COLS), spread)]
@@ -81,7 +80,7 @@
         specs.append(pl.BlockSpec((None, count, COLS), lambda b, k, t: (t[0] ^ d, 0, k)))
     for piece in arrived:
         operands.append(piece)
-        specs.append(pl.BlockSpec((count, COLS), came))
+        specs.append(pl.BlockSpec((count, COLS), lambda b, k, t: (0, b * per + k)))
     aliases = {}
     if into is not None:
         aliases = {1 + len(operands): 0}
@@ -100,7 +99,7 @@
         else:
             one, other = refs[0][...].astype(F32), refs[1][...].astype(F32)
             total = total + jnp.where(t_ref[0] == choose, one, other)
-        out_ref[...] = total.astype(BF16)
+        out_ref[...] = total.astype(dtype)
 
     out_cols = whole if whole else (2 if half is None else 4) * width
     return pl.pallas_call(
@@ -111,7 +110,7 @@
             in_specs=specs,
             out_specs=pl.BlockSpec((count, COLS), spread if whole else packed),
         ),
-        out_shape=jax.ShapeDtypeStruct((count, out_cols), BF16),
+        out_shape=jax.ShapeDtypeStruct((count, out_cols), dtype),
         input_output_aliases=aliases,
         compiler_params=pltpu.CompilerParams(vmem_limit_bytes=VMEM),
         cost_estimate=pl.CostEstimate(
@@ -122,38 +121,74 @@
 
 def plane_product(ti, gathered, shards):
     m, _ = gathered.shape
-    depth, cols = shards[0][1].shape
-    tm = 256
-    operands, specs = [], []
-    for d, shard in shards:
-        operands += [gathered, shard]
-        specs += [
-            pl.BlockSpec((tm, depth), lambda i, t, d=d: (i, t[0] ^ d)),
-            pl.BlockSpec((depth, cols), lambda i, t: (0, 0)),
-        ]
+    n = len(shards)
+    depth, cols = shards[0][0].shape
+    tm = min(512, m)
 
     def kernel(t_ref, *refs):
+        rows_refs, shard_refs = refs[:n], refs[n : 3 * n]
+        out_ref, held, sem = refs[3 * n :]
+        first = pl.program_id(0) == 0
+        end = jnp.logical_or(t_ref[0] == 0, t_ref[0] == n - 1)
+
+        @pl.when(jnp.logical_and(first, end))
+        def _():
+            for d in range(n):
+                pltpu.make_async_copy(shard_refs[2 * d], held.at[d], sem.at[d]).start()
+
+        @pl.when(jnp.logical_and(first, jnp.logical_not(end)))
+        def _():
+            for d in range(n):
+                pltpu.make_async_copy(shard_refs[2 * d + 1], held.at[d], sem.at[d]).start()
+
         acc = jnp.zeros((tm, cols), F32)
-        for at in range(len(shards)):
-            acc = acc + jnp.dot(refs[2 * at][...], refs[2 * at + 1][...], preferred_element_type=F32)
-        refs[-1][...] = acc.astype(BF16)
+        for d in range(n):
+
+            @pl.when(first)
+            def _():
+                pltpu.make_async_copy(shard_refs[2 * d], held.at[d], sem.at[d]).wait()
+
+            acc = acc + jnp.dot(rows_refs[d][...], held[d], preferred_element_type=F32)
+        out_ref[...] = acc.astype(BF16)
 
     return pl.pallas_call(
         kernel,
         grid_spec=pltpu.PrefetchScalarGridSpec(
             num_scalar_prefetch=1,
             grid=(m // tm,),
-            in_specs=specs,
+            in_specs=[pl.BlockSpec((tm, depth), lambda i, t, d=d: (i, t[0] ^ d)) for d in range(n)]
+            + [pl.BlockSpec(memory_space=pl.ANY)] * (2 * n),
             out_specs=pl.BlockSpec((tm, cols), lambda i, t: (i, 0)),
+            scratch_shapes=[pltpu.VMEM((n, depth, cols), BF16), pltpu.SemaphoreType.DMA((n,))],
         ),
         out_shape=jax.ShapeDtypeStruct((m, cols), BF16),
         compiler_params=pltpu.CompilerParams(vmem_limit_bytes=VMEM),
         cost_estimate=pl.CostEstimate(
-            flops=2 * m * depth * cols * len(shards),
-            bytes_accessed=(2 * m * depth + 2 * depth * cols) * len(shards) + 2 * m * cols,
+            flops=2 * m * depth * cols * n,
+            bytes_accessed=(2 * m * depth + 2 * depth * cols) * n + 2 * m * cols,
             transcendentals=0,
         ),
-    )(ti, *operands)
+    )(ti, *[gathered] * n, *[ref for pair in shards for ref in pair])
+
+
+def add_arrived(own, arrived, width, feat, into):
+    count = own.shape[0]
+    step, per = feat // COLS, width // COLS
+    packed = lambda b, k: (0, b * per + k)
+    spread = lambda b, k: (0, jnp.where(b < 2, b + 1, (b - 2) * 3) * step + k)
+
+    def kernel(own_ref, one_ref, other_ref, into_ref, out_ref):
+        out_ref[...] = (own_ref[...] + one_ref[...].astype(F32) + other_ref[...].astype(F32)).astype(BF16)
+
+    return pl.pallas_call(
+        kernel,
+        grid=(4, per),
+        in_specs=[pl.BlockSpec((count, COLS), packed)] * 3 + [pl.BlockSpec(memory_space=pl.ANY)],
+        out_specs=pl.BlockSpec((count, COLS), spread),
+        out_shape=jax.ShapeDtypeStruct(into.shape, BF16),
+        input_output_aliases={3: 0},
+        cost_estimate=pl.CostEstimate(flops=8 * count * width, bytes_accessed=40 * count * width, transcendentals=0),
+    )(own, *arrived, into)
 
 
 def plane_finish(ti, back, low, up_plane, feat, width, into, h):
@@ -161,7 +196,10 @@
     per = (feat - width) // cols
     rank = low.shape[-1]
 
-    def kernel(t_ref, back_ref, low_ref, up_ref, into_ref, out_ref):
+    given = [] if into is None else [into]
+
+    def kernel(t_ref, back_ref, low_ref, up_ref, *refs):
+        out_ref = refs[-1]
         delta = jnp.dot(low_ref[...], up_ref[...], preferred_element_type=F32).astype(BF16)
         out_ref[...] = (back_ref[...].astype(F32) + delta.astype(F32)).astype(BF16)
 
@@ -174,17 +212,17 @@
                 pl.BlockSpec((None, tile, cols), lambda j, k, t: (j * per + k, 0, 0)),
                 pl.BlockSpec((None, None, tile, rank), lambda j, k, t: (t[0], h, 0, 0)),
                 pl.BlockSpec((None, None, rank, cols), lambda j, k, t: (j, h, 0, k)),
-                pl.BlockSpec(memory_space=pl.ANY),
-            ],
+            ]
+            + [pl.BlockSpec(memory_space=pl.ANY)] * len(given),
             out_specs=pl.BlockSpec((tile, cols), lambda j, k, t: (h, j * (feat // cols) + width // cols + k)),
         ),
-        out_shape=jax.ShapeDtypeStruct(into.shape, BF16),
-        input_output_aliases={4: 0},
+        out_shape=jax.ShapeDtypeStruct((low.shape[1] * tile, low.shape[0] * feat), BF16),
+        input_output_aliases={4: 0} if given else {},
         compiler_params=pltpu.CompilerParams(vmem_limit_bytes=VMEM),
         cost_estimate=pl.CostEstimate(
             flops=2 * parts * tile * cols * rank, bytes_accessed=5 * parts * tile * cols, transcendentals=0
         ),
-    )(ti, back, low, up_plane, into)
+    )(ti, back, low, up_plane, *given)
 
 
 def tile_slot(t, i, place):
@@ -349,7 +387,6 @@
     rank = down.shape[1]
     plane_width = feat // SPLIT
     width = feat - plane_width
-    end = (ti == 0) | (ti == n - 1)
     ends_out = [(0, 1), (3, 2)]
     inward_right, inward_left = [(0, 1), (1, 2)], [(3, 2), (2, 1)]
     middle = [(1, 2), (2, 1)]
@@ -383,19 +420,21 @@
     low = low_parts(scalars, blocks.reshape(tiles, TILE, feat), down, down_got, down_far, tiles)
     low = low + xor_perm(low.astype(BF16), "tensor", 1).astype(F32)
     low = (low + xor_perm(low.astype(BF16), "tensor", 2).astype(F32)).astype(BF16)
-    near_on, mid_on = after(w_near, low), w_mid
-    w_end2 = send(mid_on, to_ends)
-    w_mid2 = send(near_on, middle)
     terms, up_plane = adapter_terms(scalars, low, up, up_got, up_far, tiles, width)
     terms = terms.reshape(n, rows, width)
-    def partial(chunk, d, arrived=(), term=True, **kw):
-        return chunk_partial(scalar, chunk, feat, width, blocks, w, term, terms, d, arrived, **kw)
+    def partial(chunk, d, arrived=(), term=True, rows_in=blocks, **kw):
+        return chunk_partial(scalar, chunk, feat, width, rows_in, w, term, terms, d, arrived, **kw)
 
     inner, outer = (1, 1), (0, 3)
-    first = [send(partial(inner, 3, term=False), ends_out), send(partial(outer, 3), ends_out)]
-    seconds, to_near, to_mid = [], None, None
+    early = partial(inner, 3, term=False)
+    w_end2 = send(w_mid, to_ends)
+    w_mid2 = send(after(w_near, low, early), middle)
+    late = partial(outer, 3)
+    first = [send(early, ends_out), send(late, ends_out)]
+    seconds, own, to_near, to_mid = [], None, None, None
     for half, (chunk, came) in enumerate(zip((inner, outer), first)):
-        second = partial(chunk, 2, (came,))
+        own = partial(chunk, 0, rows_in=after(blocks, *(seconds or [late])), half=half, into=own, dtype=F32)
+        second = partial(chunk, 2, (came,), rows_in=after(blocks, own))
         seconds.append(second)
         right, left = send(second, inward_right), send(second, inward_left)
         to_near = partial(chunk, 1, (left, right), choose=1, half=half, into=to_near)
@@ -404,29 +443,28 @@
     arrived = (xor_perm(to_near, "tensor", 1), send(to_mid, middle))
 
     w_end3 = send(after(w_mid2, *seconds), to_ends)
-    w_two = jnp.where(end, w_end2, w_mid2)
-    w_three = jnp.where(end, w_end3, w_mid)
     up_plane = lax.all_to_all(
         up_plane.reshape(n, own_tiles, rank, plane_width), "tensor", split_axis=0, concat_axis=0, tiled=True
     )
-    shards = [(0, w_own), (1, w_near), (2, w_two), (3, w_three)]
+    shards = [(w_own, w_own), (w_near, w_near), (w_end2, w_mid2), (w_end3, w_mid)]
     waits = [lasts, lasts]
     back = []
     for h in range(own_tiles):
         total = plane_product(scalar, after(gathered[h], *waits[min(h, 1)]), shards)
         back.append(lax.all_to_all(total.reshape(members, TILE, cols), PLANE, split_axis=0, concat_axis=0, tiled=True))
 
-    out = partial(inner, 0, arrived, whole=n * feat, came_half=0)
     low = low.reshape(n, own_tiles, TILE, rank)
-    for h in range(own_tiles - 1):
+    out = None
+    for h in range(own_tiles):
+        if h == own_tiles - 1:
+            out = add_arrived(own, arrived, width, feat, out)
         out = plane_finish(scalar, back[h], low, up_plane, feat, width, out, h)
-    out = partial(outer, 0, arrived, whole=n * feat, into=out, came_half=1)
-    return plane_finish(scalar, back[-1], low, up_plane, feat, width, out, own_tiles - 1)
+    return out
 
 
 def body(x, w, down, up, ids, slot_of):
     line = lax.axis_size("tensor") == 4 and lax.axis_size("store") == 4 and lax.axis_size("groups") == 2
-    line = line and x.shape[0] % TILE == 0 and w.shape[0] % (2 * COLS) == 0
+    line = line and x.shape[0] % TILE == 0 and x.shape[0] > TILE and w.shape[0] % (2 * COLS) == 0
     return (line_body if line else general_body)(x, w, down, up, ids, slot_of)
 
 

time: 420 us -> 417 us (level)
  Pallas kernels: 148 us -> 155 us
  other arithmetic: 6.55 us -> 0.29 us
  starting transfers between devices: 83.3 us -> 78.7 us
    ppermute x11, starting transfers between devices: 47.6 us -> 33.6 us  [line_body(): send = lambda v, pairs: lax.ppermute(v, 'tensor', pairs)]
    ppermute x8, starting transfers between devices: 17.4 us -> 26.5 us  [xor_perm(): lax.ppermute(x, axis, [(i, i ^ d) for i in range(lax.axis_size(axis))])]
    pallas_call x0 -> x1, Pallas kernels: none -> 7.06 us  [add_arrived(): pl.pallas_call(kernel, grid=(4, per), in_specs=[pl.BlockSpec((count, COLS...]
    select_n x2 -> x0, other arithmetic: 6.29 us -> none  [the longest x1 3.16 us: line_body(): w_two = jnp.where(end, w_end2, w_mid2)]
    unnamed x34 -> x40, local copies, waits for them, and re-layouts: 7.84 us -> 11 us
  transfers between devices with their start and end apart: 25 -> 25, of which waited for: 9 -> 8; matrix products, arithmetic and copies ran while one was open for 3% -> 1% of each run, Pallas kernels for 30% -> 34%
where the time goes in v5:
time: 417 us; the launch traced here: 415 us
  Pallas kernels  155 us (37%)
  waiting for transfers between devices  152 us (36%)
  starting transfers between devices  78.7 us (19%)
  local copies, waits for them, and re-layouts  15.4 us (4%)
  between operations  13.8 us (3%)
    ppermute x8, waiting for transfers between devices, xor_perm(): lax.ppermute(x, axis, [(i, i ^ d) for i in range(lax.axis_size(axis))])  132 us
    pallas_call x10, Pallas kernels, chunk_partial(): pl.pallas_call(kernel, grid_spec=pltpu.PrefetchScalarGridSpec(num_scalar_...  69.7 us
    ppermute x11, starting transfers between devices, line_body(): send = lambda v, pairs: lax.ppermute(v, 'tensor', pairs)  33.6 us
    pallas_call x2, Pallas kernels, plane_product(): pl.pallas_call(kernel, grid_spec=pltpu.PrefetchScalarGridSpec(num_scalar_...  28.2 us
    ppermute x8, starting transfers between devices, xor_perm(): lax.ppermute(x, axis, [(i, i ^ d) for i in range(lax.axis_size(axis))])  26.5 us
    ppermute x11, waiting for transfers between devices, line_body(): send = lambda v, pairs: lax.ppermute(v, 'tensor', pairs)  16.6 us
    pallas_call x2, Pallas kernels, maps_for_mate(): map_call(kernel, scalars, (tiles,), in_specs, out_specs, out_shape, 8 * t...  15.7 us
    pallas_call x2, Pallas kernels, maps_for_far(): map_call(kernel, scalars, (tiles,), [pl.BlockSpec((1, rank, feat), at), p...  11 us
  transfers between devices with their start and end apart: 25, of which 8 were waited for; matrix products, arithmetic and copies ran while one was open for 1% of the time, Pallas kernels for 34%

profile of v5, /device:TPU:0, one launch (start us, length us, event | category | flops | bytes accessed | tf_op | source)
XLA Modules:
  0.0 414.8 jit_solution(13564079149684727810)
XLA Ops:
  8.0 8.8 %shard_map.64 = (bf16[2,8,64,2048]{3,2,1,0:T(8,128)(2,1)}, bf16[4,256,2048]{2,1,0:T(8,128)(2,1)}) custom-call(s32[4096]{0:T(1024)S(1)} %copy-done.15, s32[128]{0:T(128)S(1)} %copy-done.17, s32[3]{0:T(128)S(1)} %pad_add_fusion.meta, bf16[32,64,2048]{2,1,0:T(8,128)(2,1)} %bank_ref.6, bf16[32,64,2048]{2,1,0:T(8,128)(2,1)} %bank_ref.6, bf16[256,8192]{1,0:T(8,128)(2,1)} %refs_0_.1), custom_call_target="tpu_custom_call" | custom-call | bytes 8388608 | tf_op jit(solution)/shard_map/pallas_call | solution.py:276
  17.9 6.9 %shard_map.65 = bf16[2,8,64,2048]{3,2,1,0:T(8,128)(2,1)} custom-call(s32[4096]{0:T(1024)S(1)} %copy-done.15, s32[128]{0:T(128)S(1)} %copy-done.17, s32[3]{0:T(128)S(1)} %pad_add_fusion.meta, bf16[32,64,2048]{2,1,0:T(8,128)(2,1)} %bank_ref.7, bf16[32,64,2048]{2,1,0:T(8,128)(2,1)} %bank_ref.7), custom_call_target="tpu_custom_call" | custom-call | bytes 8388608 | tf_op jit(solution)/shard_map/pallas_call | solution.py:276
  46.8 38.1 %collective-permute-done.3.far_ref = bf16[8,64,2048]{2,1,0:T(8,128)(2,1)S(1)} collective-permute-done((bf16[8,64,2048]{2,1,0:T(8,128)(2,1)S(1)}, bf16[8,64,2048]{2,1,0:T(8,128)(2,1)S(1)}, u32[]{:S(2)}, u32[]{:S(2)}) %collective-permute-start.3) | collective-permute-done | bytes 2097184 | tf_op jit(solution)/shard_map/ppermute | solution.py:14
  86.3 43.2 %collective-permute-done.1.far_ref = bf16[8,64,2048]{2,1,0:T(8,128)(2,1)S(1)} collective-permute-done((bf16[8,64,2048]{2,1,0:T(8,128)(2,1)S(1)}, bf16[8,64,2048]{2,1,0:T(8,128)(2,1)S(1)}, u32[]{:S(2)}, u32[]{:S(2)}) %collective-permute-start.1) | collective-permute-done | bytes 2097184 | tf_op jit(solution)/shard_map/ppermute | solution.py:14
  133.9 7.9 %shard_map.68 = f32[8,128,64]{2,1,0:T(8,128)S(1)} custom-call(s32[4096]{0:T(1024)S(1)} %copy-done.16, s32[128]{0:T(128)S(1)} %copy-done.18, s32[3]{0:T(128)S(1)} %pad_add_fusion.meta, bf16[8,128,2048]{2,1,0:T(8,128)(2,1)} %bitcast.4.rows_ref, bf16[32,64,2048]{2,1,0:T(8,128)(2,1)} %bank_ref.6, bf16[16,64,2048]{2,1,0:T(8,128)(2,1)} %collective-permute-done.2.got_ref, ...), custom_call_target="tpu_custom_call" | custom-call | flops 268435456 | bytes 10485760 | tf_op jit(solution)/shard_map/pallas_call | solution.py:340
  144.2 41.0 %collective-permute-done.4 = bf16[8,128,64]{2,1,0:T(8,128)(2,1)S(1)} collective-permute-done((bf16[8,128,64]{2,1,0:T(8,128)(2,1)S(1)}, bf16[8,128,64]{2,1,0:T(8,128)(2,1)S(1)}, u32[]{:S(2)}, u32[]{:S(2)}) %collective-permute-start.4) | collective-permute-done | bytes 131104 | tf_op jit(solution)/shard_map/ppermute | solution.py:14
  193.4 9.3 %collective-permute-done.5 = bf16[8,128,64]{2,1,0:T(8,128)(2,1)S(1)} collective-permute-done((bf16[8,128,64]{2,1,0:T(8,128)(2,1)S(1)}, bf16[8,128,64]{2,1,0:T(8,128)(2,1)S(1)}, u32[]{:S(2)}, u32[]{:S(2)}) %collective-permute-start.5) | collective-permute-done | bytes 131104 | tf_op jit(solution)/shard_map/ppermute | solution.py:14
  206.9 6.2 %shard_map.69 = (bf16[8,128,1024]{2,1,0:T(8,128)(2,1)S(1)}, bf16[8,64,1024]{2,1,0:T(8,128)(2,1)S(1)}) custom-call(s32[4096]{0:T(1024)S(1)} %copy-done.16, s32[128]{0:T(128)S(1)} %copy-done.18, s32[3]{0:T(128)S(1)} %pad_add_fusion.meta, bf16[8,128,64]{2,1,0:T(8,128)(2,1)S(1)} %add_convert_fusion.low_ref, bf16[32,64,2048]{2,1,0:T(8,128)(2,1)} %bank_ref.7, ...), custom_call_target="tpu_custom_call" | custom-call | flops 134217728 | bytes 9437184 | tf_op jit(solution)/shard_map/pallas_call | solution.py:360
  214.1 6.9 %shard_map.70 = bf16[256,2048]{1,0:T(8,128)(2,1)S(1)} custom-call(s32[1]{0:T(128)} %bitcast.t_ref, bf16[4,256,2048]{2,1,0:T(8,128)(2,1)} %all-to-all-done.rows_ref, bf16[2048,8192]{1,0:T(8,128)(2,1)} %w_ref.19, bf16[4,256,1024]{2,1,0:T(8,128)(2,1)S(1)} %bitcast.10), custom_call_target="tpu_custom_call" | custom-call | flops 2147483648 | bytes 10485760 | tf_op jit(solution)/shard_map/pallas_call | solution.py:105
  223.7 7.1 %shard_map.71.refs_1_ = f32[256,4096]{1,0:T(8,128)} custom-call(s32[1]{0:T(128)} %bitcast.t_ref, bf16[4,256,2048]{2,1,0:T(8,128)(2,1)} %all-to-all-done.rows_ref, bf16[2048,8192]{1,0:T(8,128)(2,1)} %w_ref.19, bf16[4,256,1024]{2,1,0:T(8,128)(2,1)S(1)} %bitcast.11), custom_call_target="tpu_custom_call" | custom-call | flops 2147483648 | bytes 10485760 | tf_op jit(solution)/shard_map/pallas_call | solution.py:105
  230.7 7.3 %shard_map.73 = bf16[256,2048]{1,0:T(8,128)(2,1)} custom-call(s32[1]{0:T(128)} %bitcast.t_ref, bf16[4,256,2048]{2,1,0:T(8,128)(2,1)} %all-to-all-done.rows_ref, bf16[2048,8192]{1,0:T(8,128)(2,1)} %w_ref.19, bf16[4,256,1024]{2,1,0:T(8,128)(2,1)S(1)} %bitcast.12, bf16[256,2048]{1,0:T(8,128)(2,1)S(1)} %collective-permute-done.6.refs_1_), custom_call_target="tpu_custom_call" | custom-call | flops 2147483648 | bytes 10485760 | tf_op jit(solution)/shard_map/pallas_call | solution.py:105
  238.8 6.9 %shard_map.74.own_ref = f32[256,4096]{1,0:T(8,128)} custom-call(s32[1]{0:T(128)} %bitcast.t_ref, bf16[4,256,2048]{2,1,0:T(8,128)(2,1)} %all-to-all-done.rows_ref, bf16[2048,8192]{1,0:T(8,128)(2,1)} %w_ref.19, bf16[4,256,1024]{2,1,0:T(8,128)(2,1)S(1)} %bitcast.13, f32[256,4096]{1,0:T(8,128)} %shard_map.71.refs_1_), custom_call_target="tpu_custom_call", output_to_operand_aliasing={{}: (4, {})} | custom-call | flops 2147483648 | bytes 10485760 | tf_op jit(solution)/shard_map/pallas_call | solution.py:105
  249.7 6.7 %shard_map.75 = bf16[256,2048]{1,0:T(8,128)(2,1)} custom-call(s32[1]{0:T(128)} %bitcast.t_ref, bf16[4,256,2048]{2,1,0:T(8,128)(2,1)} %all-to-all-done.rows_ref, bf16[2048,8192]{1,0:T(8,128)(2,1)} %w_ref.19, bf16[4,256,1024]{2,1,0:T(8,128)(2,1)S(1)} %bitcast.14, bf16[256,2048]{1,0:T(8,128)(2,1)S(1)} %collective-permute-done.7.refs_1_), custom_call_target="tpu_custom_call" | custom-call | flops 2147483648 | bytes 10485760 | tf_op jit(solution)/shard_map/pallas_call | solution.py:105
  257.7 6.9 %collective-permute-start.11 = (bf16[256,2048]{1,0:T(8,128)(2,1)}, bf16[256,2048]{1,0:T(8,128)(2,1)}, u32[]{:S(2)}, u32[]{:S(2)}) collective-permute-start(bf16[256,2048]{1,0:T(8,128)(2,1)} %shard_map.73), channel_id=1, source_target_pairs={{0,1},{1,2},{4,5},{5,6},{8,9},{9,10},{12,13},{13,14},{16,17},{17,1... | collective-permute-start | bytes 3145736 | tf_op jit(solution)/shard_map/ppermute | solution.py:394
  265.3 13.2 %collective-permute-start.9 = (bf16[256,2048]{1,0:T(8,128)(2,1)}, bf16[256,2048]{1,0:T(8,128)(2,1)}, u32[]{:S(2)}, u32[]{:S(2)}) collective-permute-start(bf16[256,2048]{1,0:T(8,128)(2,1)} %shard_map.75), channel_id=1, source_target_pairs={{0,1},{1,2},{4,5},{5,6},{8,9},{9,10},{12,13},{13,14},{16,17},{17,1... | collective-permute-start | bytes 3145736 | tf_op jit(solution)/shard_map/ppermute | solution.py:394
  287.5 7.3 %shard_map.78.refs_3_ = bf16[256,4096]{1,0:T(8,128)(2,1)} custom-call(s32[1]{0:T(128)} %bitcast.t_ref, bf16[4,256,2048]{2,1,0:T(8,128)(2,1)} %all-to-all-done.rows_ref, bf16[2048,8192]{1,0:T(8,128)(2,1)} %w_ref.19, bf16[4,256,1024]{2,1,0:T(8,128)(2,1)} %bitcast.15, bf16[256,2048]{1,0:T(8,128)(2,1)} %collective-permute-done.11.refs_2_.refs_1_, ...), custom_call_target="tpu_custom_call" | custom-call | flops 2147483648 | bytes 10485760 | tf_op jit(solution)/shard_map/pallas_call | solution.py:105
  294.8 7.3 %shard_map.76.refs_3_ = bf16[256,4096]{1,0:T(8,128)(2,1)} custom-call(s32[1]{0:T(128)} %bitcast.t_ref, bf16[4,256,2048]{2,1,0:T(8,128)(2,1)} %all-to-all-done.rows_ref, bf16[2048,8192]{1,0:T(8,128)(2,1)} %w_ref.19, bf16[4,256,1024]{2,1,0:T(8,128)(2,1)} %bitcast.16, bf16[256,2048]{1,0:T(8,128)(2,1)S(1)} %collective-permute-done.10.refs_1_.refs_2_, ...), custom_call_target="tpu_custom_call" | custom-call | flops 2147483648 | bytes 10485760 | tf_op jit(solution)/shard_map/pallas_call | solution.py:105
  302.1 7.8 %collective-permute-done.9.refs_2_.refs_1_ = bf16[256,2048]{1,0:T(8,128)(2,1)} collective-permute-done((bf16[256,2048]{1,0:T(8,128)(2,1)}, bf16[256,2048]{1,0:T(8,128)(2,1)}, u32[]{:S(2)}, u32[]{:S(2)}) %collective-permute-start.9) | collective-permute-done | bytes 1048608 | tf_op jit(solution)/shard_map/ppermute | solution.py:394
  309.9 7.3 %shard_map.79 = bf16[256,4096]{1,0:T(8,128)(2,1)} custom-call(s32[1]{0:T(128)} %bitcast.t_ref, bf16[4,256,2048]{2,1,0:T(8,128)(2,1)} %all-to-all-done.rows_ref, bf16[2048,8192]{1,0:T(8,128)(2,1)} %w_ref.19, bf16[4,256,1024]{2,1,0:T(8,128)(2,1)} %bitcast.17, bf16[256,2048]{1,0:T(8,128)(2,1)} %collective-permute-done.9.refs_2_.refs_1_, ...), custom_call_target="tpu_custom_call", output_to_operand_aliasing={{}: (6, {})} | custom-call | flops 2147483648 | bytes 10485760 | tf_op jit(solution)/shard_map/pallas_call | solution.py:105
  321.6 7.1 %shard_map.77 = bf16[256,4096]{1,0:T(8,128)(2,1)} custom-call(s32[1]{0:T(128)} %bitcast.t_ref, bf16[4,256,2048]{2,1,0:T(8,128)(2,1)} %all-to-all-done.rows_ref, bf16[2048,8192]{1,0:T(8,128)(2,1)} %w_ref.19, bf16[4,256,1024]{2,1,0:T(8,128)(2,1)} %bitcast.18, bf16[256,2048]{1,0:T(8,128)(2,1)S(1)} %copy-done.11, ...), custom_call_target="tpu_custom_call", output_to_operand_aliasing={{}: (6, {})} | custom-call | flops 2147483648 | bytes 10485760 | tf_op jit(solution)/shard_map/pallas_call | solution.py:105
  328.7 18.5 %collective-permute-start.17 = (bf16[256,4096]{1,0:T(8,128)(2,1)}, bf16[256,4096]{1,0:T(8,128)(2,1)}, u32[]{:S(2)}, u32[]{:S(2)}) collective-permute-start(bf16[256,4096]{1,0:T(8,128)(2,1)} %shard_map.77), channel_id=1, source_target_pairs={{0,1},{1,0},{2,3},{3,2},{4,5},{5,4},{6,7},{7,6},{8,9},{9,8},{10,11... | collective-permute-start | bytes 6291464 | tf_op jit(solution)/shard_map/ppermute | solution.py:14
  348.8 14.1 %shard_map.81 = bf16[1024,512]{1,0:T(8,128)(2,1)S(1)} custom-call(s32[1]{0:T(128)} %bitcast.t_ref, bf16[1024,8192]{1,0:T(8,128)(2,1)} %all-gather.5.cloned.1.call-done.refs_0_.refs_1_.refs_2_.refs_3_, bf16[1024,8192]{1,0:T(8,128)(2,1)} %all-gather.5.cloned.1.call-done.refs_0_.refs_1_.refs_2_.refs_3_, ...), custom_call_target="tpu_custom_call" | custom-call | flops 8589934592 | bytes 26214400 | tf_op jit(solution)/shard_map/pallas_call | solution.py:154
  369.7 14.1 %shard_map.80 = bf16[1024,512]{1,0:T(8,128)(2,1)S(1)} custom-call(s32[1]{0:T(128)} %bitcast.t_ref, bf16[1024,8192]{1,0:T(8,128)(2,1)} %all-gather.3.cloned.1.call-done.refs_0_.refs_1_.refs_2_.refs_3_, bf16[1024,8192]{1,0:T(8,128)(2,1)} %all-gather.3.cloned.1.call-done.refs_0_.refs_1_.refs_2_.refs_3_, ...), custom_call_target="tpu_custom_call" | custom-call | flops 8589934592 | bytes 26214400 | tf_op jit(solution)/shard_map/pallas_call | solution.py:154
  394.8 7.1 %shard_map.83.refs_0_ = bf16[256,8192]{1,0:T(8,128)(2,1)} custom-call(f32[256,4096]{1,0:T(8,128)} %shard_map.74.own_ref, bf16[256,4096]{1,0:T(8,128)(2,1)} %collective-permute-done.17.one_ref, bf16[256,4096]{1,0:T(8,128)(2,1)} %collective-permute-done.18.other_ref, bf16[256,8192]{1,0:T(8,128)(2,1)} %shard_map.82.into_ref), custom_call_target="tpu_custom_call", output_to_operand_aliasing={{}: (3, {})} | custom-call | flops 2097152 | bytes 10485760 | tf_op jit(solution)/shard_map/pallas_call | solution.py:183
  (95 shorter events, 94.1 us)
Async XLA Ops:
  16.8 14.3 %collective-permute-start.2 = (bf16[16,64,2048]{2,1,0:T(8,128)(2,1)}, bf16[16,64,2048]{2,1,0:T(8,128)(2,1)}, u32[]{:S(2)}, u32[]{:S(2)}) collective-permute-start(bf16[16,64,2048]{2,1,0:T(8,128)(2,1)} %bitcast.2), channel_id=1, source_target_pairs={{0,4},{4,0},{8,12},{12,8},{1,5},{5,1},{9,13},{13,9},{2,6},{6,2},{1... | collective-permute-start | bytes 12582920 | tf_op jit(solution)/shard_map/ppermute | solution.py:14
  25.3 104.2 %all-to-all-start = ((bf16[4,256,2048]{2,1,0:T(8,128)(2,1)}), bf16[4,256,2048]{2,1,0:T(8,128)(2,1)}, u32[]{:S(2)}, u32[]{:S(2)}) async-start(bf16[4,256,2048]{2,1,0:T(8,128)(2,1)} %get-tuple-element.26), calls=%async_computation | async-start | bytes 8388608 | tf_op jit(solution)/shard_map/all_to_all | solution.py:401
  31.1 316.1 %all-gather.5.cloned.1.call-start = ((), (), s32[]{:S(2)}) async-start(), calls=%async_computation.5 | async-start | bytes 18874368 | tf_op jit(solution)/shard_map/all_gather | solution.py:418
  36.5 48.5 %collective-permute-start.3 = (bf16[8,64,2048]{2,1,0:T(8,128)(2,1)S(1)}, bf16[8,64,2048]{2,1,0:T(8,128)(2,1)S(1)}, u32[]{:S(2)}, u32[]{:S(2)}) collective-permute-start(bf16[8,64,2048]{2,1,0:T(8,128)(2,1)S(1)} %shard_map.67), channel_id=1, source_target_pairs={{0,8},{4,12},{8,0},{12,4},{1,9},{5,13},{9,1},{13,5},{2,10},{6,14},... | collective-permute-start | bytes 6291464 | tf_op jit(solution)/shard_map/ppermute | solution.py:14
  44.0 85.5 %collective-permute-start.1 = (bf16[8,64,2048]{2,1,0:T(8,128)(2,1)S(1)}, bf16[8,64,2048]{2,1,0:T(8,128)(2,1)S(1)}, u32[]{:S(2)}, u32[]{:S(2)}) collective-permute-start(bf16[8,64,2048]{2,1,0:T(8,128)(2,1)S(1)} %shard_map.66), channel_id=1, source_target_pairs={{0,8},{4,12},{8,0},{12,4},{1,9},{5,13},{9,1},{13,5},{2,10},{6,14},... | collective-permute-start | bytes 6291464 | tf_op jit(solution)/shard_map/ppermute | solution.py:14
  129.5 238.6 %all-gather.3.cloned.1.call-start = ((), (), s32[]{:S(2)}) async-start(), calls=%async_computation.4 | async-start | bytes 18874368 | tf_op jit(solution)/shard_map/all_gather | solution.py:418
  132.2 70.6 %collective-permute-start.12 = (bf16[2048,512]{1,0:T(8,128)(2,1)S(1)}, bf16[2048,512]{1,0:T(8,128)(2,1)S(1)}, u32[]{:S(2)}, u32[]{:S(2)}) collective-permute-start(bf16[2048,512]{1,0:T(8,128)(2,1)S(1)} %constant_dynamic-slice_fusion.refs_4_.refs_5_), channel_id=1, source_target_pairs={{0,1},{1,0},{2,3},{3,2},{4,5},{5,4},{6,7},{7,6},{8,9},{9,8},{10,11... | collective-permute-start | bytes 6291464 | tf_op jit(solution)/shard_map/ppermute | solution.py:14
  141.8 43.3 %collective-permute-start.4 = (bf16[8,128,64]{2,1,0:T(8,128)(2,1)S(1)}, bf16[8,128,64]{2,1,0:T(8,128)(2,1)S(1)}, u32[]{:S(2)}, u32[]{:S(2)}) collective-permute-start(bf16[8,128,64]{2,1,0:T(8,128)(2,1)S(1)} %convert_element_type.15), channel_id=1, source_target_pairs={{0,1},{1,0},{2,3},{3,2},{4,5},{5,4},{6,7},{7,6},{8,9},{9,8},{10,11... | collective-permute-start | bytes 393224 | tf_op jit(solution)/shard_map/ppermute | solution.py:14
  142.1 80.2 %collective-permute-start.13 = (bf16[2048,512]{1,0:T(8,128)(2,1)S(1)}, bf16[2048,512]{1,0:T(8,128)(2,1)}, u32[]{:S(2)}, u32[]{:S(2)}) collective-permute-start(bf16[2048,512]{1,0:T(8,128)(2,1)S(1)} %constant_dynamic-slice_fusion.refs_4_.refs_5_), channel_id=1, source_target_pairs={{1,2},{2,1},{5,6},{6,5},{9,10},{10,9},{13,14},{14,13},{17,18},{18,... | collective-permute-start | bytes 6291464 | tf_op jit(solution)/shard_map/ppermute | solution.py:394
  185.2 17.5 %collective-permute-start.5 = (bf16[8,128,64]{2,1,0:T(8,128)(2,1)S(1)}, bf16[8,128,64]{2,1,0:T(8,128)(2,1)S(1)}, u32[]{:S(2)}, u32[]{:S(2)}) collective-permute-start(bf16[8,128,64]{2,1,0:T(8,128)(2,1)S(1)} %fusion), channel_id=1, source_target_pairs={{0,2},{1,3},{2,0},{3,1},{4,6},{5,7},{6,4},{7,5},{8,10},{9,11},{10,... | collective-permute-start | bytes 393224 | tf_op jit(solution)/shard_map/ppermute | solution.py:14
  202.9 53.5 %collective-permute-start.15 = (bf16[2048,512]{1,0:T(8,128)(2,1)S(1)}, bf16[2048,512]{1,0:T(8,128)(2,1)}, u32[]{:S(2)}, u32[]{:S(2)}) collective-permute-start(bf16[2048,512]{1,0:T(8,128)(2,1)S(1)} %collective-permute-done.12.refs_6_.refs_7_), channel_id=1, source_target_pairs={{1,2},{2,1},{5,6},{6,5},{9,10},{10,9},{13,14},{14,13},{17,18},{18,... | collective-permute-start | bytes 6291464 | tf_op jit(solution)/shard_map/ppermute | solution.py:394
  205.0 25.8 %collective-permute-start.6 = (bf16[256,2048]{1,0:T(8,128)(2,1)S(1)}, bf16[256,2048]{1,0:T(8,128)(2,1)S(1)}, u32[]{:S(2)}, u32[]{:S(2)}) collective-permute-start(bf16[256,2048]{1,0:T(8,128)(2,1)S(1)} %shard_map.72), channel_id=1, source_target_pairs={{0,1},{3,2},{4,5},{7,6},{8,9},{11,10},{12,13},{15,14},{16,17},{19,... | collective-permute-start | bytes 3145736 | tf_op jit(solution)/shard_map/ppermute | solution.py:394
  221.0 28.7 %collective-permute-start.7 = (bf16[256,2048]{1,0:T(8,128)(2,1)S(1)}, bf16[256,2048]{1,0:T(8,128)(2,1)S(1)}, u32[]{:S(2)}, u32[]{:S(2)}) collective-permute-start(bf16[256,2048]{1,0:T(8,128)(2,1)S(1)} %shard_map.70), channel_id=1, source_target_pairs={{0,1},{3,2},{4,5},{7,6},{8,9},{11,10},{12,13},{15,14},{16,17},{19,... | collective-permute-start | bytes 3145736 | tf_op jit(solution)/shard_map/ppermute | solution.py:394
  222.4 124.8 %collective-permute-start.14 = (bf16[2048,512]{1,0:T(8,128)(2,1)}, bf16[2048,512]{1,0:T(8,128)(2,1)}, u32[]{:S(2)}, u32[]{:S(2)}) collective-permute-start(bf16[2048,512]{1,0:T(8,128)(2,1)} %collective-permute-done.13.refs_11_), channel_id=1, source_target_pairs={{1,0},{2,3},{5,4},{6,7},{9,8},{10,11},{13,12},{14,15},{17,16},{18,... | collective-permute-start | bytes 6291464 | tf_op jit(solution)/shard_map/ppermute | solution.py:394
  238.0 27.2 %collective-permute-start.10 = (bf16[256,2048]{1,0:T(8,128)(2,1)}, bf16[256,2048]{1,0:T(8,128)(2,1)S(1)}, u32[]{:S(2)}, u32[]{:S(2)}) collective-permute-start(bf16[256,2048]{1,0:T(8,128)(2,1)} %shard_map.73), channel_id=1, source_target_pairs={{3,2},{2,1},{7,6},{6,5},{11,10},{10,9},{15,14},{14,13},{19,18},{18... | collective-permute-start | bytes 3145736 | tf_op jit(solution)/shard_map/ppermute | solution.py:394
  256.4 90.8 %collective-permute-start.16 = (bf16[2048,512]{1,0:T(8,128)(2,1)}, bf16[2048,512]{1,0:T(8,128)(2,1)}, u32[]{:S(2)}, u32[]{:S(2)}) collective-permute-start(bf16[2048,512]{1,0:T(8,128)(2,1)} %collective-permute-done.15.refs_9_), channel_id=1, source_target_pairs={{1,0},{2,3},{5,4},{6,7},{9,8},{10,11},{13,12},{14,15},{17,16},{18,... | collective-permute-start | bytes 6291464 | tf_op jit(solution)/shard_map/ppermute | solution.py:394
  257.7 29.8 %collective-permute-start.11 = (bf16[256,2048]{1,0:T(8,128)(2,1)}, bf16[256,2048]{1,0:T(8,128)(2,1)}, u32[]{:S(2)}, u32[]{:S(2)}) collective-permute-start(bf16[256,2048]{1,0:T(8,128)(2,1)} %shard_map.73), channel_id=1, source_target_pairs={{0,1},{1,2},{4,5},{5,6},{8,9},{9,10},{12,13},{13,14},{16,17},{17,1... | collective-permute-start | bytes 3145736 | tf_op jit(solution)/shard_map/ppermute | solution.py:394
  264.5 37.6 %collective-permute-start.8 = (bf16[256,2048]{1,0:T(8,128)(2,1)}, bf16[256,2048]{1,0:T(8,128)(2,1)S(1)}, u32[]{:S(2)}, u32[]{:S(2)}) collective-permute-start(bf16[256,2048]{1,0:T(8,128)(2,1)} %shard_map.75), channel_id=1, source_target_pairs={{3,2},{2,1},{7,6},{6,5},{11,10},{10,9},{15,14},{14,13},{19,18},{18... | collective-permute-start | bytes 3145736 | tf_op jit(solution)/shard_map/ppermute | solution.py:394
  265.3 44.7 %collective-permute-start.9 = (bf16[256,2048]{1,0:T(8,128)(2,1)}, bf16[256,2048]{1,0:T(8,128)(2,1)}, u32[]{:S(2)}, u32[]{:S(2)}) collective-permute-start(bf16[256,2048]{1,0:T(8,128)(2,1)} %shard_map.75), channel_id=1, source_target_pairs={{0,1},{1,2},{4,5},{5,6},{8,9},{9,10},{12,13},{13,14},{16,17},{17,1... | collective-permute-start | bytes 3145736 | tf_op jit(solution)/shard_map/ppermute | solution.py:394
  278.5 85.4 %all-to-all-start.2 = ((bf16[4,2,64,1024]{3,2,1,0:T(8,128)(2,1)}), bf16[4,2,64,1024]{3,2,1,0:T(8,128)(2,1)S(1)}, u32[]{:S(2)}, u32[]{:S(2)}) async-start(bf16[4,2,64,1024]{3,2,1,0:T(8,128)(2,1)} %bitcast.23), calls=%async_computation.2 | async-start | bytes 2097152 | tf_op jit(solution)/shard_map/all_to_all | solution.py:446
  318.3 76.6 %collective-permute-start.18 = (bf16[256,4096]{1,0:T(8,128)(2,1)}, bf16[256,4096]{1,0:T(8,128)(2,1)}, u32[]{:S(2)}, u32[]{:S(2)}) collective-permute-start(bf16[256,4096]{1,0:T(8,128)(2,1)} %shard_map.79), channel_id=1, source_target_pairs={{1,2},{2,1},{5,6},{6,5},{9,10},{10,9},{13,14},{14,13},{17,18},{18,... | collective-permute-start | bytes 6291464 | tf_op jit(solution)/shard_map/ppermute | solution.py:394
  328.7 66.1 %collective-permute-start.17 = (bf16[256,4096]{1,0:T(8,128)(2,1)}, bf16[256,4096]{1,0:T(8,128)(2,1)}, u32[]{:S(2)}, u32[]{:S(2)}) collective-permute-start(bf16[256,4096]{1,0:T(8,128)(2,1)} %shard_map.77), channel_id=1, source_target_pairs={{0,1},{1,0},{2,3},{3,2},{4,5},{5,4},{6,7},{7,6},{8,9},{9,8},{10,11... | collective-permute-start | bytes 6291464 | tf_op jit(solution)/shard_map/ppermute | solution.py:14
  363.9 20.9 %all-to-all-start.3 = ((bf16[8,128,512]{2,1,0:T(8,128)(2,1)}), bf16[8,128,512]{2,1,0:T(8,128)(2,1)}, u32[]{:S(2)}, u32[]{:S(2)}) async-start(bf16[8,128,512]{2,1,0:T(8,128)(2,1)} %bitcast.20), calls=%async_computation.3 | async-start | bytes 2097152 | tf_op jit(solution)/shard_map/all_to_all | solution.py:454
  384.8 19.6 %all-to-all-start.1 = ((bf16[8,128,512]{2,1,0:T(8,128)(2,1)}), bf16[8,128,512]{2,1,0:T(8,128)(2,1)S(1)}, u32[]{:S(2)}, u32[]{:S(2)}) async-start(bf16[8,128,512]{2,1,0:T(8,128)(2,1)} %bitcast.19), calls=%async_computation.1 | async-start | bytes 2097152 | tf_op jit(solution)/shard_map/all_to_all | solution.py:454
  (21 other events, 145.0 us)
Sparse Core Ops, SparseCore 0:
  129.6 90.7 all-gather.4
  222.3 89.8 all-gather.2

commit v6 on v5

--- a/solution.py
+++ b/solution.py
@@ -62,7 +62,7 @@
 
 
 PLANE = ("groups", "store")
-COLS = 512
+COLS = 1024
 VMEM = 48 * 1024 * 1024
 
 

time: 417 us -> 413 us (level)
  Pallas kernels: 155 us -> 145 us
    pallas_call x10, Pallas kernels: 69.7 us -> 62.1 us  [chunk_partial(): pl.pallas_call(kernel, grid_spec=pltpu.PrefetchScalarGridSpec(num_scalar_...]
  transfers between devices with their start and end apart: 25 -> 25, of which waited for: 8 -> 9; matrix products, arithmetic and copies ran while one was open for 1% -> 1% of each run, Pallas kernels for 34% -> 32%
where the time goes in v6:
time: 413 us; the launch traced here: 412 us
  waiting for transfers between devices  156 us (38%)
  Pallas kernels  145 us (35%)
  starting transfers between devices  81 us (20%)
  local copies, waits for them, and re-layouts  15.4 us (4%)
  between operations  13.7 us (3%)
    ppermute x8, waiting for transfers between devices, xor_perm(): lax.ppermute(x, axis, [(i, i ^ d) for i in range(lax.axis_size(axis))])  132 us
    pallas_call x10, Pallas kernels, chunk_partial(): pl.pallas_call(kernel, grid_spec=pltpu.PrefetchScalarGridSpec(num_scalar_...  62.1 us
    ppermute x11, starting transfers between devices, line_body(): send = lambda v, pairs: lax.ppermute(v, 'tensor', pairs)  34.8 us
    pallas_call x2, Pallas kernels, plane_product(): pl.pallas_call(kernel, grid_spec=pltpu.PrefetchScalarGridSpec(num_scalar_...  28.2 us
    ppermute x8, starting transfers between devices, xor_perm(): lax.ppermute(x, axis, [(i, i ^ d) for i in range(lax.axis_size(axis))])  26.3 us
    ppermute x11, waiting for transfers between devices, line_body(): send = lambda v, pairs: lax.ppermute(v, 'tensor', pairs)  19.5 us
    pallas_call x2, Pallas kernels, maps_for_mate(): map_call(kernel, scalars, (tiles,), in_specs, out_specs, out_shape, 8 * t...  15.9 us
    unnamed x40, local copies, waits for them, and re-layouts  11 us
  transfers between devices with their start and end apart: 25, of which 9 were waited for; matrix products, arithmetic and copies ran while one was open for 1% of the time, Pallas kernels for 32%

profile of v6, /device:TPU:0, one launch (start us, length us, event | category | flops | bytes accessed | tf_op | source)
XLA Modules:
  0.0 412.0 jit_solution(17045289450238337910)
XLA Ops:
  8.0 8.9 %shard_map.64 = (bf16[2,8,64,2048]{3,2,1,0:T(8,128)(2,1)}, bf16[4,256,2048]{2,1,0:T(8,128)(2,1)}) custom-call(s32[4096]{0:T(1024)S(1)} %copy-done.15, s32[128]{0:T(128)S(1)} %copy-done.17, s32[3]{0:T(128)S(1)} %pad_add_fusion.meta, bf16[32,64,2048]{2,1,0:T(8,128)(2,1)} %bank_ref.6, bf16[32,64,2048]{2,1,0:T(8,128)(2,1)} %bank_ref.6, bf16[256,8192]{1,0:T(8,128)(2,1)} %refs_0_.1), custom_call_target="tpu_custom_call" | custom-call | bytes 8388608 | tf_op jit(solution)/shard_map/pallas_call | solution.py:276
  17.5 7.1 %shard_map.65 = bf16[2,8,64,2048]{3,2,1,0:T(8,128)(2,1)} custom-call(s32[4096]{0:T(1024)S(1)} %copy-done.15, s32[128]{0:T(128)S(1)} %copy-done.17, s32[3]{0:T(128)S(1)} %pad_add_fusion.meta, bf16[32,64,2048]{2,1,0:T(8,128)(2,1)} %bank_ref.7, bf16[32,64,2048]{2,1,0:T(8,128)(2,1)} %bank_ref.7), custom_call_target="tpu_custom_call" | custom-call | bytes 8388608 | tf_op jit(solution)/shard_map/pallas_call | solution.py:276
  24.9 6.3 %all-to-all-start = ((bf16[4,256,2048]{2,1,0:T(8,128)(2,1)}), bf16[4,256,2048]{2,1,0:T(8,128)(2,1)}, u32[]{:S(2)}, u32[]{:S(2)}) async-start(bf16[4,256,2048]{2,1,0:T(8,128)(2,1)} %get-tuple-element.26), calls=%async_computation | async-start | bytes 8388608 | tf_op jit(solution)/shard_map/all_to_all | solution.py:401
  46.8 38.2 %collective-permute-done.3.far_ref = bf16[8,64,2048]{2,1,0:T(8,128)(2,1)S(1)} collective-permute-done((bf16[8,64,2048]{2,1,0:T(8,128)(2,1)S(1)}, bf16[8,64,2048]{2,1,0:T(8,128)(2,1)S(1)}, u32[]{:S(2)}, u32[]{:S(2)}) %collective-permute-start.3) | collective-permute-done | bytes 2097184 | tf_op jit(solution)/shard_map/ppermute | solution.py:14
  86.3 42.9 %collective-permute-done.1.far_ref = bf16[8,64,2048]{2,1,0:T(8,128)(2,1)S(1)} collective-permute-done((bf16[8,64,2048]{2,1,0:T(8,128)(2,1)S(1)}, bf16[8,64,2048]{2,1,0:T(8,128)(2,1)S(1)}, u32[]{:S(2)}, u32[]{:S(2)}) %collective-permute-start.1) | collective-permute-done | bytes 2097184 | tf_op jit(solution)/shard_map/ppermute | solution.py:14
  133.6 7.7 %shard_map.68 = f32[8,128,64]{2,1,0:T(8,128)S(1)} custom-call(s32[4096]{0:T(1024)S(1)} %copy-done.16, s32[128]{0:T(128)S(1)} %copy-done.18, s32[3]{0:T(128)S(1)} %pad_add_fusion.meta, bf16[8,128,2048]{2,1,0:T(8,128)(2,1)} %bitcast.4.rows_ref, bf16[32,64,2048]{2,1,0:T(8,128)(2,1)} %bank_ref.6, bf16[16,64,2048]{2,1,0:T(8,128)(2,1)} %collective-permute-done.2.got_ref, ...), custom_call_target="tpu_custom_call" | custom-call | flops 268435456 | bytes 10485760 | tf_op jit(solution)/shard_map/pallas_call | solution.py:340
  143.7 40.8 %collective-permute-done.4 = bf16[8,128,64]{2,1,0:T(8,128)(2,1)S(1)} collective-permute-done((bf16[8,128,64]{2,1,0:T(8,128)(2,1)S(1)}, bf16[8,128,64]{2,1,0:T(8,128)(2,1)S(1)}, u32[]{:S(2)}, u32[]{:S(2)}) %collective-permute-start.4) | collective-permute-done | bytes 131104 | tf_op jit(solution)/shard_map/ppermute | solution.py:14
  192.0 9.9 %collective-permute-done.5 = bf16[8,128,64]{2,1,0:T(8,128)(2,1)S(1)} collective-permute-done((bf16[8,128,64]{2,1,0:T(8,128)(2,1)S(1)}, bf16[8,128,64]{2,1,0:T(8,128)(2,1)S(1)}, u32[]{:S(2)}, u32[]{:S(2)}) %collective-permute-start.5) | collective-permute-done | bytes 131104 | tf_op jit(solution)/shard_map/ppermute | solution.py:14
  206.1 6.2 %shard_map.69 = (bf16[8,128,1024]{2,1,0:T(8,128)(2,1)S(1)}, bf16[8,64,1024]{2,1,0:T(8,128)(2,1)S(1)}) custom-call(s32[4096]{0:T(1024)S(1)} %copy-done.16, s32[128]{0:T(128)S(1)} %copy-done.18, s32[3]{0:T(128)S(1)} %pad_add_fusion.meta, bf16[8,128,64]{2,1,0:T(8,128)(2,1)S(1)} %add_convert_fusion.low_ref, bf16[32,64,2048]{2,1,0:T(8,128)(2,1)} %bank_ref.7, ...), custom_call_target="tpu_custom_call" | custom-call | flops 134217728 | bytes 9437184 | tf_op jit(solution)/shard_map/pallas_call | solution.py:360
  213.3 5.9 %shard_map.70 = bf16[256,2048]{1,0:T(8,128)(2,1)S(1)} custom-call(s32[1]{0:T(128)} %bitcast.t_ref, bf16[4,256,2048]{2,1,0:T(8,128)(2,1)} %all-to-all-done.rows_ref, bf16[2048,8192]{1,0:T(8,128)(2,1)} %w_ref.19, bf16[4,256,1024]{2,1,0:T(8,128)(2,1)S(1)} %bitcast.10), custom_call_target="tpu_custom_call" | custom-call | flops 2147483648 | bytes 10485760 | tf_op jit(solution)/shard_map/pallas_call | solution.py:105
  221.9 6.0 %shard_map.71.refs_1_ = f32[256,4096]{1,0:T(8,128)} custom-call(s32[1]{0:T(128)} %bitcast.t_ref, bf16[4,256,2048]{2,1,0:T(8,128)(2,1)} %all-to-all-done.rows_ref, bf16[2048,8192]{1,0:T(8,128)(2,1)} %w_ref.19, bf16[4,256,1024]{2,1,0:T(8,128)(2,1)S(1)} %bitcast.11), custom_call_target="tpu_custom_call" | custom-call | flops 2147483648 | bytes 10485760 | tf_op jit(solution)/shard_map/pallas_call | solution.py:105
  229.6 7.4 %shard_map.73 = bf16[256,2048]{1,0:T(8,128)(2,1)} custom-call(s32[1]{0:T(128)} %bitcast.t_ref, bf16[4,256,2048]{2,1,0:T(8,128)(2,1)} %all-to-all-done.rows_ref, bf16[2048,8192]{1,0:T(8,128)(2,1)} %w_ref.19, bf16[4,256,1024]{2,1,0:T(8,128)(2,1)S(1)} %bitcast.12, bf16[256,2048]{1,0:T(8,128)(2,1)S(1)} %collective-permute-done.6.refs_1_), custom_call_target="tpu_custom_call" | custom-call | flops 2147483648 | bytes 10485760 | tf_op jit(solution)/shard_map/pallas_call | solution.py:105
  237.7 6.1 %shard_map.74.own_ref = f32[256,4096]{1,0:T(8,128)} custom-call(s32[1]{0:T(128)} %bitcast.t_ref, bf16[4,256,2048]{2,1,0:T(8,128)(2,1)} %all-to-all-done.rows_ref, bf16[2048,8192]{1,0:T(8,128)(2,1)} %w_ref.19, bf16[4,256,1024]{2,1,0:T(8,128)(2,1)S(1)} %bitcast.13, f32[256,4096]{1,0:T(8,128)} %shard_map.71.refs_1_), custom_call_target="tpu_custom_call", output_to_operand_aliasing={{}: (4, {})} | custom-call | flops 2147483648 | bytes 10485760 | tf_op jit(solution)/shard_map/pallas_call | solution.py:105
  248.5 6.0 %shard_map.75 = bf16[256,2048]{1,0:T(8,128)(2,1)} custom-call(s32[1]{0:T(128)} %bitcast.t_ref, bf16[4,256,2048]{2,1,0:T(8,128)(2,1)} %all-to-all-done.rows_ref, bf16[2048,8192]{1,0:T(8,128)(2,1)} %w_ref.19, bf16[4,256,1024]{2,1,0:T(8,128)(2,1)S(1)} %bitcast.14, bf16[256,2048]{1,0:T(8,128)(2,1)S(1)} %collective-permute-done.7.refs_1_), custom_call_target="tpu_custom_call" | custom-call | flops 2147483648 | bytes 10485760 | tf_op jit(solution)/shard_map/pallas_call | solution.py:105
  255.7 6.9 %collective-permute-start.11 = (bf16[256,2048]{1,0:T(8,128)(2,1)}, bf16[256,2048]{1,0:T(8,128)(2,1)}, u32[]{:S(2)}, u32[]{:S(2)}) collective-permute-start(bf16[256,2048]{1,0:T(8,128)(2,1)} %shard_map.73), channel_id=1, source_target_pairs={{0,1},{1,2},{4,5},{5,6},{8,9},{9,10},{12,13},{13,14},{16,17},{17,1... | collective-permute-start | bytes 3145736 | tf_op jit(solution)/shard_map/ppermute | solution.py:394
  263.3 14.4 %collective-permute-start.9 = (bf16[256,2048]{1,0:T(8,128)(2,1)}, bf16[256,2048]{1,0:T(8,128)(2,1)}, u32[]{:S(2)}, u32[]{:S(2)}) collective-permute-start(bf16[256,2048]{1,0:T(8,128)(2,1)} %shard_map.75), channel_id=1, source_target_pairs={{0,1},{1,2},{4,5},{5,6},{8,9},{9,10},{12,13},{13,14},{16,17},{17,1... | collective-permute-start | bytes 3145736 | tf_op jit(solution)/shard_map/ppermute | solution.py:394
  285.5 6.5 %shard_map.78.refs_3_ = bf16[256,4096]{1,0:T(8,128)(2,1)} custom-call(s32[1]{0:T(128)} %bitcast.t_ref, bf16[4,256,2048]{2,1,0:T(8,128)(2,1)} %all-to-all-done.rows_ref, bf16[2048,8192]{1,0:T(8,128)(2,1)} %w_ref.19, bf16[4,256,1024]{2,1,0:T(8,128)(2,1)} %bitcast.15, bf16[256,2048]{1,0:T(8,128)(2,1)} %collective-permute-done.11.refs_2_.refs_1_, ...), custom_call_target="tpu_custom_call" | custom-call | flops 2147483648 | bytes 10485760 | tf_op jit(solution)/shard_map/pallas_call | solution.py:105
  292.0 6.4 %shard_map.76.refs_3_ = bf16[256,4096]{1,0:T(8,128)(2,1)} custom-call(s32[1]{0:T(128)} %bitcast.t_ref, bf16[4,256,2048]{2,1,0:T(8,128)(2,1)} %all-to-all-done.rows_ref, bf16[2048,8192]{1,0:T(8,128)(2,1)} %w_ref.19, bf16[4,256,1024]{2,1,0:T(8,128)(2,1)} %bitcast.16, bf16[256,2048]{1,0:T(8,128)(2,1)S(1)} %collective-permute-done.10.refs_1_.refs_2_, ...), custom_call_target="tpu_custom_call" | custom-call | flops 2147483648 | bytes 10485760 | tf_op jit(solution)/shard_map/pallas_call | solution.py:105
  298.4 9.6 %collective-permute-done.9.refs_2_.refs_1_ = bf16[256,2048]{1,0:T(8,128)(2,1)} collective-permute-done((bf16[256,2048]{1,0:T(8,128)(2,1)}, bf16[256,2048]{1,0:T(8,128)(2,1)}, u32[]{:S(2)}, u32[]{:S(2)}) %collective-permute-start.9) | collective-permute-done | bytes 1048608 | tf_op jit(solution)/shard_map/ppermute | solution.py:394
  308.0 6.5 %shard_map.79 = bf16[256,4096]{1,0:T(8,128)(2,1)} custom-call(s32[1]{0:T(128)} %bitcast.t_ref, bf16[4,256,2048]{2,1,0:T(8,128)(2,1)} %all-to-all-done.rows_ref, bf16[2048,8192]{1,0:T(8,128)(2,1)} %w_ref.19, bf16[4,256,1024]{2,1,0:T(8,128)(2,1)} %bitcast.17, bf16[256,2048]{1,0:T(8,128)(2,1)} %collective-permute-done.9.refs_2_.refs_1_, ...), custom_call_target="tpu_custom_call", output_to_operand_aliasing={{}: (6, {})} | custom-call | flops 2147483648 | bytes 10485760 | tf_op jit(solution)/shard_map/pallas_call | solution.py:105
  318.9 6.3 %shard_map.77 = bf16[256,4096]{1,0:T(8,128)(2,1)} custom-call(s32[1]{0:T(128)} %bitcast.t_ref, bf16[4,256,2048]{2,1,0:T(8,128)(2,1)} %all-to-all-done.rows_ref, bf16[2048,8192]{1,0:T(8,128)(2,1)} %w_ref.19, bf16[4,256,1024]{2,1,0:T(8,128)(2,1)} %bitcast.18, bf16[256,2048]{1,0:T(8,128)(2,1)S(1)} %copy-done.11, ...), custom_call_target="tpu_custom_call", output_to_operand_aliasing={{}: (6, {})} | custom-call | flops 2147483648 | bytes 10485760 | tf_op jit(solution)/shard_map/pallas_call | solution.py:105
  325.1 18.4 %collective-permute-start.17 = (bf16[256,4096]{1,0:T(8,128)(2,1)}, bf16[256,4096]{1,0:T(8,128)(2,1)}, u32[]{:S(2)}, u32[]{:S(2)}) collective-permute-start(bf16[256,4096]{1,0:T(8,128)(2,1)} %shard_map.77), channel_id=1, source_target_pairs={{0,1},{1,0},{2,3},{3,2},{4,5},{5,4},{6,7},{7,6},{8,9},{9,8},{10,11... | collective-permute-start | bytes 6291464 | tf_op jit(solution)/shard_map/ppermute | solution.py:14
  345.1 14.1 %shard_map.81 = bf16[1024,512]{1,0:T(8,128)(2,1)S(1)} custom-call(s32[1]{0:T(128)} %bitcast.t_ref, bf16[1024,8192]{1,0:T(8,128)(2,1)} %all-gather.5.cloned.1.call-done.refs_0_.refs_1_.refs_2_.refs_3_, bf16[1024,8192]{1,0:T(8,128)(2,1)} %all-gather.5.cloned.1.call-done.refs_0_.refs_1_.refs_2_.refs_3_, ...), custom_call_target="tpu_custom_call" | custom-call | flops 8589934592 | bytes 26214400 | tf_op jit(solution)/shard_map/pallas_call | solution.py:154
  366.8 14.1 %shard_map.80 = bf16[1024,512]{1,0:T(8,128)(2,1)S(1)} custom-call(s32[1]{0:T(128)} %bitcast.t_ref, bf16[1024,8192]{1,0:T(8,128)(2,1)} %all-gather.3.cloned.1.call-done.refs_0_.refs_1_.refs_2_.refs_3_, bf16[1024,8192]{1,0:T(8,128)(2,1)} %all-gather.3.cloned.1.call-done.refs_0_.refs_1_.refs_2_.refs_3_, ...), custom_call_target="tpu_custom_call" | custom-call | flops 8589934592 | bytes 26214400 | tf_op jit(solution)/shard_map/pallas_call | solution.py:154
  (95 shorter events, 95.9 us)
Async XLA Ops:
  16.9 14.3 %collective-permute-start.2 = (bf16[16,64,2048]{2,1,0:T(8,128)(2,1)}, bf16[16,64,2048]{2,1,0:T(8,128)(2,1)}, u32[]{:S(2)}, u32[]{:S(2)}) collective-permute-start(bf16[16,64,2048]{2,1,0:T(8,128)(2,1)} %bitcast.2), channel_id=1, source_target_pairs={{0,4},{4,0},{8,12},{12,8},{1,5},{5,1},{9,13},{13,9},{2,6},{6,2},{1... | collective-permute-start | bytes 12582920 | tf_op jit(solution)/shard_map/ppermute | solution.py:14
  24.9 104.3 %all-to-all-start = ((bf16[4,256,2048]{2,1,0:T(8,128)(2,1)}), bf16[4,256,2048]{2,1,0:T(8,128)(2,1)}, u32[]{:S(2)}, u32[]{:S(2)}) async-start(bf16[4,256,2048]{2,1,0:T(8,128)(2,1)} %get-tuple-element.26), calls=%async_computation | async-start | bytes 8388608 | tf_op jit(solution)/shard_map/all_to_all | solution.py:401
  31.2 312.3 %all-gather.5.cloned.1.call-start = ((), (), s32[]{:S(2)}) async-start(), calls=%async_computation.5 | async-start | bytes 18874368 | tf_op jit(solution)/shard_map/all_gather | solution.py:418
  36.3 48.7 %collective-permute-start.3 = (bf16[8,64,2048]{2,1,0:T(8,128)(2,1)S(1)}, bf16[8,64,2048]{2,1,0:T(8,128)(2,1)S(1)}, u32[]{:S(2)}, u32[]{:S(2)}) collective-permute-start(bf16[8,64,2048]{2,1,0:T(8,128)(2,1)S(1)} %shard_map.67), channel_id=1, source_target_pairs={{0,8},{4,12},{8,0},{12,4},{1,9},{5,13},{9,1},{13,5},{2,10},{6,14},... | collective-permute-start | bytes 6291464 | tf_op jit(solution)/shard_map/ppermute | solution.py:14
  44.0 85.2 %collective-permute-start.1 = (bf16[8,64,2048]{2,1,0:T(8,128)(2,1)S(1)}, bf16[8,64,2048]{2,1,0:T(8,128)(2,1)S(1)}, u32[]{:S(2)}, u32[]{:S(2)}) collective-permute-start(bf16[8,64,2048]{2,1,0:T(8,128)(2,1)S(1)} %shard_map.66), channel_id=1, source_target_pairs={{0,8},{4,12},{8,0},{12,4},{1,9},{5,13},{9,1},{13,5},{2,10},{6,14},... | collective-permute-start | bytes 6291464 | tf_op jit(solution)/shard_map/ppermute | solution.py:14
  129.2 236.0 %all-gather.3.cloned.1.call-start = ((), (), s32[]{:S(2)}) async-start(), calls=%async_computation.4 | async-start | bytes 18874368 | tf_op jit(solution)/shard_map/all_gather | solution.py:418
  131.9 70.2 %collective-permute-start.12 = (bf16[2048,512]{1,0:T(8,128)(2,1)S(1)}, bf16[2048,512]{1,0:T(8,128)(2,1)S(1)}, u32[]{:S(2)}, u32[]{:S(2)}) collective-permute-start(bf16[2048,512]{1,0:T(8,128)(2,1)S(1)} %constant_dynamic-slice_fusion.refs_4_.refs_5_), channel_id=1, source_target_pairs={{0,1},{1,0},{2,3},{3,2},{4,5},{5,4},{6,7},{7,6},{8,9},{9,8},{10,11... | collective-permute-start | bytes 6291464 | tf_op jit(solution)/shard_map/ppermute | solution.py:14
  141.4 43.1 %collective-permute-start.4 = (bf16[8,128,64]{2,1,0:T(8,128)(2,1)S(1)}, bf16[8,128,64]{2,1,0:T(8,128)(2,1)S(1)}, u32[]{:S(2)}, u32[]{:S(2)}) collective-permute-start(bf16[8,128,64]{2,1,0:T(8,128)(2,1)S(1)} %convert_element_type.15), channel_id=1, source_target_pairs={{0,1},{1,0},{2,3},{3,2},{4,5},{5,4},{6,7},{7,6},{8,9},{9,8},{10,11... | collective-permute-start | bytes 393224 | tf_op jit(solution)/shard_map/ppermute | solution.py:14
  141.7 78.8 %collective-permute-start.13 = (bf16[2048,512]{1,0:T(8,128)(2,1)S(1)}, bf16[2048,512]{1,0:T(8,128)(2,1)}, u32[]{:S(2)}, u32[]{:S(2)}) collective-permute-start(bf16[2048,512]{1,0:T(8,128)(2,1)S(1)} %constant_dynamic-slice_fusion.refs_4_.refs_5_), channel_id=1, source_target_pairs={{1,2},{2,1},{5,6},{6,5},{9,10},{10,9},{13,14},{14,13},{17,18},{18,... | collective-permute-start | bytes 6291464 | tf_op jit(solution)/shard_map/ppermute | solution.py:394
  184.6 17.4 %collective-permute-start.5 = (bf16[8,128,64]{2,1,0:T(8,128)(2,1)S(1)}, bf16[8,128,64]{2,1,0:T(8,128)(2,1)S(1)}, u32[]{:S(2)}, u32[]{:S(2)}) collective-permute-start(bf16[8,128,64]{2,1,0:T(8,128)(2,1)S(1)} %fusion), channel_id=1, source_target_pairs={{0,2},{1,3},{2,0},{3,1},{4,6},{5,7},{6,4},{7,5},{8,10},{9,11},{10,... | collective-permute-start | bytes 393224 | tf_op jit(solution)/shard_map/ppermute | solution.py:14
  202.1 52.3 %collective-permute-start.15 = (bf16[2048,512]{1,0:T(8,128)(2,1)S(1)}, bf16[2048,512]{1,0:T(8,128)(2,1)}, u32[]{:S(2)}, u32[]{:S(2)}) collective-permute-start(bf16[2048,512]{1,0:T(8,128)(2,1)S(1)} %collective-permute-done.12.refs_6_.refs_7_), channel_id=1, source_target_pairs={{1,2},{2,1},{5,6},{6,5},{9,10},{10,9},{13,14},{14,13},{17,18},{18,... | collective-permute-start | bytes 6291464 | tf_op jit(solution)/shard_map/ppermute | solution.py:394
  204.2 25.4 %collective-permute-start.6 = (bf16[256,2048]{1,0:T(8,128)(2,1)S(1)}, bf16[256,2048]{1,0:T(8,128)(2,1)S(1)}, u32[]{:S(2)}, u32[]{:S(2)}) collective-permute-start(bf16[256,2048]{1,0:T(8,128)(2,1)S(1)} %shard_map.72), channel_id=1, source_target_pairs={{0,1},{3,2},{4,5},{7,6},{8,9},{11,10},{12,13},{15,14},{16,17},{19,... | collective-permute-start | bytes 3145736 | tf_op jit(solution)/shard_map/ppermute | solution.py:394
  219.2 29.3 %collective-permute-start.7 = (bf16[256,2048]{1,0:T(8,128)(2,1)S(1)}, bf16[256,2048]{1,0:T(8,128)(2,1)S(1)}, u32[]{:S(2)}, u32[]{:S(2)}) collective-permute-start(bf16[256,2048]{1,0:T(8,128)(2,1)S(1)} %shard_map.70), channel_id=1, source_target_pairs={{0,1},{3,2},{4,5},{7,6},{8,9},{11,10},{12,13},{15,14},{16,17},{19,... | collective-permute-start | bytes 3145736 | tf_op jit(solution)/shard_map/ppermute | solution.py:394
  220.6 122.9 %collective-permute-start.14 = (bf16[2048,512]{1,0:T(8,128)(2,1)}, bf16[2048,512]{1,0:T(8,128)(2,1)}, u32[]{:S(2)}, u32[]{:S(2)}) collective-permute-start(bf16[2048,512]{1,0:T(8,128)(2,1)} %collective-permute-done.13.refs_11_), channel_id=1, source_target_pairs={{1,0},{2,3},{5,4},{6,7},{9,8},{10,11},{13,12},{14,15},{17,16},{18,... | collective-permute-start | bytes 6291464 | tf_op jit(solution)/shard_map/ppermute | solution.py:394
  237.0 26.3 %collective-permute-start.10 = (bf16[256,2048]{1,0:T(8,128)(2,1)}, bf16[256,2048]{1,0:T(8,128)(2,1)S(1)}, u32[]{:S(2)}, u32[]{:S(2)}) collective-permute-start(bf16[256,2048]{1,0:T(8,128)(2,1)} %shard_map.73), channel_id=1, source_target_pairs={{3,2},{2,1},{7,6},{6,5},{11,10},{10,9},{15,14},{14,13},{19,18},{18... | collective-permute-start | bytes 3145736 | tf_op jit(solution)/shard_map/ppermute | solution.py:394
  254.4 89.1 %collective-permute-start.16 = (bf16[2048,512]{1,0:T(8,128)(2,1)}, bf16[2048,512]{1,0:T(8,128)(2,1)}, u32[]{:S(2)}, u32[]{:S(2)}) collective-permute-start(bf16[2048,512]{1,0:T(8,128)(2,1)} %collective-permute-done.15.refs_9_), channel_id=1, source_target_pairs={{1,0},{2,3},{5,4},{6,7},{9,8},{10,11},{13,12},{14,15},{17,16},{18,... | collective-permute-start | bytes 6291464 | tf_op jit(solution)/shard_map/ppermute | solution.py:394
  255.7 29.8 %collective-permute-start.11 = (bf16[256,2048]{1,0:T(8,128)(2,1)}, bf16[256,2048]{1,0:T(8,128)(2,1)}, u32[]{:S(2)}, u32[]{:S(2)}) collective-permute-start(bf16[256,2048]{1,0:T(8,128)(2,1)} %shard_map.73), channel_id=1, source_target_pairs={{0,1},{1,2},{4,5},{5,6},{8,9},{9,10},{12,13},{13,14},{16,17},{17,1... | collective-permute-start | bytes 3145736 | tf_op jit(solution)/shard_map/ppermute | solution.py:394
  262.6 35.8 %collective-permute-start.8 = (bf16[256,2048]{1,0:T(8,128)(2,1)}, bf16[256,2048]{1,0:T(8,128)(2,1)S(1)}, u32[]{:S(2)}, u32[]{:S(2)}) collective-permute-start(bf16[256,2048]{1,0:T(8,128)(2,1)} %shard_map.75), channel_id=1, source_target_pairs={{3,2},{2,1},{7,6},{6,5},{11,10},{10,9},{15,14},{14,13},{19,18},{18... | collective-permute-start | bytes 3145736 | tf_op jit(solution)/shard_map/ppermute | solution.py:394
  263.3 44.7 %collective-permute-start.9 = (bf16[256,2048]{1,0:T(8,128)(2,1)}, bf16[256,2048]{1,0:T(8,128)(2,1)}, u32[]{:S(2)}, u32[]{:S(2)}) collective-permute-start(bf16[256,2048]{1,0:T(8,128)(2,1)} %shard_map.75), channel_id=1, source_target_pairs={{0,1},{1,2},{4,5},{5,6},{8,9},{9,10},{12,13},{13,14},{16,17},{17,1... | collective-permute-start | bytes 3145736 | tf_op jit(solution)/shard_map/ppermute | solution.py:394
  277.7 82.5 %all-to-all-start.2 = ((bf16[4,2,64,1024]{3,2,1,0:T(8,128)(2,1)}), bf16[4,2,64,1024]{3,2,1,0:T(8,128)(2,1)S(1)}, u32[]{:S(2)}, u32[]{:S(2)}) async-start(bf16[4,2,64,1024]{3,2,1,0:T(8,128)(2,1)} %bitcast.23), calls=%async_computation.2 | async-start | bytes 2097152 | tf_op jit(solution)/shard_map/all_to_all | solution.py:446
  315.5 76.5 %collective-permute-start.18 = (bf16[256,4096]{1,0:T(8,128)(2,1)}, bf16[256,4096]{1,0:T(8,128)(2,1)}, u32[]{:S(2)}, u32[]{:S(2)}) collective-permute-start(bf16[256,4096]{1,0:T(8,128)(2,1)} %shard_map.79), channel_id=1, source_target_pairs={{1,2},{2,1},{5,6},{6,5},{9,10},{10,9},{13,14},{14,13},{17,18},{18,... | collective-permute-start | bytes 6291464 | tf_op jit(solution)/shard_map/ppermute | solution.py:394
  325.1 66.9 %collective-permute-start.17 = (bf16[256,4096]{1,0:T(8,128)(2,1)}, bf16[256,4096]{1,0:T(8,128)(2,1)}, u32[]{:S(2)}, u32[]{:S(2)}) collective-permute-start(bf16[256,4096]{1,0:T(8,128)(2,1)} %shard_map.77), channel_id=1, source_target_pairs={{0,1},{1,0},{2,3},{3,2},{4,5},{5,4},{6,7},{7,6},{8,9},{9,8},{10,11... | collective-permute-start | bytes 6291464 | tf_op jit(solution)/shard_map/ppermute | solution.py:14
  360.2 21.7 %all-to-all-start.3 = ((bf16[8,128,512]{2,1,0:T(8,128)(2,1)}), bf16[8,128,512]{2,1,0:T(8,128)(2,1)}, u32[]{:S(2)}, u32[]{:S(2)}) async-start(bf16[8,128,512]{2,1,0:T(8,128)(2,1)} %bitcast.20), calls=%async_computation.3 | async-start | bytes 2097152 | tf_op jit(solution)/shard_map/all_to_all | solution.py:454
  381.9 19.8 %all-to-all-start.1 = ((bf16[8,128,512]{2,1,0:T(8,128)(2,1)}), bf16[8,128,512]{2,1,0:T(8,128)(2,1)S(1)}, u32[]{:S(2)}, u32[]{:S(2)}) async-start(bf16[8,128,512]{2,1,0:T(8,128)(2,1)} %bitcast.19), calls=%async_computation.1 | async-start | bytes 2097152 | tf_op jit(solution)/shard_map/all_to_all | solution.py:454
  (21 other events, 144.9 us)
Sparse Core Ops, SparseCore 0:
  129.3 91.5 all-gather.4
  222.8 89.8 all-gather.2
